TPU v7x, 32 devices: a whole 2x2x4 slice. The times are simulated.
32 devices in a mesh: elem: 8 (over z, y), face: 4 (over x, core).
Axes of the slice: x: 2, y: 2, z: 4, core: 2. Of those that a mesh axis runs over, the one named last changes fastest.
Arguments:
- vol_inverse: bfloat16 [128, 320, 320], P(('elem', 'face')), may hold values from -0.3125 to 0.3125
- vol_from_trace: bfloat16 [128, 320, 480], P(('elem', 'face')), may hold values from -0.25 to 0.25
- trace_from_vol: bfloat16 [128, 480, 320], P(('elem', 'face')), may hold values from -0.25 to 0.25
- vol_residual: bfloat16 [128, 320], P(('elem', 'face')), may hold values from -6 to 6
- face_ids: int32 [128, 6], P(('elem', 'face')), may hold values from 0 to 383, as said below
- trace_residual: float32 [384, 80], P(('elem', 'face')), may hold values from -6 to 6
- stabilization: float32 [384, 80], P(('elem', 'face')), may hold values from 1.5 to 4
Outputs:
- trace_update: float32 [384, 80], P(('elem', 'face'))
- vol_update: float32 [128, 320], P(('elem', 'face'))
Inputs may be any that keep to these rules, and one draw needn't show every extreme that they name: `face_ids`: owner group g holds elements g * 16 to (g + 1) * 16 - 1 and faces g * 48 to (g + 1) * 48 - 1. Every face is named by exactly two slots, and the 6 slots of one element name different faces. The slots of group g name faces of group g, or faces 0 to 15 of group (g - 1) mod 8; faces 0 to 15 of group g are named by one slot of group g and one slot of group (g + 1) mod 8; all other faces of group g are named by two slots of group g.
All inputs are finite; a program needn't handle non-finite values.
Results may differ from a plain program's by a relative error of at most 0.007.
Values may be sent and summed in bfloat16 or wider, within the bound.
No kernel may reach another device: no remote copies, remote signals or barrier semaphores. Data moves between devices by JAX's collectives and lax.ppermute only.
A program may use at most 64 MiB of HBM per device.

v0:
```python
import jax
import jax.numpy as jnp
from jax import lax
from jax.sharding import PartitionSpec as P

SWEEPS = 5


exact_precision = lax.Precision.HIGHEST


def shifted(block, axis, distance):
    devices = range(lax.axis_size(axis))
    route = [((i - distance) % len(devices), i) for i in devices]
    return lax.ppermute(block, axis, route)


def local(
    vol_inverse,
    vol_from_trace,
    trace_from_vol,
    vol_residual,
    face_ids,
    trace_residual,
    stabilization,
):
    groups = lax.axis_size("elem")
    members = lax.axis_size("face")
    elem_count, side_count = face_ids.shape
    own_faces, trace_width = trace_residual.shape
    group_faces = own_faces * members
    border = elem_count * members
    slot_count = elem_count * side_count
    group_index = lax.axis_index("elem")
    lower_group = (group_index + groups - 1) % groups
    slot_ids = face_ids.reshape(slot_count)
    own_hits = (slot_ids - group_index * group_faces)[:, None] == lax.broadcasted_iota(
        jnp.int32, (slot_count, group_faces), 1
    )
    lower_hits = (slot_ids - lower_group * group_faces)[:, None] == lax.broadcasted_iota(
        jnp.int32, (slot_count, border), 1
    )
    own_float = own_hits.astype(jnp.float32)
    lower_float = lower_hits.astype(jnp.float32)
    own_half = own_hits.astype(jnp.bfloat16)
    lower_half = lower_hits.astype(jnp.bfloat16)

    def assemble(contrib):
        own_sum = jnp.einsum("sf,sw->fw", own_float, contrib, precision=exact_precision)
        lower_sum = jnp.einsum("sb,sw->bw", lower_float, contrib, precision=exact_precision)
        arrived = shifted(lower_sum, "elem", -1)
        partial_value = jnp.concatenate([own_sum[:border] + arrived, own_sum[border:]], axis=0)
        summed = lax.psum(partial_value, "face")
        return summed

    def distribute(lam_rows):
        upper_rows = shifted(lam_rows[:border], "elem", 1)
        slot_values = jnp.dot(own_half, lam_rows, preferred_element_type=jnp.float32)
        slot_values = slot_values + jnp.dot(
            lower_half, upper_rows, preferred_element_type=jnp.float32
        )
        return slot_values.astype(jnp.bfloat16).reshape(elem_count, side_count * trace_width)

    base_residual, base_stab = (
        lax.all_gather(trace_residual, "face", axis=0, tiled=True),
        lax.all_gather(stabilization, "face", axis=0, tiled=True),
    )
    local_part = jnp.einsum(
        "evk,ek->ev", vol_inverse, vol_residual, preferred_element_type=jnp.float32
    )
    trace_load = jnp.einsum(
        "etv,ev->et",
        trace_from_vol,
        local_part.astype(jnp.bfloat16),
        preferred_element_type=jnp.float32,
    )
    load_sums = assemble(trace_load.reshape(slot_count, trace_width))
    couple = jnp.einsum(
        "evk,ekt->evt", vol_inverse, vol_from_trace, preferred_element_type=jnp.float32
    ).astype(jnp.bfloat16)
    schur_block = jnp.einsum(
        "etv,evs->ets", trace_from_vol, couple, preferred_element_type=jnp.float32
    ).astype(jnp.bfloat16)
    right_side = base_residual - load_sums
    trace_now = right_side / base_stab
    for sweep_index in range(SWEEPS - 1):
        lam_elem = distribute(trace_now.astype(jnp.bfloat16))
        image_terms = jnp.einsum(
            "ets,es->et", schur_block, lam_elem, preferred_element_type=jnp.float32
        )
        image_sums = assemble(image_terms.reshape(slot_count, trace_width))
        trace_now = (right_side + image_sums) / base_stab
    lam_elem = distribute(trace_now.astype(jnp.bfloat16))
    vol_update = local_part - jnp.einsum(
        "evt,et->ev", couple, lam_elem, preferred_element_type=jnp.float32
    )
    trace_now = lax.dynamic_slice_in_dim(
        trace_now, lax.axis_index("face") * own_faces, own_faces, 0
    )
    return (trace_now, vol_update)


def solution(mesh):
    in_specs = (
        P(("elem", "face"), None, None),
        P(("elem", "face"), None, None),
        P(("elem", "face"), None, None),
        P(("elem", "face"), None),
        P(("elem", "face"), None),
        P(("elem", "face"), None),
        P(("elem", "face"), None),
    )
    out_specs = (P(("elem", "face"), None), P(("elem", "face"), None))
    return jax.shard_map(local, mesh=mesh, in_specs=in_specs, out_specs=out_specs, check_vma=False)
```

profile of v0, /device:TPU:0, one launch (start us, length us, event | category | flops | bytes accessed | tf_op | source)
XLA Modules:
  0.0 129.5 jit_solution(14048758496720298639)
XLA Ops:
  0.7 1.7 %fusion.22 = f32[4,1,320]{2,1,0:T(1,128)S(1)} fusion(bf16[4,320,320]{2,1,0:T(8,128)(2,1)} %param.7, bf16[4,320,1]{1,0,2:T(4,128)(2,1)} %bitcast.71), kind=kOutput, calls=%fused_computation.53 | convolution fusion | flops 819200 | bytes 826880 | tf_op jit(solution)/shard_map/evk,ek->ev/dot_general | solution.py:68
  3.2 6.0 %collective-permute-start = (f32[16,80]{1,0:T(8,128)S(1)}, f32[16,80]{1,0:T(8,128)S(1)}, u32[]{:S(2)}, u32[]{:S(2)}) collective-permute-start(f32[16,80]{1,0:T(8,128)S(1)} %fusion.9), channel_id=1, source_target_pairs={{4,0},{8,4},{12,8},{16,12},{20,16},{24,20},{28,24},{0,28},{5,1},{9... | collective-permute-start | bytes 15368 | tf_op jit(solution)/shard_map/ppermute | solution.py:15
  9.6 5.2 %all-gather.1 = f32[4,12,80]{2,1,0:T(8,128)S(1)} all-gather(f32[1,12,80]{2,1,0:T(8,128)S(1)} %bitcast.72), channel_id=1, replica_groups=mesh['elem'=8,'face'=4] {'face'}, dimensions={0}, use_global_device_ids=true | all-gather | bytes 19200 | tf_op jit(solution)/shard_map/all_gather | solution.py:66
  14.8 2.1 %convolution_convert_fusion.1 = bf16[4,320,480]{2,1,0:T(8,128)(2,1)S(1)} fusion(bf16[4,320,320]{2,1,0:T(8,128)(2,1)S(1)} %copy-done.2, bf16[4,320,480]{2,1,0:T(8,128)(2,1)} %param.8), kind=kOutput, calls=%fused_computation.1 | convolution fusion | flops 393830400 | bytes 3276800 | tf_op jit(solution)/shard_map/evk,ekt->evt/dot_general | solution.py:78
  16.9 1.2 convolution_convert_fusion
  18.2 5.2 %all-gather = f32[4,12,80]{2,1,0:T(8,128)S(1)} all-gather(f32[1,12,80]{2,1,0:T(8,128)S(1)} %bitcast.73), channel_id=1, replica_groups=mesh['elem'=8,'face'=4] {'face'}, dimensions={0}, use_global_device_ids=true | all-gather | bytes 19200 | tf_op jit(solution)/shard_map/all_gather | solution.py:65
  23.4 11.5 %psum.35 = f32[48,80]{1,0:T(8,128)S(1)} all-reduce(f32[48,80]{1,0:T(8,128)S(1)} %pad_maximum_fusion), channel_id=1, replica_groups=mesh['elem'=8,'face'=4] {'face'}, use_global_device_ids=true, to_apply=%region_0.1 | all-reduce | flops 3840 | bytes 30720 | tf_op jit(solution)/shard_map/psum | solution.py:53
  35.3 6.1 %collective-permute-done.1 = bf16[16,80]{1,0:T(8,128)(2,1)S(1)} collective-permute-done((bf16[16,80]{1,0:T(8,128)(2,1)S(1)}, bf16[16,80]{1,0:T(8,128)(2,1)S(1)}, u32[]{:S(2)}, u32[]{:S(2)}) %collective-permute-start.1) | collective-permute-done | bytes 2592 | tf_op jit(solution)/shard_map/ppermute | solution.py:15
  41.6 0.4 fusion.46
  42.7 3.4 %collective-permute-done.2 = f32[16,80]{1,0:T(8,128)S(1)} collective-permute-done((f32[16,80]{1,0:T(8,128)S(1)}, f32[16,80]{1,0:T(8,128)S(1)}, u32[]{:S(2)}, u32[]{:S(2)}) %collective-permute-start.2) | collective-permute-done | bytes 5152 | tf_op jit(solution)/shard_map/ppermute | solution.py:15
  46.0 10.4 %psum.36 = f32[48,80]{1,0:T(8,128)S(1)} all-reduce(f32[48,80]{1,0:T(8,128)S(1)} %pad_maximum_fusion.1), channel_id=1, replica_groups=mesh['elem'=8,'face'=4] {'face'}, use_global_device_ids=true, to_apply=%region_1.2 | all-reduce | flops 3840 | bytes 30720 | tf_op jit(solution)/shard_map/psum | solution.py:53
  56.7 6.1 %collective-permute-done.3 = bf16[16,80]{1,0:T(8,128)(2,1)S(1)} collective-permute-done((bf16[16,80]{1,0:T(8,128)(2,1)S(1)}, bf16[16,80]{1,0:T(8,128)(2,1)S(1)}, u32[]{:S(2)}, u32[]{:S(2)}) %collective-permute-start.3) | collective-permute-done | bytes 2592 | tf_op jit(solution)/shard_map/ppermute | solution.py:15
  64.1 3.4 %collective-permute-done.4 = f32[16,80]{1,0:T(8,128)S(1)} collective-permute-done((f32[16,80]{1,0:T(8,128)S(1)}, f32[16,80]{1,0:T(8,128)S(1)}, u32[]{:S(2)}, u32[]{:S(2)}) %collective-permute-start.4) | collective-permute-done | bytes 5152 | tf_op jit(solution)/shard_map/ppermute | solution.py:15
  67.5 10.3 %psum.37 = f32[48,80]{1,0:T(8,128)S(1)} all-reduce(f32[48,80]{1,0:T(8,128)S(1)} %pad_maximum_fusion.2), channel_id=1, replica_groups=mesh['elem'=8,'face'=4] {'face'}, use_global_device_ids=true, to_apply=%region_2.3 | all-reduce | flops 3840 | bytes 30720 | tf_op jit(solution)/shard_map/psum | solution.py:53
  78.0 6.1 %collective-permute-done.5 = bf16[16,80]{1,0:T(8,128)(2,1)S(1)} collective-permute-done((bf16[16,80]{1,0:T(8,128)(2,1)S(1)}, bf16[16,80]{1,0:T(8,128)(2,1)S(1)}, u32[]{:S(2)}, u32[]{:S(2)}) %collective-permute-start.5) | collective-permute-done | bytes 2592 | tf_op jit(solution)/shard_map/ppermute | solution.py:15
  85.4 3.4 %collective-permute-done.6 = f32[16,80]{1,0:T(8,128)S(1)} collective-permute-done((f32[16,80]{1,0:T(8,128)S(1)}, f32[16,80]{1,0:T(8,128)S(1)}, u32[]{:S(2)}, u32[]{:S(2)}) %collective-permute-start.6) | collective-permute-done | bytes 5152 | tf_op jit(solution)/shard_map/ppermute | solution.py:15
  88.8 10.3 %psum.38 = f32[48,80]{1,0:T(8,128)S(1)} all-reduce(f32[48,80]{1,0:T(8,128)S(1)} %pad_maximum_fusion.3), channel_id=1, replica_groups=mesh['elem'=8,'face'=4] {'face'}, use_global_device_ids=true, to_apply=%region_3.4 | all-reduce | flops 3840 | bytes 30720 | tf_op jit(solution)/shard_map/psum | solution.py:53
  99.3 6.1 %collective-permute-done.7 = bf16[16,80]{1,0:T(8,128)(2,1)S(1)} collective-permute-done((bf16[16,80]{1,0:T(8,128)(2,1)S(1)}, bf16[16,80]{1,0:T(8,128)(2,1)S(1)}, u32[]{:S(2)}, u32[]{:S(2)}) %collective-permute-start.7) | collective-permute-done | bytes 2592 | tf_op jit(solution)/shard_map/ppermute | solution.py:15
  106.7 3.4 %collective-permute-done.8 = f32[16,80]{1,0:T(8,128)S(1)} collective-permute-done((f32[16,80]{1,0:T(8,128)S(1)}, f32[16,80]{1,0:T(8,128)S(1)}, u32[]{:S(2)}, u32[]{:S(2)}) %collective-permute-start.8) | collective-permute-done | bytes 5152 | tf_op jit(solution)/shard_map/ppermute | solution.py:15
  110.1 10.3 %psum.39 = f32[48,80]{1,0:T(8,128)S(1)} all-reduce(f32[48,80]{1,0:T(8,128)S(1)} %pad_maximum_fusion.4), channel_id=1, replica_groups=mesh['elem'=8,'face'=4] {'face'}, use_global_device_ids=true, to_apply=%region_4.5 | all-reduce | flops 3840 | bytes 30720 | tf_op jit(solution)/shard_map/psum | solution.py:53
  120.6 0.6 constant_dynamic-slice_fusion
  121.2 5.7 %collective-permute-done.9 = bf16[16,80]{1,0:T(8,128)(2,1)S(1)} collective-permute-done((bf16[16,80]{1,0:T(8,128)(2,1)S(1)}, bf16[16,80]{1,0:T(8,128)(2,1)S(1)}, u32[]{:S(2)}, u32[]{:S(2)}) %collective-permute-start.9) | collective-permute-done | bytes 2592 | tf_op jit(solution)/shard_map/ppermute | solution.py:15
  127.2 1.8 %fusion.50 = f32[4,1,320]{2,1,0:T(1,128)S(1)} fusion(bf16[4,320,480]{2,1,0:T(8,128)(2,1)} %copy-done.1, bf16[4,480,1]{1,2,0:T(2,128)(2,1)S(1)} %reshape.86), kind=kOutput, calls=%fused_computation.84 | convolution fusion | flops 1228800 | bytes 1237760 | tf_op jit(solution)/shard_map/evt,et->ev/dot_general | solution.py:94
  128.9 0.6 bitcast_subtract_fusion
  (92 shorter events, 7.5 us)
Async XLA Ops:
  0.6 1.8 %copy-start = (bf16[4,480,320]{1,2,0:T(8,128)(2,1)S(1)}, bf16[4,480,320]{1,2,0:T(8,128)(2,1)}, u32[]{:S(2)}) copy-start(bf16[4,480,320]{1,2,0:T(8,128)(2,1)} %param.9) | copy-start | bytes 3686404
  0.6 2.2 %copy-start.5 = (s32[4,6]{1,0:T(4,128)S(1)}, s32[4,6]{1,0:T(4,128)}, u32[]{:S(2)}) copy-start(s32[4,6]{1,0:T(4,128)} %param.11) | copy-start | bytes 292
  0.7 8.9 %copy-start.3 = (f32[12,80]{1,0:T(8,128)S(1)}, f32[12,80]{1,0:T(8,128)}, u32[]{:S(2)}) copy-start(f32[12,80]{1,0:T(8,128)} %param.13) | copy-start | bytes 11524
  0.7 14.1 %copy-start.2 = (bf16[4,320,320]{2,1,0:T(8,128)(2,1)S(1)}, bf16[4,320,320]{2,1,0:T(8,128)(2,1)}, u32[]{:S(2)}) copy-start(bf16[4,320,320]{2,1,0:T(8,128)(2,1)} %param.7) | copy-start | bytes 2457604
  3.2 20.3 %collective-permute-start = (f32[16,80]{1,0:T(8,128)S(1)}, f32[16,80]{1,0:T(8,128)S(1)}, u32[]{:S(2)}, u32[]{:S(2)}) collective-permute-start(f32[16,80]{1,0:T(8,128)S(1)} %fusion.9), channel_id=1, source_target_pairs={{4,0},{8,4},{12,8},{16,12},{20,16},{24,20},{28,24},{0,28},{5,1},{9... | collective-permute-start | bytes 15368 | tf_op jit(solution)/shard_map/ppermute | solution.py:15
  16.9 1.3 copy-start.1
  16.9 1.3 copy-start.4
  35.0 6.4 %collective-permute-start.1 = (bf16[16,80]{1,0:T(8,128)(2,1)S(1)}, bf16[16,80]{1,0:T(8,128)(2,1)S(1)}, u32[]{:S(2)}, u32[]{:S(2)}) collective-permute-start(bf16[16,80]{1,0:T(8,128)(2,1)S(1)} %slice.62), channel_id=1, source_target_pairs={{28,0},{0,4},{4,8},{8,12},{12,16},{16,20},{20,24},{24,28},{29,1},{... | collective-permute-start | bytes 7688 | tf_op jit(solution)/shard_map/ppermute | solution.py:15
  42.4 3.7 %collective-permute-start.2 = (f32[16,80]{1,0:T(8,128)S(1)}, f32[16,80]{1,0:T(8,128)S(1)}, u32[]{:S(2)}, u32[]{:S(2)}) collective-permute-start(f32[16,80]{1,0:T(8,128)S(1)} %fusion.8), channel_id=1, source_target_pairs={{4,0},{8,4},{12,8},{16,12},{20,16},{24,20},{28,24},{0,28},{5,1},{9... | collective-permute-start | bytes 15368 | tf_op jit(solution)/shard_map/ppermute | solution.py:15
  56.4 6.4 %collective-permute-start.3 = (bf16[16,80]{1,0:T(8,128)(2,1)S(1)}, bf16[16,80]{1,0:T(8,128)(2,1)S(1)}, u32[]{:S(2)}, u32[]{:S(2)}) collective-permute-start(bf16[16,80]{1,0:T(8,128)(2,1)S(1)} %slice.65), channel_id=1, source_target_pairs={{28,0},{0,4},{4,8},{8,12},{12,16},{16,20},{20,24},{24,28},{29,1},{... | collective-permute-start | bytes 7688 | tf_op jit(solution)/shard_map/ppermute | solution.py:15
  63.8 3.7 %collective-permute-start.4 = (f32[16,80]{1,0:T(8,128)S(1)}, f32[16,80]{1,0:T(8,128)S(1)}, u32[]{:S(2)}, u32[]{:S(2)}) collective-permute-start(f32[16,80]{1,0:T(8,128)S(1)} %fusion.7), channel_id=1, source_target_pairs={{4,0},{8,4},{12,8},{16,12},{20,16},{24,20},{28,24},{0,28},{5,1},{9... | collective-permute-start | bytes 15368 | tf_op jit(solution)/shard_map/ppermute | solution.py:15
  77.7 6.4 %collective-permute-start.5 = (bf16[16,80]{1,0:T(8,128)(2,1)S(1)}, bf16[16,80]{1,0:T(8,128)(2,1)S(1)}, u32[]{:S(2)}, u32[]{:S(2)}) collective-permute-start(bf16[16,80]{1,0:T(8,128)(2,1)S(1)} %slice.68), channel_id=1, source_target_pairs={{28,0},{0,4},{4,8},{8,12},{12,16},{16,20},{20,24},{24,28},{29,1},{... | collective-permute-start | bytes 7688 | tf_op jit(solution)/shard_map/ppermute | solution.py:15
  85.1 3.7 %collective-permute-start.6 = (f32[16,80]{1,0:T(8,128)S(1)}, f32[16,80]{1,0:T(8,128)S(1)}, u32[]{:S(2)}, u32[]{:S(2)}) collective-permute-start(f32[16,80]{1,0:T(8,128)S(1)} %fusion.6), channel_id=1, source_target_pairs={{4,0},{8,4},{12,8},{16,12},{20,16},{24,20},{28,24},{0,28},{5,1},{9... | collective-permute-start | bytes 15368 | tf_op jit(solution)/shard_map/ppermute | solution.py:15
  99.1 6.4 %collective-permute-start.7 = (bf16[16,80]{1,0:T(8,128)(2,1)S(1)}, bf16[16,80]{1,0:T(8,128)(2,1)S(1)}, u32[]{:S(2)}, u32[]{:S(2)}) collective-permute-start(bf16[16,80]{1,0:T(8,128)(2,1)S(1)} %slice.71), channel_id=1, source_target_pairs={{28,0},{0,4},{4,8},{8,12},{12,16},{16,20},{20,24},{24,28},{29,1},{... | collective-permute-start | bytes 7688 | tf_op jit(solution)/shard_map/ppermute | solution.py:15
  106.4 3.7 %collective-permute-start.8 = (f32[16,80]{1,0:T(8,128)S(1)}, f32[16,80]{1,0:T(8,128)S(1)}, u32[]{:S(2)}, u32[]{:S(2)}) collective-permute-start(f32[16,80]{1,0:T(8,128)S(1)} %fusion.5), channel_id=1, source_target_pairs={{4,0},{8,4},{12,8},{16,12},{20,16},{24,20},{28,24},{0,28},{5,1},{9... | collective-permute-start | bytes 15368 | tf_op jit(solution)/shard_map/ppermute | solution.py:15
  120.6 6.3 %collective-permute-start.9 = (bf16[16,80]{1,0:T(8,128)(2,1)S(1)}, bf16[16,80]{1,0:T(8,128)(2,1)S(1)}, u32[]{:S(2)}, u32[]{:S(2)}) collective-permute-start(bf16[16,80]{1,0:T(8,128)(2,1)S(1)} %slice.74), channel_id=1, source_target_pairs={{28,0},{0,4},{4,8},{8,12},{12,16},{16,20},{20,24},{24,28},{29,1},{... | collective-permute-start | bytes 7688 | tf_op jit(solution)/shard_map/ppermute | solution.py:15
where the time goes:
time: 130 us
  blocking collectives  63.1 us (49%)
  waiting for transfers between devices  43.5 us (33%)
  matrix products  13.1 us (10%)
  starting transfers between devices  6.32 us (5%)
  local copies, waits for them, and re-layouts  1.75 us (1%)
    psum x5, blocking collectives, assemble(): summed = lax.psum(partial_value, 'face')  52.7 us
    ppermute x10, waiting for transfers between devices, shifted(): return lax.ppermute(block, axis, route)  43.5 us
    ppermute x10, starting transfers between devices, shifted(): return lax.ppermute(block, axis, route)  6.32 us
    all_gather x1, blocking collectives, local(): lax.all_gather(trace_residual, 'face', axis=0, tiled=True)  5.19 us
    all_gather x1, blocking collectives, local(): lax.all_gather(stabilization, 'face', axis=0, tiled=True)  5.19 us
  transfers between devices with their start and end apart: 10, of which 9 were waited for; matrix products, arithmetic and copies ran while one was open for 5% of the time, Pallas kernels for 0%

commit v1 on v0

v1 whole, which is shorter than its diff:
```python
import jax
import jax.numpy as jnp
from jax import lax
from jax.sharding import PartitionSpec as P

SWEEPS = 5
AXES = ("elem", "face")
CORES = 2


def partners(groups, chips, offset, shifts):
    route = []
    for group in range(groups):
        side = 1 if (group - offset) % 2 == 0 else -1
        other = (group + side) % groups
        for chip in range(chips):
            for core in range(CORES):
                target = (chip + side * shifts[core]) % chips
                route.append(
                    (
                        (group * chips + chip) * CORES + core,
                        (other * chips + target) * CORES + core,
                    )
                )
    return route


def along_x(groups, chips, shift):
    return [
        (
            (group * chips + chip) * CORES + core,
            (group * chips + (chip + shift) % chips) * CORES + (core + 1) % CORES,
        )
        for group in range(groups)
        for chip in range(chips)
        for core in range(CORES)
    ]


def other_core(groups, chips):
    count = groups * chips
    return [(chip * CORES + core, chip * CORES + 1 - core) for chip in range(count) for core in range(CORES)]


def local(
    vol_inverse,
    vol_from_trace,
    trace_from_vol,
    vol_residual,
    face_ids,
    trace_residual,
    stabilization,
):
    groups = lax.axis_size("elem")
    members = lax.axis_size("face")
    chips = members // CORES
    elem_count, side_count = face_ids.shape
    own_faces, width = trace_residual.shape
    group_faces = own_faces * members
    border = elem_count * members
    rows = group_faces + border
    group_index = lax.axis_index("elem")
    member = lax.axis_index("face")
    lower_group = (group_index + groups - 1) % groups
    even = group_index % 2 == 0

    def swap_core(block):
        return lax.ppermute(block, AXES, other_core(groups, chips))

    def total(part):
        first, last = part[:border], part[group_faces:]
        to_first = jnp.where(even, first, last)
        to_second = jnp.where(even, last, first)
        from_second = from_first = 0.0
        for shift in range(0, chips, CORES):
            shifts = [shift + core for core in range(CORES)]
            got = lax.ppermute(to_second, AXES, partners(groups, chips, 1, shifts))
            from_second = from_second + got + swap_core(got)
        for shift in range(0, chips, CORES):
            shifts = [shift + core for core in range(CORES)]
            got = lax.ppermute(to_first, AXES, partners(groups, chips, 0, shifts))
            from_first = from_first + got + swap_core(got)
        own = part
        for shift in range(1, chips):
            own = own + lax.ppermute(part, AXES, along_x(groups, chips, shift))
        upper = jnp.where(even, from_first, from_second)
        lower = jnp.where(even, from_second, from_first)
        return jnp.concatenate(
            [own[:border] + upper, own[border:group_faces], own[group_faces:] + lower], axis=0
        )

    def row_of(ids):
        own = ids - group_index * group_faces
        low = ids - lower_group * group_faces
        inside = (own >= 0) & (own < group_faces)
        return jnp.where(inside, own, low + group_faces)

    own_rows = row_of(face_ids)
    own_hits = (
        own_rows.reshape(-1)[:, None] == lax.broadcasted_iota(jnp.int32, (1, rows), 1)
    ).astype(jnp.float32)

    local_part = jnp.einsum(
        "evk,ek->ev", vol_inverse, vol_residual, preferred_element_type=jnp.float32
    )
    trace_load = jnp.einsum(
        "etv,ev->et",
        trace_from_vol,
        local_part.astype(jnp.bfloat16),
        preferred_element_type=jnp.float32,
    )
    load_sums = jnp.einsum(
        "sf,sw->fw", own_hits, trace_load.reshape(-1, width), precision=lax.Precision.HIGHEST
    )
    blank = jnp.zeros((rows, width), jnp.float32)
    place = member * own_faces
    residual_rows = lax.dynamic_update_slice(blank, trace_residual, (place, 0))
    stab_rows = lax.dynamic_update_slice(blank, stabilization, (place, 0))
    slots = elem_count * side_count
    id_column = jnp.pad(own_rows.reshape(slots, 1).astype(jnp.float32), ((0, rows - slots), (0, 0)))
    packet = jnp.concatenate([residual_rows - load_sums, stab_rows, id_column], axis=1)
    mate = swap_core(packet)
    first_total = total((packet + mate)[:, : 2 * width])
    mate_rows = mate[:slots, 2 * width].astype(jnp.int32)
    hits = jnp.concatenate([own_rows.reshape(-1), mate_rows])[:, None] == lax.broadcasted_iota(
        jnp.int32, (1, rows), 1
    )
    hits_half = hits.astype(jnp.bfloat16)
    hits_float = hits.astype(jnp.float32)

    couple = jnp.einsum(
        "evk,ekt->evt", vol_inverse, vol_from_trace, preferred_element_type=jnp.float32
    ).astype(jnp.bfloat16)
    schur_own = jnp.einsum(
        "etv,evs->ets", trace_from_vol, couple, preferred_element_type=jnp.float32
    ).astype(jnp.bfloat16)
    schur_mate = swap_core(schur_own)

    right_side = first_total[:, :width]
    inverse_stab = 1.0 / first_total[:, width:]

    def gather(trace_now):
        values = jnp.dot(hits_half, trace_now.astype(jnp.bfloat16), preferred_element_type=jnp.float32)
        return values.astype(jnp.bfloat16).reshape(2 * elem_count, side_count * width)

    trace_now = right_side * inverse_stab
    for _ in range(SWEEPS - 1):
        lam = gather(trace_now)
        image = jnp.concatenate(
            [
                jnp.einsum("ets,es->et", block, part, preferred_element_type=jnp.float32)
                for block, part in ((schur_own, lam[:elem_count]), (schur_mate, lam[elem_count:]))
            ]
        )
        image_sums = jnp.einsum(
            "sf,sw->fw", hits_float, image.reshape(-1, width), precision=lax.Precision.HIGHEST
        )
        trace_now = (right_side + total(image_sums)) * inverse_stab
    lam = gather(trace_now)[:elem_count]
    vol_update = local_part - jnp.einsum(
        "evt,et->ev", couple, lam, preferred_element_type=jnp.float32
    )
    return lax.dynamic_slice_in_dim(trace_now, place, own_faces, 0), vol_update


def solution(mesh):
    in_specs = (
        P(AXES, None, None),
        P(AXES, None, None),
        P(AXES, None, None),
        P(AXES, None),
        P(AXES, None),
        P(AXES, None),
        P(AXES, None),
    )
    out_specs = (P(AXES, None), P(AXES, None))
    return jax.shard_map(local, mesh=mesh, in_specs=in_specs, out_specs=out_specs, check_vma=False)
```

time: 130 us -> 68.9 us (0.53)
  blocking collectives: 63.1 us -> 0 us
  waiting for transfers between devices: 43.5 us -> 15.1 us
  starting transfers between devices: 6.32 us -> 30.6 us
  matrix products: 13.1 us -> 17.3 us
  other arithmetic: 0.75 us -> 2.14 us
    psum x5 -> x0, blocking collectives: 52.7 us -> none  [assemble(): summed = lax.psum(partial_value, 'face')]
    ppermute x10 -> x27, waiting for transfers between devices: 43.5 us -> 15.1 us  [the longest x5 10.2 us: total(): got = lax.ppermute(to_second, AXES, partners(groups, chips, 1, shifts))]
    ppermute x10 -> x27, starting transfers between devices: 6.32 us -> 30.6 us  [the longest x5 17.7 us: total(): got = lax.ppermute(to_second, AXES, partners(groups, chips, 1, shifts))]
    all_gather x2 -> x0, blocking collectives: 10.4 us -> none  [the longest x1 5.19 us: local(): lax.all_gather(trace_residual, 'face', axis=0, tiled=True)]
    dot_general x25 -> x19, matrix products: 7.76 us -> 12.1 us  [the longest x8 9.19 us: local(): jnp.einsum('ets,es->et', block, part, preferred_element_type=jnp.float32)]
  transfers between devices with their start and end apart: 10 -> 27, of which waited for: 9 -> 13; matrix products, arithmetic and copies ran while one was open for 5% -> 7% of each run, Pallas kernels for 0% -> 0%
where the time goes in v1:
time: 68.9 us; the launch traced here: 68.6 us
  starting transfers between devices  30.6 us (44%)
  matrix products  17.3 us (25%)
  waiting for transfers between devices  15.1 us (22%)
  local copies, waits for them, and re-layouts  2.49 us (4%)
  other arithmetic  2.14 us (3%)
  between operations  1.01 us (1%)
    ppermute x5, starting transfers between devices, total(): got = lax.ppermute(to_second, AXES, partners(groups, chips, 1, shifts))  17.7 us
    ppermute x5, waiting for transfers between devices, total(): got = lax.ppermute(to_second, AXES, partners(groups, chips, 1, shifts))  10.2 us
    dot_general x8, matrix products, local(): jnp.einsum('ets,es->et', block, part, preferred_element_type=jnp.float32)  9.19 us
    ppermute x5, starting transfers between devices, total(): own = own + lax.ppermute(part, AXES, along_x(groups, chips, shift))  5.25 us
    ppermute x12, waiting for transfers between devices, swap_core(): return lax.ppermute(block, AXES, other_core(groups, chips))  3.98 us
    ppermute x5, starting transfers between devices, total(): got = lax.ppermute(to_first, AXES, partners(groups, chips, 0, shifts))  3.86 us
    ppermute x12, starting transfers between devices, swap_core(): return lax.ppermute(block, AXES, other_core(groups, chips))  3.85 us
    dot_general x1, matrix products, local(): jnp.einsum('evk,ekt->evt', vol_inverse, vol_from_trace, preferred_element...  2.14 us
  transfers between devices with their start and end apart: 27, of which 13 were waited for; matrix products, arithmetic and copies ran while one was open for 7% of the time, Pallas kernels for 0%

profile of v1, /device:TPU:0, one launch (start us, length us, event | category | flops | bytes accessed | tf_op | source)
XLA Modules:
  0.0 68.6 jit_solution(7447063629383379630)
XLA Ops:
  1.6 1.6 %fusion.28 = f32[4,1,320]{2,1,0:T(1,128)S(1)} fusion(bf16[4,320,320]{2,1,0:T(8,128)(2,1)} %param.7, bf16[4,320,1]{1,0,2:T(4,128)(2,1)} %bitcast.78), kind=kOutput, calls=%fused_computation.80 | convolution fusion | flops 819200 | bytes 826880 | tf_op jit(solution)/shard_map/evk,ek->ev/dot_general | solution.py:103
  5.0 2.1 %convolution_convert_fusion.1 = bf16[4,320,480]{2,1,0:T(8,128)(2,1)S(1)} fusion(bf16[4,320,320]{2,1,0:T(8,128)(2,1)S(1)} %copy-done.3, bf16[4,320,480]{2,1,0:T(8,128)(2,1)} %param.8), kind=kOutput, calls=%fused_computation.1 | convolution fusion | flops 393830400 | bytes 3276800 | tf_op jit(solution)/shard_map/evk,ekt->evt/dot_general | solution.py:131
  7.2 1.2 %convolution_convert_fusion = bf16[4,480,480]{2,1,0:T(8,128)(2,1)S(1)} fusion(bf16[4,320,480]{2,1,0:T(8,128)(2,1)S(1)} %convolution_convert_fusion.1, bf16[4,480,320]{1,2,0:T(8,128)(2,1)S(1)} %copy-done), kind=kOutput, calls=%fused_computation | convolution fusion | flops 590745600 | bytes 4300800 | tf_op jit(solution)/shard_map/etv,evs->ets/dot_general | solution.py:134
  8.7 3.0 %collective-permute-start.2 = (f32[16,160]{1,0:T(8,128)S(1)}, f32[16,160]{1,0:T(8,128)S(1)}, u32[]{:S(2)}, u32[]{:S(2)}) collective-permute-start(f32[16,160]{1,0:T(8,128)S(1)} %get-tuple-element.14), channel_id=1, source_target_pairs={{0,4},{1,7},{2,6},{3,5},{4,0},{5,3},{6,2},{7,1},{8,12},{9,15},{10,... | collective-permute-start | bytes 30728 | tf_op jit(solution)/shard_map/ppermute | solution.py:81
  11.7 3.6 %collective-permute-start.4 = (f32[16,160]{1,0:T(8,128)S(1)}, f32[16,160]{1,0:T(8,128)S(1)}, u32[]{:S(2)}, u32[]{:S(2)}) collective-permute-start(f32[16,160]{1,0:T(8,128)S(1)} %get-tuple-element.15), channel_id=1, source_target_pairs={{0,28},{1,31},{2,30},{3,29},{4,8},{5,11},{6,10},{7,9},{8,4},{9,7},... | collective-permute-start | bytes 30728 | tf_op jit(solution)/shard_map/ppermute | solution.py:77
  15.2 1.5 %collective-permute-start.1 = (f32[64,160]{1,0:T(8,128)S(1)}, f32[64,160]{1,0:T(8,128)S(1)}, u32[]{:S(2)}, u32[]{:S(2)}) collective-permute-start(f32[64,160]{1,0:T(8,128)S(1)} %bitcast.69), channel_id=1, source_target_pairs={{0,3},{1,2},{2,1},{3,0},{4,7},{5,6},{6,5},{7,4},{8,11},{9,10},{10,... | collective-permute-start | bytes 122888 | tf_op jit(solution)/shard_map/ppermute | solution.py:85
  17.1 1.0 %collective-permute-done.4 = f32[16,160]{1,0:T(8,128)S(1)} collective-permute-done((f32[16,160]{1,0:T(8,128)S(1)}, f32[16,160]{1,0:T(8,128)S(1)}, u32[]{:S(2)}, u32[]{:S(2)}) %collective-permute-start.4) | collective-permute-done | bytes 10272 | tf_op jit(solution)/shard_map/ppermute | solution.py:77
  20.2 1.9 %fusion.41 = f32[4,1,480]{2,1,0:T(1,128)S(1)} fusion(bf16[4,480,480]{1,2,0:T(8,128)(2,1)} %collective-permute-done.6, bf16[4,480,1]{1,2,0:T(2,128)(2,1)S(1)} %reshape.81), kind=kOutput, calls=%fused_computation.98 | convolution fusion | flops 1843200 | bytes 1854720 | tf_op jit(solution)/shard_map/ets,es->et/dot_general | solution.py:151
  22.5 1.3 %collective-permute-start.7 = (f32[64,80]{1,0:T(8,128)S(1)}, f32[64,80]{1,0:T(8,128)S(1)}, u32[]{:S(2)}, u32[]{:S(2)}) collective-permute-start(f32[64,80]{1,0:T(8,128)S(1)} %fusion.11), channel_id=1, source_target_pairs={{0,3},{1,2},{2,1},{3,0},{4,7},{5,6},{6,5},{7,4},{8,11},{9,10},{10,... | collective-permute-start | bytes 61448 | tf_op jit(solution)/shard_map/ppermute | solution.py:85
  23.8 3.5 %collective-permute-start.10 = (f32[16,80]{1,0:T(8,128)S(1)}, f32[16,80]{1,0:T(8,128)S(1)}, u32[]{:S(2)}, u32[]{:S(2)}) collective-permute-start(f32[16,80]{1,0:T(8,128)S(1)} %get-tuple-element.23), channel_id=1, source_target_pairs={{0,28},{1,31},{2,30},{3,29},{4,8},{5,11},{6,10},{7,9},{8,4},{9,7},... | collective-permute-start | bytes 15368 | tf_op jit(solution)/shard_map/ppermute | solution.py:77
  27.7 2.4 %collective-permute-done.10 = f32[16,80]{1,0:T(8,128)S(1)} collective-permute-done((f32[16,80]{1,0:T(8,128)S(1)}, f32[16,80]{1,0:T(8,128)S(1)}, u32[]{:S(2)}, u32[]{:S(2)}) %collective-permute-start.10) | collective-permute-done | bytes 5152 | tf_op jit(solution)/shard_map/ppermute | solution.py:77
  30.3 1.0 %collective-permute-done.11 = f32[16,80]{1,0:T(8,128)S(1)} collective-permute-done((f32[16,80]{1,0:T(8,128)S(1)}, f32[16,80]{1,0:T(8,128)S(1)}, u32[]{:S(2)}, u32[]{:S(2)}) %collective-permute-start.11) | collective-permute-done | bytes 5152 | tf_op jit(solution)/shard_map/ppermute | solution.py:68
  32.1 1.9 %fusion.43 = f32[4,1,480]{2,1,0:T(1,128)S(1)} fusion(bf16[4,480,480]{1,2,0:T(8,128)(2,1)} %collective-permute-done.6, bf16[4,480,1]{1,2,0:T(2,128)(2,1)S(1)} %reshape.85), kind=kOutput, calls=%fused_computation.100 | convolution fusion | flops 1843200 | bytes 1854720 | tf_op jit(solution)/shard_map/ets,es->et/dot_general | solution.py:151
  35.6 3.6 %collective-permute-start.15 = (f32[16,80]{1,0:T(8,128)S(1)}, f32[16,80]{1,0:T(8,128)S(1)}, u32[]{:S(2)}, u32[]{:S(2)}) collective-permute-start(f32[16,80]{1,0:T(8,128)S(1)} %get-tuple-element.21), channel_id=1, source_target_pairs={{0,28},{1,31},{2,30},{3,29},{4,8},{5,11},{6,10},{7,9},{8,4},{9,7},... | collective-permute-start | bytes 15368 | tf_op jit(solution)/shard_map/ppermute | solution.py:77
  39.7 2.3 %collective-permute-done.15 = f32[16,80]{1,0:T(8,128)S(1)} collective-permute-done((f32[16,80]{1,0:T(8,128)S(1)}, f32[16,80]{1,0:T(8,128)S(1)}, u32[]{:S(2)}, u32[]{:S(2)}) %collective-permute-start.15) | collective-permute-done | bytes 5152 | tf_op jit(solution)/shard_map/ppermute | solution.py:77
  43.9 1.9 %fusion.45 = f32[4,1,480]{2,1,0:T(1,128)S(1)} fusion(bf16[4,480,480]{1,2,0:T(8,128)(2,1)} %collective-permute-done.6, bf16[4,480,1]{1,2,0:T(2,128)(2,1)S(1)} %reshape.89), kind=kOutput, calls=%fused_computation.102 | convolution fusion | flops 1843200 | bytes 1854720 | tf_op jit(solution)/shard_map/ets,es->et/dot_general | solution.py:151
  46.2 0.9 %collective-permute-start.17 = (f32[64,80]{1,0:T(8,128)S(1)}, f32[64,80]{1,0:T(8,128)S(1)}, u32[]{:S(2)}, u32[]{:S(2)}) collective-permute-start(f32[64,80]{1,0:T(8,128)S(1)} %fusion.9), channel_id=1, source_target_pairs={{0,3},{1,2},{2,1},{3,0},{4,7},{5,6},{6,5},{7,4},{8,11},{9,10},{10,... | collective-permute-start | bytes 61448 | tf_op jit(solution)/shard_map/ppermute | solution.py:85
  47.1 3.5 %collective-permute-start.20 = (f32[16,80]{1,0:T(8,128)S(1)}, f32[16,80]{1,0:T(8,128)S(1)}, u32[]{:S(2)}, u32[]{:S(2)}) collective-permute-start(f32[16,80]{1,0:T(8,128)S(1)} %get-tuple-element.19), channel_id=1, source_target_pairs={{0,28},{1,31},{2,30},{3,29},{4,8},{5,11},{6,10},{7,9},{8,4},{9,7},... | collective-permute-start | bytes 15368 | tf_op jit(solution)/shard_map/ppermute | solution.py:77
  51.2 2.3 %collective-permute-done.20 = f32[16,80]{1,0:T(8,128)S(1)} collective-permute-done((f32[16,80]{1,0:T(8,128)S(1)}, f32[16,80]{1,0:T(8,128)S(1)}, u32[]{:S(2)}, u32[]{:S(2)}) %collective-permute-start.20) | collective-permute-done | bytes 5152 | tf_op jit(solution)/shard_map/ppermute | solution.py:77
  53.6 1.0 %collective-permute-done.21 = f32[16,80]{1,0:T(8,128)S(1)} collective-permute-done((f32[16,80]{1,0:T(8,128)S(1)}, f32[16,80]{1,0:T(8,128)S(1)}, u32[]{:S(2)}, u32[]{:S(2)}) %collective-permute-start.21) | collective-permute-done | bytes 5152 | tf_op jit(solution)/shard_map/ppermute | solution.py:68
  55.4 2.0 %fusion.47 = f32[4,1,480]{2,1,0:T(1,128)S(1)} fusion(bf16[4,480,480]{1,2,0:T(8,128)(2,1)} %collective-permute-done.6, bf16[4,480,1]{1,2,0:T(2,128)(2,1)S(1)} %reshape.93), kind=kOutput, calls=%fused_computation.104 | convolution fusion | flops 1843200 | bytes 1854720 | tf_op jit(solution)/shard_map/ets,es->et/dot_general | solution.py:151
  57.8 0.9 %collective-permute-start.22 = (f32[64,80]{1,0:T(8,128)S(1)}, f32[64,80]{1,0:T(8,128)S(1)}, u32[]{:S(2)}, u32[]{:S(2)}) collective-permute-start(f32[64,80]{1,0:T(8,128)S(1)} %fusion.8), channel_id=1, source_target_pairs={{0,3},{1,2},{2,1},{3,0},{4,7},{5,6},{6,5},{7,4},{8,11},{9,10},{10,... | collective-permute-start | bytes 61448 | tf_op jit(solution)/shard_map/ppermute | solution.py:85
  59.0 3.5 %collective-permute-start.25 = (f32[16,80]{1,0:T(8,128)S(1)}, f32[16,80]{1,0:T(8,128)S(1)}, u32[]{:S(2)}, u32[]{:S(2)}) collective-permute-start(f32[16,80]{1,0:T(8,128)S(1)} %get-tuple-element.17), channel_id=1, source_target_pairs={{0,28},{1,31},{2,30},{3,29},{4,8},{5,11},{6,10},{7,9},{8,4},{9,7},... | collective-permute-start | bytes 15368 | tf_op jit(solution)/shard_map/ppermute | solution.py:77
  63.2 2.2 %collective-permute-done.25 = f32[16,80]{1,0:T(8,128)S(1)} collective-permute-done((f32[16,80]{1,0:T(8,128)S(1)}, f32[16,80]{1,0:T(8,128)S(1)}, u32[]{:S(2)}, u32[]{:S(2)}) %collective-permute-start.25) | collective-permute-done | bytes 5152 | tf_op jit(solution)/shard_map/ppermute | solution.py:77
  (132 shorter events, 17.4 us)
Async XLA Ops:
  4.5 4.1 %collective-permute-start = (f32[64,161]{1,0:T(8,128)S(1)}, f32[64,161]{1,0:T(8,128)S(1)}, u32[]{:S(2)}, u32[]{:S(2)}) collective-permute-start(f32[64,161]{1,0:T(8,128)S(1)} %select_maximum_fusion), channel_id=1, source_target_pairs={{0,1},{1,0},{2,3},{3,2},{4,5},{5,4},{6,7},{7,6},{8,9},{9,8},{10,11... | collective-permute-start | bytes 123656 | tf_op jit(solution)/shard_map/ppermute | solution.py:68
  8.4 11.8 %collective-permute-start.6 = (bf16[4,480,480]{1,2,0:T(8,128)(2,1)S(1)}, bf16[4,480,480]{1,2,0:T(8,128)(2,1)}, u32[]{:S(2)}, u32[]{:S(2)}) collective-permute-start(bf16[4,480,480]{1,2,0:T(8,128)(2,1)S(1)} %bitcast.68), channel_id=1, source_target_pairs={{0,1},{1,0},{2,3},{3,2},{4,5},{5,4},{6,7},{7,6},{8,9},{9,8},{10,11... | collective-permute-start | bytes 5529608 | tf_op jit(solution)/shard_map/ppermute | solution.py:68
  8.7 8.3 %collective-permute-start.2 = (f32[16,160]{1,0:T(8,128)S(1)}, f32[16,160]{1,0:T(8,128)S(1)}, u32[]{:S(2)}, u32[]{:S(2)}) collective-permute-start(f32[16,160]{1,0:T(8,128)S(1)} %get-tuple-element.14), channel_id=1, source_target_pairs={{0,4},{1,7},{2,6},{3,5},{4,0},{5,3},{6,2},{7,1},{8,12},{9,15},{10,... | collective-permute-start | bytes 30728 | tf_op jit(solution)/shard_map/ppermute | solution.py:81
  11.7 6.4 %collective-permute-start.4 = (f32[16,160]{1,0:T(8,128)S(1)}, f32[16,160]{1,0:T(8,128)S(1)}, u32[]{:S(2)}, u32[]{:S(2)}) collective-permute-start(f32[16,160]{1,0:T(8,128)S(1)} %get-tuple-element.15), channel_id=1, source_target_pairs={{0,28},{1,31},{2,30},{3,29},{4,8},{5,11},{6,10},{7,9},{8,4},{9,7},... | collective-permute-start | bytes 30728 | tf_op jit(solution)/shard_map/ppermute | solution.py:77
  15.2 3.9 %collective-permute-start.1 = (f32[64,160]{1,0:T(8,128)S(1)}, f32[64,160]{1,0:T(8,128)S(1)}, u32[]{:S(2)}, u32[]{:S(2)}) collective-permute-start(f32[64,160]{1,0:T(8,128)S(1)} %bitcast.69), channel_id=1, source_target_pairs={{0,3},{1,2},{2,1},{3,0},{4,7},{5,6},{6,5},{7,4},{8,11},{9,10},{10,... | collective-permute-start | bytes 122888 | tf_op jit(solution)/shard_map/ppermute | solution.py:85
  17.0 2.2 %collective-permute-start.3 = (f32[16,160]{1,0:T(8,128)S(1)}, f32[16,160]{1,0:T(8,128)S(1)}, u32[]{:S(2)}, u32[]{:S(2)}) collective-permute-start(f32[16,160]{1,0:T(8,128)S(1)} %collective-permute-done.2), channel_id=1, source_target_pairs={{0,1},{1,0},{2,3},{3,2},{4,5},{5,4},{6,7},{7,6},{8,9},{9,8},{10,11... | collective-permute-start | bytes 30728 | tf_op jit(solution)/shard_map/ppermute | solution.py:68
  18.1 1.3 %collective-permute-start.5 = (f32[16,160]{1,0:T(8,128)S(1)}, f32[16,160]{1,0:T(8,128)S(1)}, u32[]{:S(2)}, u32[]{:S(2)}) collective-permute-start(f32[16,160]{1,0:T(8,128)S(1)} %collective-permute-done.4), channel_id=1, source_target_pairs={{0,1},{1,0},{2,3},{3,2},{4,5},{5,4},{6,7},{7,6},{8,9},{9,8},{10,11... | collective-permute-start | bytes 30728 | tf_op jit(solution)/shard_map/ppermute | solution.py:68
  22.5 7.7 %collective-permute-start.7 = (f32[64,80]{1,0:T(8,128)S(1)}, f32[64,80]{1,0:T(8,128)S(1)}, u32[]{:S(2)}, u32[]{:S(2)}) collective-permute-start(f32[64,80]{1,0:T(8,128)S(1)} %fusion.11), channel_id=1, source_target_pairs={{0,3},{1,2},{2,1},{3,0},{4,7},{5,6},{6,5},{7,4},{8,11},{9,10},{10,... | collective-permute-start | bytes 61448 | tf_op jit(solution)/shard_map/ppermute | solution.py:85
  23.8 3.7 %collective-permute-start.8 = (f32[16,80]{1,0:T(8,128)S(1)}, f32[16,80]{1,0:T(8,128)S(1)}, u32[]{:S(2)}, u32[]{:S(2)}) collective-permute-start(f32[16,80]{1,0:T(8,128)S(1)} %get-tuple-element.22), channel_id=1, source_target_pairs={{0,4},{1,7},{2,6},{3,5},{4,0},{5,3},{6,2},{7,1},{8,12},{9,15},{10,... | collective-permute-start | bytes 15368 | tf_op jit(solution)/shard_map/ppermute | solution.py:81
  23.8 6.3 %collective-permute-start.10 = (f32[16,80]{1,0:T(8,128)S(1)}, f32[16,80]{1,0:T(8,128)S(1)}, u32[]{:S(2)}, u32[]{:S(2)}) collective-permute-start(f32[16,80]{1,0:T(8,128)S(1)} %get-tuple-element.23), channel_id=1, source_target_pairs={{0,28},{1,31},{2,30},{3,29},{4,8},{5,11},{6,10},{7,9},{8,4},{9,7},... | collective-permute-start | bytes 15368 | tf_op jit(solution)/shard_map/ppermute | solution.py:77
  27.4 2.8 %collective-permute-start.9 = (f32[16,80]{1,0:T(8,128)S(1)}, f32[16,80]{1,0:T(8,128)S(1)}, u32[]{:S(2)}, u32[]{:S(2)}) collective-permute-start(f32[16,80]{1,0:T(8,128)S(1)} %collective-permute-done.8), channel_id=1, source_target_pairs={{0,1},{1,0},{2,3},{3,2},{4,5},{5,4},{6,7},{7,6},{8,9},{9,8},{10,11... | collective-permute-start | bytes 15368 | tf_op jit(solution)/shard_map/ppermute | solution.py:68
  30.1 1.2 %collective-permute-start.11 = (f32[16,80]{1,0:T(8,128)S(1)}, f32[16,80]{1,0:T(8,128)S(1)}, u32[]{:S(2)}, u32[]{:S(2)}) collective-permute-start(f32[16,80]{1,0:T(8,128)S(1)} %collective-permute-done.10), channel_id=1, source_target_pairs={{0,1},{1,0},{2,3},{3,2},{4,5},{5,4},{6,7},{7,6},{8,9},{9,8},{10,11... | collective-permute-start | bytes 15368 | tf_op jit(solution)/shard_map/ppermute | solution.py:68
  34.4 7.9 %collective-permute-start.12 = (f32[64,80]{1,0:T(8,128)S(1)}, f32[64,80]{1,0:T(8,128)S(1)}, u32[]{:S(2)}, u32[]{:S(2)}) collective-permute-start(f32[64,80]{1,0:T(8,128)S(1)} %fusion.10), channel_id=1, source_target_pairs={{0,3},{1,2},{2,1},{3,0},{4,7},{5,6},{6,5},{7,4},{8,11},{9,10},{10,... | collective-permute-start | bytes 61448 | tf_op jit(solution)/shard_map/ppermute | solution.py:85
  35.1 4.1 %collective-permute-start.13 = (f32[16,80]{1,0:T(8,128)S(1)}, f32[16,80]{1,0:T(8,128)S(1)}, u32[]{:S(2)}, u32[]{:S(2)}) collective-permute-start(f32[16,80]{1,0:T(8,128)S(1)} %get-tuple-element.20), channel_id=1, source_target_pairs={{0,4},{1,7},{2,6},{3,5},{4,0},{5,3},{6,2},{7,1},{8,12},{9,15},{10,... | collective-permute-start | bytes 15368 | tf_op jit(solution)/shard_map/ppermute | solution.py:81
  35.6 6.3 %collective-permute-start.15 = (f32[16,80]{1,0:T(8,128)S(1)}, f32[16,80]{1,0:T(8,128)S(1)}, u32[]{:S(2)}, u32[]{:S(2)}) collective-permute-start(f32[16,80]{1,0:T(8,128)S(1)} %get-tuple-element.21), channel_id=1, source_target_pairs={{0,28},{1,31},{2,30},{3,29},{4,8},{5,11},{6,10},{7,9},{8,4},{9,7},... | collective-permute-start | bytes 15368 | tf_op jit(solution)/shard_map/ppermute | solution.py:77
  39.2 3.1 %collective-permute-start.14 = (f32[16,80]{1,0:T(8,128)S(1)}, f32[16,80]{1,0:T(8,128)S(1)}, u32[]{:S(2)}, u32[]{:S(2)}) collective-permute-start(f32[16,80]{1,0:T(8,128)S(1)} %collective-permute-done.13), channel_id=1, source_target_pairs={{0,1},{1,0},{2,3},{3,2},{4,5},{5,4},{6,7},{7,6},{8,9},{9,8},{10,11... | collective-permute-start | bytes 15368 | tf_op jit(solution)/shard_map/ppermute | solution.py:68
  46.2 7.4 %collective-permute-start.17 = (f32[64,80]{1,0:T(8,128)S(1)}, f32[64,80]{1,0:T(8,128)S(1)}, u32[]{:S(2)}, u32[]{:S(2)}) collective-permute-start(f32[64,80]{1,0:T(8,128)S(1)} %fusion.9), channel_id=1, source_target_pairs={{0,3},{1,2},{2,1},{3,0},{4,7},{5,6},{6,5},{7,4},{8,11},{9,10},{10,... | collective-permute-start | bytes 61448 | tf_op jit(solution)/shard_map/ppermute | solution.py:85
  47.1 3.7 %collective-permute-start.18 = (f32[16,80]{1,0:T(8,128)S(1)}, f32[16,80]{1,0:T(8,128)S(1)}, u32[]{:S(2)}, u32[]{:S(2)}) collective-permute-start(f32[16,80]{1,0:T(8,128)S(1)} %get-tuple-element.18), channel_id=1, source_target_pairs={{0,4},{1,7},{2,6},{3,5},{4,0},{5,3},{6,2},{7,1},{8,12},{9,15},{10,... | collective-permute-start | bytes 15368 | tf_op jit(solution)/shard_map/ppermute | solution.py:81
  47.1 6.3 %collective-permute-start.20 = (f32[16,80]{1,0:T(8,128)S(1)}, f32[16,80]{1,0:T(8,128)S(1)}, u32[]{:S(2)}, u32[]{:S(2)}) collective-permute-start(f32[16,80]{1,0:T(8,128)S(1)} %get-tuple-element.19), channel_id=1, source_target_pairs={{0,28},{1,31},{2,30},{3,29},{4,8},{5,11},{6,10},{7,9},{8,4},{9,7},... | collective-permute-start | bytes 15368 | tf_op jit(solution)/shard_map/ppermute | solution.py:77
  50.8 2.8 %collective-permute-start.19 = (f32[16,80]{1,0:T(8,128)S(1)}, f32[16,80]{1,0:T(8,128)S(1)}, u32[]{:S(2)}, u32[]{:S(2)}) collective-permute-start(f32[16,80]{1,0:T(8,128)S(1)} %collective-permute-done.18), channel_id=1, source_target_pairs={{0,1},{1,0},{2,3},{3,2},{4,5},{5,4},{6,7},{7,6},{8,9},{9,8},{10,11... | collective-permute-start | bytes 15368 | tf_op jit(solution)/shard_map/ppermute | solution.py:68
  57.8 7.9 %collective-permute-start.22 = (f32[64,80]{1,0:T(8,128)S(1)}, f32[64,80]{1,0:T(8,128)S(1)}, u32[]{:S(2)}, u32[]{:S(2)}) collective-permute-start(f32[64,80]{1,0:T(8,128)S(1)} %fusion.8), channel_id=1, source_target_pairs={{0,3},{1,2},{2,1},{3,0},{4,7},{5,6},{6,5},{7,4},{8,11},{9,10},{10,... | collective-permute-start | bytes 61448 | tf_op jit(solution)/shard_map/ppermute | solution.py:85
  58.7 3.8 %collective-permute-start.23 = (f32[16,80]{1,0:T(8,128)S(1)}, f32[16,80]{1,0:T(8,128)S(1)}, u32[]{:S(2)}, u32[]{:S(2)}) collective-permute-start(f32[16,80]{1,0:T(8,128)S(1)} %get-tuple-element.16), channel_id=1, source_target_pairs={{0,4},{1,7},{2,6},{3,5},{4,0},{5,3},{6,2},{7,1},{8,12},{9,15},{10,... | collective-permute-start | bytes 15368 | tf_op jit(solution)/shard_map/ppermute | solution.py:81
  59.0 6.3 %collective-permute-start.25 = (f32[16,80]{1,0:T(8,128)S(1)}, f32[16,80]{1,0:T(8,128)S(1)}, u32[]{:S(2)}, u32[]{:S(2)}) collective-permute-start(f32[16,80]{1,0:T(8,128)S(1)} %get-tuple-element.17), channel_id=1, source_target_pairs={{0,28},{1,31},{2,30},{3,29},{4,8},{5,11},{6,10},{7,9},{8,4},{9,7},... | collective-permute-start | bytes 15368 | tf_op jit(solution)/shard_map/ppermute | solution.py:77
  62.6 3.1 %collective-permute-start.24 = (f32[16,80]{1,0:T(8,128)S(1)}, f32[16,80]{1,0:T(8,128)S(1)}, u32[]{:S(2)}, u32[]{:S(2)}) collective-permute-start(f32[16,80]{1,0:T(8,128)S(1)} %collective-permute-done.23), channel_id=1, source_target_pairs={{0,1},{1,0},{2,3},{3,2},{4,5},{5,4},{6,7},{7,6},{8,9},{9,8},{10,11... | collective-permute-start | bytes 15368 | tf_op jit(solution)/shard_map/ppermute | solution.py:68
  (9 other events, 30.2 us)

commit v2 on v1

v2 whole, which is shorter than its diff:
```python
import functools

import jax
import jax.numpy as jnp
from jax import lax
from jax.experimental import pallas as pl
from jax.experimental.pallas import tpu as pltpu
from jax.sharding import PartitionSpec as P

SWEEPS = 5
AXES = ("elem", "face")
CORES = 2
F32 = jnp.float32
HALF = jnp.bfloat16
VMEM = pl.BlockSpec(memory_space=pltpu.VMEM)
HBM = pl.BlockSpec(memory_space=pltpu.HBM)


def partners(groups, chips, offset, shifts):
    route = []
    for group in range(groups):
        side = 1 if (group - offset) % 2 == 0 else -1
        other = (group + side) % groups
        for chip in range(chips):
            for core in range(CORES):
                target = (chip + side * shifts[core]) % chips
                route.append(
                    (
                        (group * chips + chip) * CORES + core,
                        (other * chips + target) * CORES + core,
                    )
                )
    return route


def along_x(groups, chips, shift):
    return [
        (
            (group * chips + chip) * CORES + core,
            (group * chips + (chip + shift) % chips) * CORES + (core + 1) % CORES,
        )
        for group in range(groups)
        for chip in range(chips)
        for core in range(CORES)
    ]


def other_core(groups, chips):
    return [
        (chip * CORES + core, chip * CORES + 1 - core)
        for chip in range(groups * chips)
        for core in range(CORES)
    ]


def call(body, shapes, *args, limit=16, stay=0, scratch=()):
    outs = [jax.ShapeDtypeStruct(shape, kind) for shape, kind in shapes]
    args = [
        pltpu.with_memory_space_constraint(arg, pltpu.HBM) if n < stay else arg
        for n, arg in enumerate(args)
    ]
    return pl.pallas_call(
        body,
        out_shape=outs,
        in_specs=[HBM] * stay + [VMEM] * (len(args) - stay),
        out_specs=[VMEM] * len(outs),
        scratch_shapes=list(scratch),
        compiler_params=pltpu.CompilerParams(vmem_limit_bytes=limit * 2**20),
    )(*args)


def fetch(sources, targets, sems):
    copies = [
        [
            pltpu.make_async_copy(source.at[e], target.at[e], sems.at[n, e])
            for e in range(source.shape[0])
        ]
        for n, (source, target) in enumerate(zip(sources, targets))
    ]
    for row in zip(*copies):
        for copy in row:
            copy.start()
    return copies


def contract(left, right, left_dim, right_dim):
    return lax.dot_general(
        left, right, (((left_dim,), (right_dim,)), ((), ())), preferred_element_type=F32
    )


def add_up(refs):
    value = refs[0][...]
    for ref in refs[1:]:
        value = value + ref[...]
    return value


def to_lanes(rows, elems, sides):
    return jnp.concatenate([rows[elems * k : elems * (k + 1)] for k in range(sides)], axis=1)


def to_rows(lanes, sides, width):
    return jnp.concatenate([lanes[:, width * k : width * (k + 1)] for k in range(sides)], axis=0)


def spread(spread_hits, values):
    high = values.astype(HALF)
    low = (values - high.astype(F32)).astype(HALF)
    return contract(spread_hits, high, 1, 0) + contract(spread_hits, low, 1, 0)


def hit_rows(ids, rows, group_faces, border, groups):
    group = lax.axis_index("elem")
    own = ids - group * group_faces
    low = ids - lax.rem(group + groups - 1, groups) * group_faces
    place = jnp.where((own >= 0) & (own < group_faces), own, low + group_faces)
    place = jnp.where(ids < 0, -1, place)
    elems, sides = ids.shape
    lane = lax.broadcasted_iota(jnp.int32, (elems, rows), 1)
    return jnp.concatenate(
        [(place[:, k : k + 1] == lane).astype(F32) for k in range(sides)], axis=0
    )


def masked(rows, element):
    index = lax.broadcasted_iota(jnp.int32, rows.shape, 0)
    return jnp.where(index == element, rows, 0.0).astype(HALF)


def load_kernel(dims, *refs):
    groups, elems, sides, width, group_faces, border = dims
    big, small, (local_ref, packet_ref, ids_ref, inverse, down) = refs[:2], refs[2:6], refs[6:11]
    residual, ids, residual_rows, stab_rows, big_sems, small_sems = refs[11:]
    rows = group_faces + border
    lines = 2 * elems
    smalls = [
        pltpu.make_async_copy(source, target, small_sems.at[n])
        for n, (source, target) in enumerate(zip(small, (residual, ids, residual_rows, stab_rows)))
    ]
    for copy in smalls:
        copy.start()
    inverse_copies, down_copies = fetch(big, (inverse, down), big_sems)
    for copy in smalls:
        copy.wait()
    ids_ref[...] = jnp.full((lines, sides), -1, jnp.int32)
    ids_ref[:elems] = ids[...]
    hits = hit_rows(ids_ref[...], rows, group_faces, border, groups)
    spread_hits = hits.T.astype(HALF)
    own_faces = residual_rows.shape[0]
    place = lax.axis_index("face") * own_faces
    blank = jnp.zeros((rows - own_faces, width), F32)
    right = pltpu.roll(jnp.concatenate([residual_rows[...], blank], axis=0), place, 0)
    scale = pltpu.roll(jnp.concatenate([stab_rows[...], blank], axis=0), place, 0)
    packet_ref[:lines, 2 * width :] = ids_ref[...].astype(F32)
    local_ref[...] = jnp.zeros(local_ref.shape, F32)
    source = jnp.concatenate([residual[...].astype(F32), jnp.zeros((elems, residual.shape[1]), F32)], axis=0)
    load = None
    for e in range(elems):
        inverse_copies[e].wait()
        local = contract(masked(source, e), inverse[e], 1, 1)
        local_ref[...] += local
        down_copies[e].wait()
        part = contract(local.astype(HALF), down[e], 1, 0)
        load = part if load is None else load + part
    sums = spread(spread_hits, to_rows(load, sides, width))
    packet_ref[:, : 2 * width] = jnp.concatenate([right - sums, scale], axis=1)


def join_kernel(border, width, packet, mate, sums_ref, first_ref, second_ref):
    sums = packet[:, : 2 * width] + mate[:, : 2 * width]
    sums_ref[...] = sums
    deal(sums, border, first_ref, second_ref)


def deal(sums, border, first_ref, second_ref):
    even = lax.rem(lax.axis_index("elem"), 2) == 0
    upper, lower = sums[:border], sums[sums.shape[0] - border :]
    first_ref[...] = jnp.where(even, upper, lower)
    second_ref[:border] = jnp.where(even, lower, upper)
    second_ref[border:] = first_ref[...]


def hits_kernel(dims, ids, mate, hits_ref, spread_ref):
    groups, elems, sides, width, group_faces, border = dims
    far = mate[:elems, 2 * width :].astype(jnp.int32)
    both = jnp.concatenate([ids[:elems], far], axis=0)
    hits = hit_rows(both, group_faces + border, group_faces, border, groups)
    hits_ref[...] = hits.astype(HALF)
    spread_ref[...] = hits.T.astype(HALF)


def whole(own, first, second, border):
    even = lax.rem(lax.axis_index("elem"), 2) == 0
    a, b = add_up(first), add_up(second)[:border]
    upper, lower = jnp.where(even, a, b), jnp.where(even, b, a)
    sums = add_up(own)
    last = sums.shape[0] - border
    return jnp.concatenate([sums[:border] + upper, sums[border:last], sums[last:] + lower], axis=0)


def image(trace_now, hits, spread_hits, schur_own, schur_mate, sides):
    elems = schur_own.shape[0]
    width = trace_now.shape[1]
    picked = contract(hits[...], trace_now.astype(HALF), 1, 0)
    lam = to_lanes(picked, 2 * elems, sides)
    terms = None
    for e in range(2 * elems):
        block = schur_own[e] if e < elems else schur_mate[e - elems]
        part = contract(masked(lam, e), block, 1, 0)
        terms = part if terms is None else terms + part
    return spread(spread_hits[...], to_rows(terms, sides, width))


def first_kernel(counts, border, sides, *refs):
    own, first, second, rest = split(counts, refs)
    hits, spread_hits, schur_own, schur_mate, right_ref, scale_ref, sums_ref, first_ref, second_ref = rest
    both = whole(own, first, second, border)
    width = both.shape[1] // 2
    right = both[:, :width]
    scale = 1.0 / both[:, width:]
    right_ref[...] = right
    scale_ref[...] = scale
    sums = image(right * scale, hits, spread_hits, schur_own, schur_mate, sides)
    sums_ref[...] = sums
    deal(sums, border, first_ref, second_ref)


def step_kernel(counts, border, sides, *refs):
    own, first, second, rest = split(counts, refs)
    right, scale, hits, spread_hits, schur_own, schur_mate, sums_ref, first_ref, second_ref = rest
    trace_now = (whole(own, first, second, border) + right[...]) * scale[...]
    sums = image(trace_now, hits, spread_hits, schur_own, schur_mate, sides)
    sums_ref[...] = sums
    deal(sums, border, first_ref, second_ref)


def last_kernel(counts, border, sides, *refs):
    own, first, second, rest = split(counts, refs)
    right, scale, hits, couple, local, trace_ref, vol_ref = rest
    trace_now = (whole(own, first, second, border) + right[...]) * scale[...]
    own_faces = trace_ref.shape[0]
    place = lax.axis_index("face") * own_faces
    rows = trace_now.shape[0]
    trace_ref[...] = pltpu.roll(trace_now, lax.rem(rows - place, rows), 0)[:own_faces]
    elems = couple.shape[0]
    picked = contract(hits[...], trace_now.astype(HALF), 1, 0)
    lam = to_lanes(picked, 2 * elems, sides)
    value = local[...]
    for e in range(elems):
        value = value - contract(masked(lam, e), couple[e], 1, 1)
    vol_ref[...] = value[:elems]


def split(counts, refs):
    a, b, c = counts
    return refs[:a], refs[a : a + b], refs[a + b : a + b + c], refs[a + b + c :]


def local(
    vol_inverse,
    vol_from_trace,
    trace_from_vol,
    vol_residual,
    face_ids,
    trace_residual,
    stabilization,
):
    groups = lax.axis_size("elem")
    members = lax.axis_size("face")
    chips = members // CORES
    elems, sides = face_ids.shape
    volume = vol_residual.shape[1]
    own_faces, width = trace_residual.shape
    group_faces = own_faces * members
    border = elems * members
    rows = group_faces + border
    slots = 2 * elems * sides
    trace = sides * width
    dims = (groups, elems, sides, width, group_faces, border)

    def swap_core(block):
        return lax.ppermute(block, AXES, other_core(groups, chips))

    def exchange(part, to_first, to_second):
        straight = [
            [shift + core for core in range(CORES)] for shift in range(0, chips, CORES)
        ]
        second = [lax.ppermute(to_second, AXES, partners(groups, chips, 1, s)) for s in straight]
        first = [lax.ppermute(to_first, AXES, partners(groups, chips, 0, s)) for s in straight]
        own = [part] + [
            lax.ppermute(part, AXES, along_x(groups, chips, shift)) for shift in range(1, chips)
        ]
        first = first + [swap_core(block) for block in first]
        second = second + [swap_core(block) for block in second]
        return own, first, second

    down = jnp.swapaxes(trace_from_vol, 1, 2)
    large = (vol_inverse, down)
    small = (vol_residual, face_ids, trace_residual, stabilization)
    local_part, packet, ids, inverse, down = call(
        functools.partial(load_kernel, dims),
        [
            ((2 * elems, volume), F32),
            ((rows, 2 * width + sides), F32),
            ((2 * elems, sides), jnp.int32),
            *((array.shape, array.dtype) for array in large),
        ],
        *large, *small,
        stay=6,
        scratch=[
            *(pltpu.VMEM(array.shape, array.dtype) for array in small),
            pltpu.SemaphoreType.DMA((len(large), elems)),
            pltpu.SemaphoreType.DMA((len(small),)),
        ],
    )
    mate = swap_core(packet)
    couple = jnp.einsum(
        "evk,ekt->evt", inverse, vol_from_trace, preferred_element_type=F32
    ).astype(HALF)
    schur_own = jnp.einsum("evs,evt->est", couple, down, preferred_element_type=F32).astype(HALF)
    mate, schur_own = lax.optimization_barrier((mate, schur_own))
    schur_mate = swap_core(schur_own)
    sums, to_first, to_second = call(
        functools.partial(join_kernel, border, width),
        [((rows, 2 * width), F32), ((border, 2 * width), F32), ((2 * border, 2 * width), F32)],
        packet, mate,
    )
    hits, spread_hits = call(
        functools.partial(hits_kernel, dims),
        [((slots, rows), HALF), ((rows, slots), HALF)],
        ids, mate,
    )

    def counted(kernel, parts):
        return functools.partial(kernel, tuple(len(part) for part in parts), border, sides)

    def flat(parts):
        return [ref for part in parts for ref in part]

    dealt = [((rows, width), F32), ((border, width), F32), ((2 * border, width), F32)]
    parts = exchange(sums, to_first, to_second)
    right, scale, *out = call(
        counted(first_kernel, parts),
        [((rows, width), F32)] * 2 + dealt,
        *flat(parts), hits, spread_hits, schur_own, schur_mate,
    )
    for _ in range(SWEEPS - 2):
        parts = exchange(*out)
        out = call(
            counted(step_kernel, parts), dealt,
            *flat(parts), right, scale, hits, spread_hits, schur_own, schur_mate,
        )
    parts = exchange(*out)
    trace_update, vol_update = call(
        counted(last_kernel, parts),
        [((own_faces, width), F32), ((elems, volume), F32)],
        *flat(parts), right, scale, hits, couple, local_part,
    )
    return trace_update, vol_update


def solution(mesh):
    in_specs = (
        P(AXES, None, None),
        P(AXES, None, None),
        P(AXES, None, None),
        P(AXES, None),
        P(AXES, None),
        P(AXES, None),
        P(AXES, None),
    )
    out_specs = (P(AXES, None), P(AXES, None))
    return jax.shard_map(local, mesh=mesh, in_specs=in_specs, out_specs=out_specs, check_vma=False)
```

time: 68.9 us -> 57.2 us (0.83)
  matrix products: 17.3 us -> 2.06 us
  Pallas kernels: 0 us -> 8.78 us
  starting transfers between devices: 30.6 us -> 22.5 us
  waiting for transfers between devices: 15.1 us -> 23 us
  local copies, waits for them, and re-layouts: 2.49 us -> 0.01 us
  other arithmetic: 2.14 us -> 0 us
    dot_general x23 -> x2, matrix products: 17.3 us -> 2.06 us  [the longest x1 1.22 us: local(): jnp.einsum('evs,evt->est', couple, down, preferred_element_type=F32)]
    pallas_call x0 -> x8, Pallas kernels: none -> 8.78 us  [call(): pl.pallas_call(body, out_shape=outs, in_specs=[HBM] * stay + [VMEM] * (le...]
    ppermute x15, waiting for transfers between devices: 11.1 us -> 18.3 us  [the longest x5 14.2 us: exchange(): lax.ppermute(to_second, AXES, partners(groups, chips, 1, s))]
    ppermute x15, starting transfers between devices: 26.8 us -> 20.6 us  [the longest x5 15.7 us: exchange(): lax.ppermute(to_second, AXES, partners(groups, chips, 1, s))]
    ppermute x12, starting transfers between devices: 3.85 us -> 1.85 us  [swap_core(): return lax.ppermute(block, AXES, other_core(groups, chips))]
    convert_element_type x2 -> x0, other arithmetic: 1.02 us -> none  [the longest x1 0.84 us: local(): own_rows.reshape(slots, 1).astype(jnp.float32)]
    slice x19 -> x0, local copies, waits for them, and re-layouts: 0.85 us -> none  [the longest x8 0.38 us: local(): lam[:elem_count]]
    ppermute x12, waiting for transfers between devices: 3.98 us -> 4.68 us  [swap_core(): return lax.ppermute(block, AXES, other_core(groups, chips))]
  transfers between devices with their start and end apart: 27 -> 27, of which waited for: 13 -> 15; matrix products, arithmetic and copies ran while one was open for 7% -> 4% of each run, Pallas kernels for 0% -> 0%
where the time goes in v2:
time: 57.2 us; the launch traced here: 57.1 us
  waiting for transfers between devices  23 us (40%)
  starting transfers between devices  22.5 us (39%)
  Pallas kernels  8.78 us (15%)
  matrix products  2.06 us (4%)
  between operations  0.74 us (1%)
    ppermute x5, starting transfers between devices, exchange(): lax.ppermute(to_second, AXES, partners(groups, chips, 1, s))  15.7 us
    ppermute x5, waiting for transfers between devices, exchange(): lax.ppermute(to_second, AXES, partners(groups, chips, 1, s))  14.2 us
    pallas_call x8, Pallas kernels, call(): pl.pallas_call(body, out_shape=outs, in_specs=[HBM] * stay + [VMEM] * (le...  8.78 us
    ppermute x5, starting transfers between devices, exchange(): lax.ppermute(part, AXES, along_x(groups, chips, shift))  4.89 us
    ppermute x12, waiting for transfers between devices, swap_core(): return lax.ppermute(block, AXES, other_core(groups, chips))  4.68 us
    ppermute x5, waiting for transfers between devices, exchange(): lax.ppermute(to_first, AXES, partners(groups, chips, 0, s))  4.06 us
    ppermute x12, starting transfers between devices, swap_core(): return lax.ppermute(block, AXES, other_core(groups, chips))  1.85 us
    dot_general x1, matrix products, local(): jnp.einsum('evs,evt->est', couple, down, preferred_element_type=F32)  1.22 us
  transfers between devices with their start and end apart: 27, of which 15 were waited for; matrix products, arithmetic and copies ran while one was open for 4% of the time, Pallas kernels for 0%

profile of v2, /device:TPU:0, one launch (start us, length us, event | category | flops | bytes accessed | tf_op | source)
XLA Modules:
  0.0 57.1 jit_solution(3324577934819009636)
XLA Ops:
  0.6 3.2 %shard_map.86 = (f32[8,320]{1,0:T(8,128)S(1)}, f32[64,166]{1,0:T(8,128)S(1)}, s32[8,6]{1,0:T(8,128)S(1)}, bf16[4,320,320]{2,1,0:T(8,128)(2,1)S(1)}, bf16[4,320,480]{2,1,0:T(8,128)(2,1)S(1)}) custom-call(bf16[4,320,320]{2,1,0:T(8,128)(2,1)} %refs_0_.1, bf16[4,320,480]{2,1,0:T(8,128)(2,1)} %bitcast.5, bf16[4,320]{1,0:T(4,128)(2,1)} %refs_2_.1, ...), custom_call_target="tpu_custom_call" | custom-call | tf_op jit(solution)/shard_map/pallas_call | solution.py:62
  5.2 1.2 %convolution_convert_fusion.refs_8_.refs_10_ = bf16[4,480,480]{2,1,0:T(8,128)(2,1)S(1)} fusion(bf16[4,320,480]{2,1,0:T(8,128)(2,1)S(1)} %convolution_convert_fusion.1.refs_9_, bf16[4,320,480]{2,1,0:T(8,128)(2,1)S(1)} %get-tuple-element.30), kind=kOutput, calls=%fused_computation | convolution fusion | flops 590745600 | bytes 4300800 | tf_op jit(solution)/shard_map/evs,evt->est/dot_general | solution.py:321
  6.6 6.1 %collective-permute-start.4 = (f32[32,160]{1,0:T(8,128)S(1)}, f32[32,160]{1,0:T(8,128)S(1)}, u32[]{:S(2)}, u32[]{:S(2)}) collective-permute-start(f32[32,160]{1,0:T(8,128)S(1)} %get-tuple-element.34), channel_id=1, source_target_pairs={{0,28},{1,31},{2,30},{3,29},{4,8},{5,11},{6,10},{7,9},{8,4},{9,7},... | collective-permute-start | bytes 61448 | tf_op jit(solution)/shard_map/ppermute | solution.py:289
  13.5 1.4 %collective-permute-done.4.refs_4_ = f32[32,160]{1,0:T(8,128)S(1)} collective-permute-done((f32[32,160]{1,0:T(8,128)S(1)}, f32[32,160]{1,0:T(8,128)S(1)}, u32[]{:S(2)}, u32[]{:S(2)}) %collective-permute-start.4) | collective-permute-done | bytes 20512 | tf_op jit(solution)/shard_map/ppermute | solution.py:289
  14.9 2.3 %collective-permute-done.2.refs_2_ = f32[16,160]{1,0:T(8,128)S(1)} collective-permute-done((f32[16,160]{1,0:T(8,128)S(1)}, f32[16,160]{1,0:T(8,128)S(1)}, u32[]{:S(2)}, u32[]{:S(2)}) %collective-permute-start.2) | collective-permute-done | bytes 10272 | tf_op jit(solution)/shard_map/ppermute | solution.py:290
  18.6 1.1 %shard_map.89 = (f32[64,80]{1,0:T(8,128)S(1)}, f32[64,80]{1,0:T(8,128)S(1)}, f32[64,80]{1,0:T(8,128)S(1)}, f32[16,80]{1,0:T(8,128)S(1)}, f32[32,80]{1,0:T(8,128)S(1)}) custom-call(f32[64,160]{1,0:T(8,128)S(1)} %get-tuple-element.32.refs_0_, f32[64,160]{1,0:T(8,128)S(1)} %collective-permute-done.1.refs_1_, f32[16,160]{1,0:T(8,128)S(1)} %collective-permute-done.2.refs_2_, ...), custom_call_target="tpu_custom_call" | custom-call | tf_op jit(solution)/shard_map/pallas_call | solution.py:62
  19.7 2.4 %collective-permute-start.10 = (f32[32,80]{1,0:T(8,128)S(1)}, f32[32,80]{1,0:T(8,128)S(1)}, u32[]{:S(2)}, u32[]{:S(2)}) collective-permute-start(f32[32,80]{1,0:T(8,128)S(1)} %get-tuple-element.41), channel_id=1, source_target_pairs={{0,28},{1,31},{2,30},{3,29},{4,8},{5,11},{6,10},{7,9},{8,4},{9,7},... | collective-permute-start | bytes 30728 | tf_op jit(solution)/shard_map/ppermute | solution.py:289
  22.1 1.1 %collective-permute-start.7 = (f32[64,80]{1,0:T(8,128)S(1)}, f32[64,80]{1,0:T(8,128)S(1)}, u32[]{:S(2)}, u32[]{:S(2)}) collective-permute-start(f32[64,80]{1,0:T(8,128)S(1)} %get-tuple-element.39.refs_0_), channel_id=1, source_target_pairs={{0,3},{1,2},{2,1},{3,0},{4,7},{5,6},{6,5},{7,4},{8,11},{9,10},{10,... | collective-permute-start | bytes 61448 | tf_op jit(solution)/shard_map/ppermute | solution.py:292
  23.3 3.0 %collective-permute-done.10.refs_4_ = f32[32,80]{1,0:T(8,128)S(1)} collective-permute-done((f32[32,80]{1,0:T(8,128)S(1)}, f32[32,80]{1,0:T(8,128)S(1)}, u32[]{:S(2)}, u32[]{:S(2)}) %collective-permute-start.10) | collective-permute-done | bytes 10272 | tf_op jit(solution)/shard_map/ppermute | solution.py:289
  27.0 1.1 %collective-permute-done.9.refs_3_ = f32[16,80]{1,0:T(8,128)S(1)} collective-permute-done((f32[16,80]{1,0:T(8,128)S(1)}, f32[16,80]{1,0:T(8,128)S(1)}, u32[]{:S(2)}, u32[]{:S(2)}) %collective-permute-start.9) | collective-permute-done | bytes 5152 | tf_op jit(solution)/shard_map/ppermute | solution.py:283
  28.1 1.0 %shard_map.90 = (f32[64,80]{1,0:T(8,128)S(1)}, f32[16,80]{1,0:T(8,128)S(1)}, f32[32,80]{1,0:T(8,128)S(1)}) custom-call(f32[64,80]{1,0:T(8,128)S(1)} %get-tuple-element.39.refs_0_, f32[64,80]{1,0:T(8,128)S(1)} %collective-permute-done.7.refs_1_, f32[16,80]{1,0:T(8,128)S(1)} %collective-permute-done.8.refs_2_, f32[16,80]{1,0:T(8,128)S(1)} %collective-permute-done.9.refs_3_, ...), custom_call_target="tpu_custom_call" | custom-call | tf_op jit(solution)/shard_map/pallas_call | solution.py:62
  29.1 2.4 %collective-permute-start.15 = (f32[32,80]{1,0:T(8,128)S(1)}, f32[32,80]{1,0:T(8,128)S(1)}, u32[]{:S(2)}, u32[]{:S(2)}) collective-permute-start(f32[32,80]{1,0:T(8,128)S(1)} %get-tuple-element.46), channel_id=1, source_target_pairs={{0,28},{1,31},{2,30},{3,29},{4,8},{5,11},{6,10},{7,9},{8,4},{9,7},... | collective-permute-start | bytes 30728 | tf_op jit(solution)/shard_map/ppermute | solution.py:289
  32.5 3.3 %collective-permute-done.15.refs_4_ = f32[32,80]{1,0:T(8,128)S(1)} collective-permute-done((f32[32,80]{1,0:T(8,128)S(1)}, f32[32,80]{1,0:T(8,128)S(1)}, u32[]{:S(2)}, u32[]{:S(2)}) %collective-permute-start.15) | collective-permute-done | bytes 10272 | tf_op jit(solution)/shard_map/ppermute | solution.py:289
  36.4 1.0 %collective-permute-done.14.refs_3_ = f32[16,80]{1,0:T(8,128)S(1)} collective-permute-done((f32[16,80]{1,0:T(8,128)S(1)}, f32[16,80]{1,0:T(8,128)S(1)}, u32[]{:S(2)}, u32[]{:S(2)}) %collective-permute-start.14) | collective-permute-done | bytes 5152 | tf_op jit(solution)/shard_map/ppermute | solution.py:283
  37.3 1.0 %shard_map.91 = (f32[64,80]{1,0:T(8,128)S(1)}, f32[16,80]{1,0:T(8,128)S(1)}, f32[32,80]{1,0:T(8,128)S(1)}) custom-call(f32[64,80]{1,0:T(8,128)S(1)} %get-tuple-element.44.refs_0_, f32[64,80]{1,0:T(8,128)S(1)} %collective-permute-done.12.refs_1_, f32[16,80]{1,0:T(8,128)S(1)} %collective-permute-done.13.refs_2_, f32[16,80]{1,0:T(8,128)S(1)} %collective-permute-done.14.refs_3_, ...), custom_call_target="tpu_custom_call" | custom-call | tf_op jit(solution)/shard_map/pallas_call | solution.py:62
  38.3 2.4 %collective-permute-start.20 = (f32[32,80]{1,0:T(8,128)S(1)}, f32[32,80]{1,0:T(8,128)S(1)}, u32[]{:S(2)}, u32[]{:S(2)}) collective-permute-start(f32[32,80]{1,0:T(8,128)S(1)} %get-tuple-element.49), channel_id=1, source_target_pairs={{0,28},{1,31},{2,30},{3,29},{4,8},{5,11},{6,10},{7,9},{8,4},{9,7},... | collective-permute-start | bytes 30728 | tf_op jit(solution)/shard_map/ppermute | solution.py:289
  40.8 1.0 %collective-permute-start.17 = (f32[64,80]{1,0:T(8,128)S(1)}, f32[64,80]{1,0:T(8,128)S(1)}, u32[]{:S(2)}, u32[]{:S(2)}) collective-permute-start(f32[64,80]{1,0:T(8,128)S(1)} %get-tuple-element.47.refs_0_), channel_id=1, source_target_pairs={{0,3},{1,2},{2,1},{3,0},{4,7},{5,6},{6,5},{7,4},{8,11},{9,10},{10,... | collective-permute-start | bytes 61448 | tf_op jit(solution)/shard_map/ppermute | solution.py:292
  41.8 3.1 %collective-permute-done.20.refs_4_ = f32[32,80]{1,0:T(8,128)S(1)} collective-permute-done((f32[32,80]{1,0:T(8,128)S(1)}, f32[32,80]{1,0:T(8,128)S(1)}, u32[]{:S(2)}, u32[]{:S(2)}) %collective-permute-start.20) | collective-permute-done | bytes 10272 | tf_op jit(solution)/shard_map/ppermute | solution.py:289
  45.6 1.0 %collective-permute-done.19.refs_3_ = f32[16,80]{1,0:T(8,128)S(1)} collective-permute-done((f32[16,80]{1,0:T(8,128)S(1)}, f32[16,80]{1,0:T(8,128)S(1)}, u32[]{:S(2)}, u32[]{:S(2)}) %collective-permute-start.19) | collective-permute-done | bytes 5152 | tf_op jit(solution)/shard_map/ppermute | solution.py:283
  46.6 1.0 %shard_map.92 = (f32[64,80]{1,0:T(8,128)S(1)}, f32[16,80]{1,0:T(8,128)S(1)}, f32[32,80]{1,0:T(8,128)S(1)}) custom-call(f32[64,80]{1,0:T(8,128)S(1)} %get-tuple-element.47.refs_0_, f32[64,80]{1,0:T(8,128)S(1)} %collective-permute-done.17.refs_1_, f32[16,80]{1,0:T(8,128)S(1)} %collective-permute-done.18.refs_2_, f32[16,80]{1,0:T(8,128)S(1)} %collective-permute-done.19.refs_3_, ...), custom_call_target="tpu_custom_call" | custom-call | tf_op jit(solution)/shard_map/pallas_call | solution.py:62
  47.6 2.4 %collective-permute-start.25 = (f32[32,80]{1,0:T(8,128)S(1)}, f32[32,80]{1,0:T(8,128)S(1)}, u32[]{:S(2)}, u32[]{:S(2)}) collective-permute-start(f32[32,80]{1,0:T(8,128)S(1)} %get-tuple-element.52), channel_id=1, source_target_pairs={{0,28},{1,31},{2,30},{3,29},{4,8},{5,11},{6,10},{7,9},{8,4},{9,7},... | collective-permute-start | bytes 30728 | tf_op jit(solution)/shard_map/ppermute | solution.py:289
  51.0 3.3 %collective-permute-done.25.refs_4_ = f32[32,80]{1,0:T(8,128)S(1)} collective-permute-done((f32[32,80]{1,0:T(8,128)S(1)}, f32[32,80]{1,0:T(8,128)S(1)}, u32[]{:S(2)}, u32[]{:S(2)}) %collective-permute-start.25) | collective-permute-done | bytes 10272 | tf_op jit(solution)/shard_map/ppermute | solution.py:289
  54.8 1.0 %collective-permute-done.24.refs_3_ = f32[16,80]{1,0:T(8,128)S(1)} collective-permute-done((f32[16,80]{1,0:T(8,128)S(1)}, f32[16,80]{1,0:T(8,128)S(1)}, u32[]{:S(2)}, u32[]{:S(2)}) %collective-permute-start.24) | collective-permute-done | bytes 5152 | tf_op jit(solution)/shard_map/ppermute | solution.py:283
  55.8 1.2 %shard_map.93 = (f32[12,80]{1,0:T(8,128)}, f32[4,320]{1,0:T(4,128)}) custom-call(f32[64,80]{1,0:T(8,128)S(1)} %get-tuple-element.50.refs_0_, f32[64,80]{1,0:T(8,128)S(1)} %collective-permute-done.22.refs_1_, f32[16,80]{1,0:T(8,128)S(1)} %collective-permute-done.23.refs_2_, f32[16,80]{1,0:T(8,128)S(1)} %collective-permute-done.24.refs_3_, ...), custom_call_target="tpu_custom_call" | custom-call | tf_op jit(solution)/shard_map/pallas_call | solution.py:62
  (42 shorter events, 8.1 us)
Async XLA Ops:
  3.9 2.6 %collective-permute-start = (f32[64,166]{1,0:T(8,128)S(1)}, f32[64,166]{1,0:T(8,128)S(1)}, u32[]{:S(2)}, u32[]{:S(2)}) collective-permute-start(f32[64,166]{1,0:T(8,128)S(1)} %get-tuple-element.28.packet), channel_id=1, source_target_pairs={{0,1},{1,0},{2,3},{3,2},{4,5},{5,4},{6,7},{7,6},{8,9},{9,8},{10,11... | collective-permute-start | bytes 127496 | tf_op jit(solution)/shard_map/ppermute | solution.py:283
  6.5 12.2 %collective-permute-start.6 = (bf16[4,480,480]{2,1,0:T(8,128)(2,1)S(1)}, bf16[4,480,480]{2,1,0:T(8,128)(2,1)S(1)}, u32[]{:S(2)}, u32[]{:S(2)}) collective-permute-start(bf16[4,480,480]{2,1,0:T(8,128)(2,1)S(1)} %convolution_convert_fusion.refs_8_.refs_10_), channel_id=1, source_target_pairs={{0,1},{1,0},{2,3},{3,2},{4,5},{5,4},{6,7},{7,6},{8,9},{9,8},{10,11... | collective-permute-start | bytes 5529608 | tf_op jit(solution)/shard_map/ppermute | solution.py:283
  6.6 8.3 %collective-permute-start.4 = (f32[32,160]{1,0:T(8,128)S(1)}, f32[32,160]{1,0:T(8,128)S(1)}, u32[]{:S(2)}, u32[]{:S(2)}) collective-permute-start(f32[32,160]{1,0:T(8,128)S(1)} %get-tuple-element.34), channel_id=1, source_target_pairs={{0,28},{1,31},{2,30},{3,29},{4,8},{5,11},{6,10},{7,9},{8,4},{9,7},... | collective-permute-start | bytes 61448 | tf_op jit(solution)/shard_map/ppermute | solution.py:289
  12.7 5.9 %collective-permute-start.1 = (f32[64,160]{1,0:T(8,128)S(1)}, f32[64,160]{1,0:T(8,128)S(1)}, u32[]{:S(2)}, u32[]{:S(2)}) collective-permute-start(f32[64,160]{1,0:T(8,128)S(1)} %get-tuple-element.32.refs_0_), channel_id=1, source_target_pairs={{0,3},{1,2},{2,1},{3,0},{4,7},{5,6},{6,5},{7,4},{8,11},{9,10},{10,... | collective-permute-start | bytes 122888 | tf_op jit(solution)/shard_map/ppermute | solution.py:292
  13.5 3.7 %collective-permute-start.2 = (f32[16,160]{1,0:T(8,128)S(1)}, f32[16,160]{1,0:T(8,128)S(1)}, u32[]{:S(2)}, u32[]{:S(2)}) collective-permute-start(f32[16,160]{1,0:T(8,128)S(1)} %get-tuple-element.33), channel_id=1, source_target_pairs={{0,4},{1,7},{2,6},{3,5},{4,0},{5,3},{6,2},{7,1},{8,12},{9,15},{10,... | collective-permute-start | bytes 30728 | tf_op jit(solution)/shard_map/ppermute | solution.py:290
  14.9 3.7 %collective-permute-start.5 = (f32[32,160]{1,0:T(8,128)S(1)}, f32[32,160]{1,0:T(8,128)S(1)}, u32[]{:S(2)}, u32[]{:S(2)}) collective-permute-start(f32[32,160]{1,0:T(8,128)S(1)} %collective-permute-done.4.refs_4_), channel_id=1, source_target_pairs={{0,1},{1,0},{2,3},{3,2},{4,5},{5,4},{6,7},{7,6},{8,9},{9,8},{10,11... | collective-permute-start | bytes 61448 | tf_op jit(solution)/shard_map/ppermute | solution.py:283
  17.2 1.4 %collective-permute-start.3 = (f32[16,160]{1,0:T(8,128)S(1)}, f32[16,160]{1,0:T(8,128)S(1)}, u32[]{:S(2)}, u32[]{:S(2)}) collective-permute-start(f32[16,160]{1,0:T(8,128)S(1)} %collective-permute-done.2.refs_2_), channel_id=1, source_target_pairs={{0,1},{1,0},{2,3},{3,2},{4,5},{5,4},{6,7},{7,6},{8,9},{9,8},{10,11... | collective-permute-start | bytes 30728 | tf_op jit(solution)/shard_map/ppermute | solution.py:283
  19.7 6.6 %collective-permute-start.10 = (f32[32,80]{1,0:T(8,128)S(1)}, f32[32,80]{1,0:T(8,128)S(1)}, u32[]{:S(2)}, u32[]{:S(2)}) collective-permute-start(f32[32,80]{1,0:T(8,128)S(1)} %get-tuple-element.41), channel_id=1, source_target_pairs={{0,28},{1,31},{2,30},{3,29},{4,8},{5,11},{6,10},{7,9},{8,4},{9,7},... | collective-permute-start | bytes 30728 | tf_op jit(solution)/shard_map/ppermute | solution.py:289
  22.1 6.0 %collective-permute-start.7 = (f32[64,80]{1,0:T(8,128)S(1)}, f32[64,80]{1,0:T(8,128)S(1)}, u32[]{:S(2)}, u32[]{:S(2)}) collective-permute-start(f32[64,80]{1,0:T(8,128)S(1)} %get-tuple-element.39.refs_0_), channel_id=1, source_target_pairs={{0,3},{1,2},{2,1},{3,0},{4,7},{5,6},{6,5},{7,4},{8,11},{9,10},{10,... | collective-permute-start | bytes 61448 | tf_op jit(solution)/shard_map/ppermute | solution.py:292
  23.3 3.7 %collective-permute-start.8 = (f32[16,80]{1,0:T(8,128)S(1)}, f32[16,80]{1,0:T(8,128)S(1)}, u32[]{:S(2)}, u32[]{:S(2)}) collective-permute-start(f32[16,80]{1,0:T(8,128)S(1)} %get-tuple-element.40), channel_id=1, source_target_pairs={{0,4},{1,7},{2,6},{3,5},{4,0},{5,3},{6,2},{7,1},{8,12},{9,15},{10,... | collective-permute-start | bytes 15368 | tf_op jit(solution)/shard_map/ppermute | solution.py:290
  26.3 1.8 %collective-permute-start.11 = (f32[32,80]{1,0:T(8,128)S(1)}, f32[32,80]{1,0:T(8,128)S(1)}, u32[]{:S(2)}, u32[]{:S(2)}) collective-permute-start(f32[32,80]{1,0:T(8,128)S(1)} %collective-permute-done.10.refs_4_), channel_id=1, source_target_pairs={{0,1},{1,0},{2,3},{3,2},{4,5},{5,4},{6,7},{7,6},{8,9},{9,8},{10,11... | collective-permute-start | bytes 30728 | tf_op jit(solution)/shard_map/ppermute | solution.py:283
  26.9 1.2 %collective-permute-start.9 = (f32[16,80]{1,0:T(8,128)S(1)}, f32[16,80]{1,0:T(8,128)S(1)}, u32[]{:S(2)}, u32[]{:S(2)}) collective-permute-start(f32[16,80]{1,0:T(8,128)S(1)} %collective-permute-done.8.refs_2_), channel_id=1, source_target_pairs={{0,1},{1,0},{2,3},{3,2},{4,5},{5,4},{6,7},{7,6},{8,9},{9,8},{10,11... | collective-permute-start | bytes 15368 | tf_op jit(solution)/shard_map/ppermute | solution.py:283
  29.1 6.7 %collective-permute-start.15 = (f32[32,80]{1,0:T(8,128)S(1)}, f32[32,80]{1,0:T(8,128)S(1)}, u32[]{:S(2)}, u32[]{:S(2)}) collective-permute-start(f32[32,80]{1,0:T(8,128)S(1)} %get-tuple-element.46), channel_id=1, source_target_pairs={{0,28},{1,31},{2,30},{3,29},{4,8},{5,11},{6,10},{7,9},{8,4},{9,7},... | collective-permute-start | bytes 30728 | tf_op jit(solution)/shard_map/ppermute | solution.py:289
  31.5 5.8 %collective-permute-start.12 = (f32[64,80]{1,0:T(8,128)S(1)}, f32[64,80]{1,0:T(8,128)S(1)}, u32[]{:S(2)}, u32[]{:S(2)}) collective-permute-start(f32[64,80]{1,0:T(8,128)S(1)} %get-tuple-element.44.refs_0_), channel_id=1, source_target_pairs={{0,3},{1,2},{2,1},{3,0},{4,7},{5,6},{6,5},{7,4},{8,11},{9,10},{10,... | collective-permute-start | bytes 61448 | tf_op jit(solution)/shard_map/ppermute | solution.py:292
  32.5 3.7 %collective-permute-start.13 = (f32[16,80]{1,0:T(8,128)S(1)}, f32[16,80]{1,0:T(8,128)S(1)}, u32[]{:S(2)}, u32[]{:S(2)}) collective-permute-start(f32[16,80]{1,0:T(8,128)S(1)} %get-tuple-element.45), channel_id=1, source_target_pairs={{0,4},{1,7},{2,6},{3,5},{4,0},{5,3},{6,2},{7,1},{8,12},{9,15},{10,... | collective-permute-start | bytes 15368 | tf_op jit(solution)/shard_map/ppermute | solution.py:290
  35.8 1.5 %collective-permute-start.16 = (f32[32,80]{1,0:T(8,128)S(1)}, f32[32,80]{1,0:T(8,128)S(1)}, u32[]{:S(2)}, u32[]{:S(2)}) collective-permute-start(f32[32,80]{1,0:T(8,128)S(1)} %collective-permute-done.15.refs_4_), channel_id=1, source_target_pairs={{0,1},{1,0},{2,3},{3,2},{4,5},{5,4},{6,7},{7,6},{8,9},{9,8},{10,11... | collective-permute-start | bytes 30728 | tf_op jit(solution)/shard_map/ppermute | solution.py:283
  38.3 6.6 %collective-permute-start.20 = (f32[32,80]{1,0:T(8,128)S(1)}, f32[32,80]{1,0:T(8,128)S(1)}, u32[]{:S(2)}, u32[]{:S(2)}) collective-permute-start(f32[32,80]{1,0:T(8,128)S(1)} %get-tuple-element.49), channel_id=1, source_target_pairs={{0,28},{1,31},{2,30},{3,29},{4,8},{5,11},{6,10},{7,9},{8,4},{9,7},... | collective-permute-start | bytes 30728 | tf_op jit(solution)/shard_map/ppermute | solution.py:289
  40.8 5.9 %collective-permute-start.17 = (f32[64,80]{1,0:T(8,128)S(1)}, f32[64,80]{1,0:T(8,128)S(1)}, u32[]{:S(2)}, u32[]{:S(2)}) collective-permute-start(f32[64,80]{1,0:T(8,128)S(1)} %get-tuple-element.47.refs_0_), channel_id=1, source_target_pairs={{0,3},{1,2},{2,1},{3,0},{4,7},{5,6},{6,5},{7,4},{8,11},{9,10},{10,... | collective-permute-start | bytes 61448 | tf_op jit(solution)/shard_map/ppermute | solution.py:292
  41.8 3.7 %collective-permute-start.18 = (f32[16,80]{1,0:T(8,128)S(1)}, f32[16,80]{1,0:T(8,128)S(1)}, u32[]{:S(2)}, u32[]{:S(2)}) collective-permute-start(f32[16,80]{1,0:T(8,128)S(1)} %get-tuple-element.48), channel_id=1, source_target_pairs={{0,4},{1,7},{2,6},{3,5},{4,0},{5,3},{6,2},{7,1},{8,12},{9,15},{10,... | collective-permute-start | bytes 15368 | tf_op jit(solution)/shard_map/ppermute | solution.py:290
  44.9 1.7 %collective-permute-start.21 = (f32[32,80]{1,0:T(8,128)S(1)}, f32[32,80]{1,0:T(8,128)S(1)}, u32[]{:S(2)}, u32[]{:S(2)}) collective-permute-start(f32[32,80]{1,0:T(8,128)S(1)} %collective-permute-done.20.refs_4_), channel_id=1, source_target_pairs={{0,1},{1,0},{2,3},{3,2},{4,5},{5,4},{6,7},{7,6},{8,9},{9,8},{10,11... | collective-permute-start | bytes 30728 | tf_op jit(solution)/shard_map/ppermute | solution.py:283
  47.6 6.7 %collective-permute-start.25 = (f32[32,80]{1,0:T(8,128)S(1)}, f32[32,80]{1,0:T(8,128)S(1)}, u32[]{:S(2)}, u32[]{:S(2)}) collective-permute-start(f32[32,80]{1,0:T(8,128)S(1)} %get-tuple-element.52), channel_id=1, source_target_pairs={{0,28},{1,31},{2,30},{3,29},{4,8},{5,11},{6,10},{7,9},{8,4},{9,7},... | collective-permute-start | bytes 30728 | tf_op jit(solution)/shard_map/ppermute | solution.py:289
  50.0 5.8 %collective-permute-start.22 = (f32[64,80]{1,0:T(8,128)S(1)}, f32[64,80]{1,0:T(8,128)S(1)}, u32[]{:S(2)}, u32[]{:S(2)}) collective-permute-start(f32[64,80]{1,0:T(8,128)S(1)} %get-tuple-element.50.refs_0_), channel_id=1, source_target_pairs={{0,3},{1,2},{2,1},{3,0},{4,7},{5,6},{6,5},{7,4},{8,11},{9,10},{10,... | collective-permute-start | bytes 61448 | tf_op jit(solution)/shard_map/ppermute | solution.py:292
  51.0 3.7 %collective-permute-start.23 = (f32[16,80]{1,0:T(8,128)S(1)}, f32[16,80]{1,0:T(8,128)S(1)}, u32[]{:S(2)}, u32[]{:S(2)}) collective-permute-start(f32[16,80]{1,0:T(8,128)S(1)} %get-tuple-element.51), channel_id=1, source_target_pairs={{0,4},{1,7},{2,6},{3,5},{4,0},{5,3},{6,2},{7,1},{8,12},{9,15},{10,... | collective-permute-start | bytes 15368 | tf_op jit(solution)/shard_map/ppermute | solution.py:290
  54.3 1.5 %collective-permute-start.26 = (f32[32,80]{1,0:T(8,128)S(1)}, f32[32,80]{1,0:T(8,128)S(1)}, u32[]{:S(2)}, u32[]{:S(2)}) collective-permute-start(f32[32,80]{1,0:T(8,128)S(1)} %collective-permute-done.25.refs_4_), channel_id=1, source_target_pairs={{0,1},{1,0},{2,3},{3,2},{4,5},{5,4},{6,7},{7,6},{8,9},{9,8},{10,11... | collective-permute-start | bytes 30728 | tf_op jit(solution)/shard_map/ppermute | solution.py:283
  (4 other events, 7.3 us)

commit v3 on v2

--- a/solution.py
+++ b/solution.py
@@ -69,20 +69,6 @@
     )(*args)
 
 
-def fetch(sources, targets, sems):
-    copies = [
-        [
-            pltpu.make_async_copy(source.at[e], target.at[e], sems.at[n, e])
-            for e in range(source.shape[0])
-        ]
-        for n, (source, target) in enumerate(zip(sources, targets))
-    ]
-    for row in zip(*copies):
-        for copy in row:
-            copy.start()
-    return copies
-
-
 def contract(left, right, left_dim, right_dim):
     return lax.dot_general(
         left, right, (((left_dim,), (right_dim,)), ((), ())), preferred_element_type=F32
@@ -90,9 +76,9 @@
 
 
 def add_up(refs):
-    value = refs[0][...]
+    value = refs[0][...].astype(F32)
     for ref in refs[1:]:
-        value = value + ref[...]
+        value = value + ref[...].astype(F32)
     return value
 
 
@@ -130,40 +116,50 @@
 
 def load_kernel(dims, *refs):
     groups, elems, sides, width, group_faces, border = dims
-    big, small, (local_ref, packet_ref, ids_ref, inverse, down) = refs[:2], refs[2:6], refs[6:11]
-    residual, ids, residual_rows, stab_rows, big_sems, small_sems = refs[11:]
+    sources, (local_ref, packet_ref, ids_ref, inverse, down) = refs[:6], refs[6:11]
+    residual, ids, residual_rows, stab_rows, sems = refs[11:]
     rows = group_faces + border
     lines = 2 * elems
-    smalls = [
-        pltpu.make_async_copy(source, target, small_sems.at[n])
-        for n, (source, target) in enumerate(zip(small, (residual, ids, residual_rows, stab_rows)))
-    ]
-    for copy in smalls:
+
+    def fetch(index, target, at, count, sem):
+        piece = pl.ds(at, count)
+        copy = pltpu.make_async_copy(sources[index].at[piece], target.at[piece], sems.at[sem])
         copy.start()
-    inverse_copies, down_copies = fetch(big, (inverse, down), big_sems)
-    for copy in smalls:
+        return copy
+
+    inverse_hbm, down_hbm, residual_hbm, ids_hbm, residual_rows_hbm, stab_rows_hbm = range(6)
+    own_faces = residual_rows.shape[0]
+    first = [fetch(residual_hbm, residual, 0, elems, 0), fetch(inverse_hbm, inverse, 0, elems, 1)]
+    half = elems // 1
+    pieces = [fetch(down_hbm, down, half * n, half, 2 + n) for n in range(1)]
+    small = [
+        fetch(ids_hbm, ids, 0, elems, 2 + 1),
+        fetch(residual_rows_hbm, residual_rows, 0, own_faces, 3 + 1),
+        fetch(stab_rows_hbm, stab_rows, 0, own_faces, 4 + 1),
+    ]
+    for copy in first:
+        copy.wait()
+    source = residual[...].astype(F32)
+    source = jnp.concatenate([source, jnp.zeros_like(source)], axis=0)
+    local = add_up([contract(masked(source, e), inverse[e], 1, 1) for e in range(elems)])
+    local_ref[...] = local
+    for copy in small:
         copy.wait()
     ids_ref[...] = jnp.full((lines, sides), -1, jnp.int32)
     ids_ref[:elems] = ids[...]
     hits = hit_rows(ids_ref[...], rows, group_faces, border, groups)
     spread_hits = hits.T.astype(HALF)
-    own_faces = residual_rows.shape[0]
     place = lax.axis_index("face") * own_faces
     blank = jnp.zeros((rows - own_faces, width), F32)
     right = pltpu.roll(jnp.concatenate([residual_rows[...], blank], axis=0), place, 0)
     scale = pltpu.roll(jnp.concatenate([stab_rows[...], blank], axis=0), place, 0)
     packet_ref[:lines, 2 * width :] = ids_ref[...].astype(F32)
-    local_ref[...] = jnp.zeros(local_ref.shape, F32)
-    source = jnp.concatenate([residual[...].astype(F32), jnp.zeros((elems, residual.shape[1]), F32)], axis=0)
-    load = None
-    for e in range(elems):
-        inverse_copies[e].wait()
-        local = contract(masked(source, e), inverse[e], 1, 1)
-        local_ref[...] += local
-        down_copies[e].wait()
-        part = contract(local.astype(HALF), down[e], 1, 0)
-        load = part if load is None else load + part
-    sums = spread(spread_hits, to_rows(load, sides, width))
+    load = []
+    for n in range(1):
+        pieces[n].wait()
+        for e in range(half * n, half * (n + 1)):
+            load.append(contract(masked(local, e), down[e], 1, 0))
+    sums = spread(spread_hits, to_rows(add_up(load), sides, width))
     packet_ref[:, : 2 * width] = jnp.concatenate([right - sums, scale], axis=1)
 
 
@@ -176,9 +172,10 @@
 def deal(sums, border, first_ref, second_ref):
     even = lax.rem(lax.axis_index("elem"), 2) == 0
     upper, lower = sums[:border], sums[sums.shape[0] - border :]
-    first_ref[...] = jnp.where(even, upper, lower)
-    second_ref[:border] = jnp.where(even, lower, upper)
-    second_ref[border:] = first_ref[...]
+    kind = first_ref.dtype
+    first_ref[...] = jnp.where(even, upper, lower).astype(kind)
+    second_ref[:border] = jnp.where(even, lower, upper).astype(kind)
+    second_ref[border:] = first_ref[: second_ref.shape[0] - border]
 
 
 def hits_kernel(dims, ids, mate, hits_ref, spread_ref):
@@ -190,9 +187,14 @@
     spread_ref[...] = hits.T.astype(HALF)
 
 
-def whole(own, first, second, border):
+def whole(parts, border):
+    own, first, second, (mate,) = parts
     even = lax.rem(lax.axis_index("elem"), 2) == 0
+    blocks = mate[...].astype(F32)
     a, b = add_up(first), add_up(second)[:border]
+    for n in range(len(first)):
+        a = a + blocks[n * border : (n + 1) * border]
+        b = b + blocks[(len(first) + n) * border : (len(first) + n + 1) * border]
     upper, lower = jnp.where(even, a, b), jnp.where(even, b, a)
     sums = add_up(own)
     last = sums.shape[0] - border
@@ -213,9 +215,9 @@
 
 
 def first_kernel(counts, border, sides, *refs):
-    own, first, second, rest = split(counts, refs)
-    hits, spread_hits, schur_own, schur_mate, right_ref, scale_ref, sums_ref, first_ref, second_ref = rest
-    both = whole(own, first, second, border)
+    parts, rest = split(counts, refs)
+    hits, spread_hits, schur_own, schur_mate, right_ref, scale_ref, sums_ref, sent_ref, first_ref, second_ref = rest
+    both = whole(parts, border)
     width = both.shape[1] // 2
     right = both[:, :width]
     scale = 1.0 / both[:, width:]
@@ -223,22 +225,24 @@
     scale_ref[...] = scale
     sums = image(right * scale, hits, spread_hits, schur_own, schur_mate, sides)
     sums_ref[...] = sums
+    sent_ref[...] = sums.astype(HALF)
     deal(sums, border, first_ref, second_ref)
 
 
 def step_kernel(counts, border, sides, *refs):
-    own, first, second, rest = split(counts, refs)
-    right, scale, hits, spread_hits, schur_own, schur_mate, sums_ref, first_ref, second_ref = rest
-    trace_now = (whole(own, first, second, border) + right[...]) * scale[...]
+    parts, rest = split(counts, refs)
+    right, scale, hits, spread_hits, schur_own, schur_mate, sums_ref, sent_ref, first_ref, second_ref = rest
+    trace_now = (whole(parts, border) + right[...]) * scale[...]
     sums = image(trace_now, hits, spread_hits, schur_own, schur_mate, sides)
     sums_ref[...] = sums
+    sent_ref[...] = sums.astype(HALF)
     deal(sums, border, first_ref, second_ref)
 
 
 def last_kernel(counts, border, sides, *refs):
-    own, first, second, rest = split(counts, refs)
+    parts, rest = split(counts, refs)
     right, scale, hits, couple, local, trace_ref, vol_ref = rest
-    trace_now = (whole(own, first, second, border) + right[...]) * scale[...]
+    trace_now = (whole(parts, border) + right[...]) * scale[...]
     own_faces = trace_ref.shape[0]
     place = lax.axis_index("face") * own_faces
     rows = trace_now.shape[0]
@@ -253,8 +257,11 @@
 
 
 def split(counts, refs):
-    a, b, c = counts
-    return refs[:a], refs[a : a + b], refs[a + b : a + b + c], refs[a + b + c :]
+    parts = []
+    for count in counts:
+        parts.append(refs[:count])
+        refs = refs[count:]
+    return parts, refs
 
 
 def local(
@@ -282,18 +289,17 @@
     def swap_core(block):
         return lax.ppermute(block, AXES, other_core(groups, chips))
 
-    def exchange(part, to_first, to_second):
+    def exchange(part, sent, to_first, to_second):
         straight = [
             [shift + core for core in range(CORES)] for shift in range(0, chips, CORES)
         ]
         second = [lax.ppermute(to_second, AXES, partners(groups, chips, 1, s)) for s in straight]
         first = [lax.ppermute(to_first, AXES, partners(groups, chips, 0, s)) for s in straight]
         own = [part] + [
-            lax.ppermute(part, AXES, along_x(groups, chips, shift)) for shift in range(1, chips)
+            lax.ppermute(sent, AXES, along_x(groups, chips, shift)) for shift in range(1, chips)
         ]
-        first = first + [swap_core(block) for block in first]
-        second = second + [swap_core(block) for block in second]
-        return own, first, second
+        mate = swap_core(jnp.concatenate([*first, *(block[:border] for block in second)]))
+        return own, first, second, [mate]
 
     down = jnp.swapaxes(trace_from_vol, 1, 2)
     large = (vol_inverse, down)
@@ -310,8 +316,7 @@
         stay=6,
         scratch=[
             *(pltpu.VMEM(array.shape, array.dtype) for array in small),
-            pltpu.SemaphoreType.DMA((len(large), elems)),
-            pltpu.SemaphoreType.DMA((len(small),)),
+            pltpu.SemaphoreType.DMA((6,)),
         ],
     )
     mate = swap_core(packet)
@@ -323,7 +328,7 @@
     schur_mate = swap_core(schur_own)
     sums, to_first, to_second = call(
         functools.partial(join_kernel, border, width),
-        [((rows, 2 * width), F32), ((border, 2 * width), F32), ((2 * border, 2 * width), F32)],
+        [((rows, 2 * width), F32), ((border, 2 * width), F32), ((border + 8, 2 * width), F32)],
         packet, mate,
     )
     hits, spread_hits = call(
@@ -338,8 +343,13 @@
     def flat(parts):
         return [ref for part in parts for ref in part]
 
-    dealt = [((rows, width), F32), ((border, width), F32), ((2 * border, width), F32)]
-    parts = exchange(sums, to_first, to_second)
+    dealt = [
+        ((rows, width), F32),
+        ((rows, width), HALF),
+        ((border, width), HALF),
+        ((2 * border, width), HALF),
+    ]
+    parts = exchange(sums, sums, to_first, to_second)
     right, scale, *out = call(
         counted(first_kernel, parts),
         [((rows, width), F32)] * 2 + dealt,

time: 57.2 us -> 53.9 us (0.942)
  waiting for transfers between devices: 23 us -> 17.9 us
  starting transfers between devices: 22.5 us -> 24.7 us
    ppermute x5, waiting for transfers between devices: 14.2 us -> 11.6 us  [exchange(): lax.ppermute(to_second, AXES, partners(groups, chips, 1, s))]
    ppermute x5, starting transfers between devices: 15.7 us -> 17.7 us  [exchange(): lax.ppermute(to_second, AXES, partners(groups, chips, 1, s))]
    ppermute x5, waiting for transfers between devices: 4.06 us -> 2.13 us  [exchange(): lax.ppermute(to_first, AXES, partners(groups, chips, 0, s))]
    ppermute x12 -> x7, starting transfers between devices: 1.85 us -> 2.35 us  [swap_core(): return lax.ppermute(block, AXES, other_core(groups, chips))]
    ppermute x12 -> x7, waiting for transfers between devices: 4.68 us -> 4.23 us  [swap_core(): return lax.ppermute(block, AXES, other_core(groups, chips))]
  transfers between devices with their start and end apart: 27 -> 22, of which waited for: 15 -> 13; matrix products, arithmetic and copies ran while one was open for 4% -> 4% of each run, Pallas kernels for 0% -> 0%
where the time goes in v3:
time: 53.9 us; the launch traced here: 53.8 us
  starting transfers between devices  24.7 us (46%)
  waiting for transfers between devices  17.9 us (33%)
  Pallas kernels  8.32 us (15%)
  matrix products  2.07 us (4%)
  between operations  0.74 us (1%)
    ppermute x5, starting transfers between devices, exchange(): lax.ppermute(to_second, AXES, partners(groups, chips, 1, s))  17.7 us
    ppermute x5, waiting for transfers between devices, exchange(): lax.ppermute(to_second, AXES, partners(groups, chips, 1, s))  11.6 us
    pallas_call x8, Pallas kernels, call(): pl.pallas_call(body, out_shape=outs, in_specs=[HBM] * stay + [VMEM] * (le...  8.32 us
    ppermute x5, starting transfers between devices, exchange(): lax.ppermute(sent, AXES, along_x(groups, chips, shift))  4.62 us
    ppermute x7, waiting for transfers between devices, swap_core(): return lax.ppermute(block, AXES, other_core(groups, chips))  4.23 us
    ppermute x7, starting transfers between devices, swap_core(): return lax.ppermute(block, AXES, other_core(groups, chips))  2.35 us
    ppermute x5, waiting for transfers between devices, exchange(): lax.ppermute(to_first, AXES, partners(groups, chips, 0, s))  2.13 us
    dot_general x1, matrix products, local(): jnp.einsum('evs,evt->est', couple, down, preferred_element_type=F32)  1.22 us
  transfers between devices with their start and end apart: 22, of which 13 were waited for; matrix products, arithmetic and copies ran while one was open for 4% of the time, Pallas kernels for 0%

profile of v3, /device:TPU:0, one launch (start us, length us, event | category | flops | bytes accessed | tf_op | source)
XLA Modules:
  0.0 53.8 jit_solution(7273607359318637672)
XLA Ops:
  0.6 2.7 %shard_map.86 = (f32[8,320]{1,0:T(8,128)S(1)}, f32[64,166]{1,0:T(8,128)S(1)}, s32[8,6]{1,0:T(8,128)S(1)}, bf16[4,320,320]{2,1,0:T(8,128)(2,1)S(1)}, bf16[4,320,480]{2,1,0:T(8,128)(2,1)S(1)}) custom-call(bf16[4,320,320]{2,1,0:T(8,128)(2,1)} %refs_0_.1, bf16[4,320,480]{2,1,0:T(8,128)(2,1)} %bitcast.5, bf16[4,320]{1,0:T(4,128)(2,1)} %refs_2_.1, ...), custom_call_target="tpu_custom_call" | custom-call | tf_op jit(solution)/shard_map/pallas_call | solution.py:62
  4.8 1.2 %convolution_convert_fusion.refs_7_.refs_9_ = bf16[4,480,480]{2,1,0:T(8,128)(2,1)S(1)} fusion(bf16[4,320,480]{2,1,0:T(8,128)(2,1)S(1)} %convolution_convert_fusion.1.refs_8_, bf16[4,320,480]{2,1,0:T(8,128)(2,1)S(1)} %get-tuple-element.34), kind=kOutput, calls=%fused_computation | convolution fusion | flops 590745600 | bytes 4300800 | tf_op jit(solution)/shard_map/evs,evt->est/dot_general | solution.py:326
  6.2 6.1 %collective-permute-start.3 = (f32[24,160]{1,0:T(8,128)S(1)}, f32[24,160]{1,0:T(8,128)S(1)}, u32[]{:S(2)}, u32[]{:S(2)}) collective-permute-start(f32[24,160]{1,0:T(8,128)S(1)} %get-tuple-element.38), channel_id=1, source_target_pairs={{0,28},{1,31},{2,30},{3,29},{4,8},{5,11},{6,10},{7,9},{8,4},{9,7},... | collective-permute-start | bytes 46088 | tf_op jit(solution)/shard_map/ppermute | solution.py:296
  13.0 1.2 %collective-permute-done.3.refs_3_ = f32[24,160]{1,0:T(8,128)S(1)} collective-permute-done((f32[24,160]{1,0:T(8,128)S(1)}, f32[24,160]{1,0:T(8,128)S(1)}, u32[]{:S(2)}, u32[]{:S(2)}) %collective-permute-start.3) | collective-permute-done | bytes 15392 | tf_op jit(solution)/shard_map/ppermute | solution.py:296
  14.2 1.8 %collective-permute-done.2.refs_2_ = f32[16,160]{1,0:T(8,128)S(1)} collective-permute-done((f32[16,160]{1,0:T(8,128)S(1)}, f32[16,160]{1,0:T(8,128)S(1)}, u32[]{:S(2)}, u32[]{:S(2)}) %collective-permute-start.2) | collective-permute-done | bytes 10272 | tf_op jit(solution)/shard_map/ppermute | solution.py:297
  17.3 1.1 %shard_map.89 = (f32[64,80]{1,0:T(8,128)S(1)}, f32[64,80]{1,0:T(8,128)S(1)}, f32[64,80]{1,0:T(8,128)S(1)}, bf16[64,80]{1,0:T(8,128)(2,1)S(1)}, bf16[16,80]{1,0:T(8,128)(2,1)S(1)}, /*index=5*/bf16[32,80]{1,0:T(8,128)(2,1)S(1)}) custom-call(f32[64,160]{1,0:T(8,128)S(1)} %get-tuple-element.36.refs_0_, f32[64,160]{1,0:T(8,128)S(1)} %collective-permute-done.1.refs_1_, ...), custom_call_target="tpu_custom_call" | custom-call | tf_op jit(solution)/shard_map/pallas_call | solution.py:62
  18.3 3.1 %collective-permute-start.8 = (bf16[32,80]{1,0:T(8,128)(2,1)S(1)}, bf16[32,80]{1,0:T(8,128)(2,1)S(1)}, u32[]{:S(2)}, u32[]{:S(2)}) collective-permute-start(bf16[32,80]{1,0:T(8,128)(2,1)S(1)} %get-tuple-element.46), channel_id=1, source_target_pairs={{0,28},{1,31},{2,30},{3,29},{4,8},{5,11},{6,10},{7,9},{8,4},{9,7},... | collective-permute-start | bytes 15368 | tf_op jit(solution)/shard_map/ppermute | solution.py:296
  21.4 0.9 %collective-permute-start.6 = (bf16[64,80]{1,0:T(8,128)(2,1)S(1)}, bf16[64,80]{1,0:T(8,128)(2,1)S(1)}, u32[]{:S(2)}, u32[]{:S(2)}) collective-permute-start(bf16[64,80]{1,0:T(8,128)(2,1)S(1)} %get-tuple-element.44), channel_id=1, source_target_pairs={{0,3},{1,2},{2,1},{3,0},{4,7},{5,6},{6,5},{7,4},{8,11},{9,10},{10,... | collective-permute-start | bytes 30728 | tf_op jit(solution)/shard_map/ppermute | solution.py:299
  22.4 2.4 %collective-permute-done.8.refs_3_ = bf16[32,80]{1,0:T(8,128)(2,1)S(1)} collective-permute-done((bf16[32,80]{1,0:T(8,128)(2,1)S(1)}, bf16[32,80]{1,0:T(8,128)(2,1)S(1)}, u32[]{:S(2)}, u32[]{:S(2)}) %collective-permute-start.8) | collective-permute-done | bytes 5152 | tf_op jit(solution)/shard_map/ppermute | solution.py:296
  26.3 1.0 %shard_map.90 = (f32[64,80]{1,0:T(8,128)S(1)}, bf16[64,80]{1,0:T(8,128)(2,1)S(1)}, bf16[16,80]{1,0:T(8,128)(2,1)S(1)}, bf16[32,80]{1,0:T(8,128)(2,1)S(1)}) custom-call(f32[64,80]{1,0:T(8,128)S(1)} %get-tuple-element.43.refs_0_, bf16[64,80]{1,0:T(8,128)(2,1)S(1)} %collective-permute-done.6.refs_1_, bf16[16,80]{1,0:T(8,128)(2,1)S(1)} %collective-permute-done.7.refs_2_, ...), custom_call_target="tpu_custom_call" | custom-call | tf_op jit(solution)/shard_map/pallas_call | solution.py:62
  27.3 2.9 %collective-permute-start.12 = (bf16[32,80]{1,0:T(8,128)(2,1)S(1)}, bf16[32,80]{1,0:T(8,128)(2,1)S(1)}, u32[]{:S(2)}, u32[]{:S(2)}) collective-permute-start(bf16[32,80]{1,0:T(8,128)(2,1)S(1)} %get-tuple-element.52), channel_id=1, source_target_pairs={{0,28},{1,31},{2,30},{3,29},{4,8},{5,11},{6,10},{7,9},{8,4},{9,7},... | collective-permute-start | bytes 15368 | tf_op jit(solution)/shard_map/ppermute | solution.py:296
  30.2 1.0 %collective-permute-start.10 = (bf16[64,80]{1,0:T(8,128)(2,1)S(1)}, bf16[64,80]{1,0:T(8,128)(2,1)S(1)}, u32[]{:S(2)}, u32[]{:S(2)}) collective-permute-start(bf16[64,80]{1,0:T(8,128)(2,1)S(1)} %get-tuple-element.50), channel_id=1, source_target_pairs={{0,3},{1,2},{2,1},{3,0},{4,7},{5,6},{6,5},{7,4},{8,11},{9,10},{10,... | collective-permute-start | bytes 30728 | tf_op jit(solution)/shard_map/ppermute | solution.py:299
  31.2 2.6 %collective-permute-done.12.refs_3_ = bf16[32,80]{1,0:T(8,128)(2,1)S(1)} collective-permute-done((bf16[32,80]{1,0:T(8,128)(2,1)S(1)}, bf16[32,80]{1,0:T(8,128)(2,1)S(1)}, u32[]{:S(2)}, u32[]{:S(2)}) %collective-permute-start.12) | collective-permute-done | bytes 5152 | tf_op jit(solution)/shard_map/ppermute | solution.py:296
  35.0 1.0 %shard_map.91 = (f32[64,80]{1,0:T(8,128)S(1)}, bf16[64,80]{1,0:T(8,128)(2,1)S(1)}, bf16[16,80]{1,0:T(8,128)(2,1)S(1)}, bf16[32,80]{1,0:T(8,128)(2,1)S(1)}) custom-call(f32[64,80]{1,0:T(8,128)S(1)} %get-tuple-element.49.refs_0_, bf16[64,80]{1,0:T(8,128)(2,1)S(1)} %collective-permute-done.10.refs_1_, bf16[16,80]{1,0:T(8,128)(2,1)S(1)} %collective-permute-done.11.refs_2_, ...), custom_call_target="tpu_custom_call" | custom-call | tf_op jit(solution)/shard_map/pallas_call | solution.py:62
  36.0 2.9 %collective-permute-start.16 = (bf16[32,80]{1,0:T(8,128)(2,1)S(1)}, bf16[32,80]{1,0:T(8,128)(2,1)S(1)}, u32[]{:S(2)}, u32[]{:S(2)}) collective-permute-start(bf16[32,80]{1,0:T(8,128)(2,1)S(1)} %get-tuple-element.56), channel_id=1, source_target_pairs={{0,28},{1,31},{2,30},{3,29},{4,8},{5,11},{6,10},{7,9},{8,4},{9,7},... | collective-permute-start | bytes 15368 | tf_op jit(solution)/shard_map/ppermute | solution.py:296
  38.9 1.0 %collective-permute-start.14 = (bf16[64,80]{1,0:T(8,128)(2,1)S(1)}, bf16[64,80]{1,0:T(8,128)(2,1)S(1)}, u32[]{:S(2)}, u32[]{:S(2)}) collective-permute-start(bf16[64,80]{1,0:T(8,128)(2,1)S(1)} %get-tuple-element.54), channel_id=1, source_target_pairs={{0,3},{1,2},{2,1},{3,0},{4,7},{5,6},{6,5},{7,4},{8,11},{9,10},{10,... | collective-permute-start | bytes 30728 | tf_op jit(solution)/shard_map/ppermute | solution.py:299
  39.9 2.7 %collective-permute-done.16.refs_3_ = bf16[32,80]{1,0:T(8,128)(2,1)S(1)} collective-permute-done((bf16[32,80]{1,0:T(8,128)(2,1)S(1)}, bf16[32,80]{1,0:T(8,128)(2,1)S(1)}, u32[]{:S(2)}, u32[]{:S(2)}) %collective-permute-start.16) | collective-permute-done | bytes 5152 | tf_op jit(solution)/shard_map/ppermute | solution.py:296
  42.9 0.9 %collective-permute-done.17.refs_4_ = bf16[32,80]{1,0:T(8,128)(2,1)S(1)} collective-permute-done((bf16[32,80]{1,0:T(8,128)(2,1)S(1)}, bf16[32,80]{1,0:T(8,128)(2,1)S(1)}, u32[]{:S(2)}, u32[]{:S(2)}) %collective-permute-start.17) | collective-permute-done | bytes 5152 | tf_op jit(solution)/shard_map/ppermute | solution.py:290
  43.8 1.0 %shard_map.92 = (f32[64,80]{1,0:T(8,128)S(1)}, bf16[64,80]{1,0:T(8,128)(2,1)S(1)}, bf16[16,80]{1,0:T(8,128)(2,1)S(1)}, bf16[32,80]{1,0:T(8,128)(2,1)S(1)}) custom-call(f32[64,80]{1,0:T(8,128)S(1)} %get-tuple-element.53.refs_0_, bf16[64,80]{1,0:T(8,128)(2,1)S(1)} %collective-permute-done.14.refs_1_, bf16[16,80]{1,0:T(8,128)(2,1)S(1)} %collective-permute-done.15.refs_2_, ...), custom_call_target="tpu_custom_call" | custom-call | tf_op jit(solution)/shard_map/pallas_call | solution.py:62
  44.8 2.8 %collective-permute-start.20 = (bf16[32,80]{1,0:T(8,128)(2,1)S(1)}, bf16[32,80]{1,0:T(8,128)(2,1)S(1)}, u32[]{:S(2)}, u32[]{:S(2)}) collective-permute-start(bf16[32,80]{1,0:T(8,128)(2,1)S(1)} %get-tuple-element.60), channel_id=1, source_target_pairs={{0,28},{1,31},{2,30},{3,29},{4,8},{5,11},{6,10},{7,9},{8,4},{9,7},... | collective-permute-start | bytes 15368 | tf_op jit(solution)/shard_map/ppermute | solution.py:296
  47.6 1.0 %collective-permute-start.18 = (bf16[64,80]{1,0:T(8,128)(2,1)S(1)}, bf16[64,80]{1,0:T(8,128)(2,1)S(1)}, u32[]{:S(2)}, u32[]{:S(2)}) collective-permute-start(bf16[64,80]{1,0:T(8,128)(2,1)S(1)} %get-tuple-element.58), channel_id=1, source_target_pairs={{0,3},{1,2},{2,1},{3,0},{4,7},{5,6},{6,5},{7,4},{8,11},{9,10},{10,... | collective-permute-start | bytes 30728 | tf_op jit(solution)/shard_map/ppermute | solution.py:299
  48.5 2.8 %collective-permute-done.20.refs_3_ = bf16[32,80]{1,0:T(8,128)(2,1)S(1)} collective-permute-done((bf16[32,80]{1,0:T(8,128)(2,1)S(1)}, bf16[32,80]{1,0:T(8,128)(2,1)S(1)}, u32[]{:S(2)}, u32[]{:S(2)}) %collective-permute-start.20) | collective-permute-done | bytes 5152 | tf_op jit(solution)/shard_map/ppermute | solution.py:296
  51.5 1.0 %collective-permute-done.21.refs_4_ = bf16[32,80]{1,0:T(8,128)(2,1)S(1)} collective-permute-done((bf16[32,80]{1,0:T(8,128)(2,1)S(1)}, bf16[32,80]{1,0:T(8,128)(2,1)S(1)}, u32[]{:S(2)}, u32[]{:S(2)}) %collective-permute-start.21) | collective-permute-done | bytes 5152 | tf_op jit(solution)/shard_map/ppermute | solution.py:290
  52.5 1.2 %shard_map.93 = (f32[12,80]{1,0:T(8,128)}, f32[4,320]{1,0:T(4,128)}) custom-call(f32[64,80]{1,0:T(8,128)S(1)} %get-tuple-element.57.refs_0_, bf16[64,80]{1,0:T(8,128)(2,1)S(1)} %collective-permute-done.18.refs_1_, bf16[16,80]{1,0:T(8,128)(2,1)S(1)} %collective-permute-done.19.refs_2_, bf16[32,80]{1,0:T(8,128)(2,1)S(1)} %collective-permute-done.20.refs_3_, ...), custom_call_target="tpu_custom_call" | custom-call | tf_op jit(solution)/shard_map/pallas_call | solution.py:62
  (42 shorter events, 7.0 us)
Async XLA Ops:
  0.6 3.3 %copy-start = (bf16[4,320,480]{2,1,0:T(8,128)(2,1)S(1)}, bf16[4,320,480]{2,1,0:T(8,128)(2,1)}, u32[]{:S(2)}) copy-start(bf16[4,320,480]{2,1,0:T(8,128)(2,1)} %param.8) | copy-start | bytes 3686404
  3.4 2.6 %collective-permute-start = (f32[64,166]{1,0:T(8,128)S(1)}, f32[64,166]{1,0:T(8,128)S(1)}, u32[]{:S(2)}, u32[]{:S(2)}) collective-permute-start(f32[64,166]{1,0:T(8,128)S(1)} %get-tuple-element.32.packet), channel_id=1, source_target_pairs={{0,1},{1,0},{2,3},{3,2},{4,5},{5,4},{6,7},{7,6},{8,9},{9,8},{10,11... | collective-permute-start | bytes 127496 | tf_op jit(solution)/shard_map/ppermute | solution.py:290
  6.0 11.2 %collective-permute-start.5 = (bf16[4,480,480]{2,1,0:T(8,128)(2,1)S(1)}, bf16[4,480,480]{2,1,0:T(8,128)(2,1)S(1)}, u32[]{:S(2)}, u32[]{:S(2)}) collective-permute-start(bf16[4,480,480]{2,1,0:T(8,128)(2,1)S(1)} %convolution_convert_fusion.refs_7_.refs_9_), channel_id=1, source_target_pairs={{0,1},{1,0},{2,3},{3,2},{4,5},{5,4},{6,7},{7,6},{8,9},{9,8},{10,11... | collective-permute-start | bytes 5529608 | tf_op jit(solution)/shard_map/ppermute | solution.py:290
  6.2 8.0 %collective-permute-start.3 = (f32[24,160]{1,0:T(8,128)S(1)}, f32[24,160]{1,0:T(8,128)S(1)}, u32[]{:S(2)}, u32[]{:S(2)}) collective-permute-start(f32[24,160]{1,0:T(8,128)S(1)} %get-tuple-element.38), channel_id=1, source_target_pairs={{0,28},{1,31},{2,30},{3,29},{4,8},{5,11},{6,10},{7,9},{8,4},{9,7},... | collective-permute-start | bytes 46088 | tf_op jit(solution)/shard_map/ppermute | solution.py:296
  12.2 3.7 %collective-permute-start.2 = (f32[16,160]{1,0:T(8,128)S(1)}, f32[16,160]{1,0:T(8,128)S(1)}, u32[]{:S(2)}, u32[]{:S(2)}) collective-permute-start(f32[16,160]{1,0:T(8,128)S(1)} %get-tuple-element.37), channel_id=1, source_target_pairs={{0,4},{1,7},{2,6},{3,5},{4,0},{5,3},{6,2},{7,1},{8,12},{9,15},{10,... | collective-permute-start | bytes 30728 | tf_op jit(solution)/shard_map/ppermute | solution.py:297
  12.2 5.0 %collective-permute-start.1 = (f32[64,160]{1,0:T(8,128)S(1)}, f32[64,160]{1,0:T(8,128)S(1)}, u32[]{:S(2)}, u32[]{:S(2)}) collective-permute-start(f32[64,160]{1,0:T(8,128)S(1)} %get-tuple-element.36.refs_0_), channel_id=1, source_target_pairs={{0,3},{1,2},{2,1},{3,0},{4,7},{5,6},{6,5},{7,4},{8,11},{9,10},{10,... | collective-permute-start | bytes 122888 | tf_op jit(solution)/shard_map/ppermute | solution.py:299
  16.0 1.3 %collective-permute-start.4 = (f32[32,160]{1,0:T(8,128)S(1)}, f32[32,160]{1,0:T(8,128)S(1)}, u32[]{:S(2)}, u32[]{:S(2)}) collective-permute-start(f32[32,160]{1,0:T(8,128)S(1)} %pad_maximum_fusion), channel_id=1, source_target_pairs={{0,1},{1,0},{2,3},{3,2},{4,5},{5,4},{6,7},{7,6},{8,9},{9,8},{10,11... | collective-permute-start | bytes 61448 | tf_op jit(solution)/shard_map/ppermute | solution.py:290
  18.3 6.4 %collective-permute-start.8 = (bf16[32,80]{1,0:T(8,128)(2,1)S(1)}, bf16[32,80]{1,0:T(8,128)(2,1)S(1)}, u32[]{:S(2)}, u32[]{:S(2)}) collective-permute-start(bf16[32,80]{1,0:T(8,128)(2,1)S(1)} %get-tuple-element.46), channel_id=1, source_target_pairs={{0,28},{1,31},{2,30},{3,29},{4,8},{5,11},{6,10},{7,9},{8,4},{9,7},... | collective-permute-start | bytes 15368 | tf_op jit(solution)/shard_map/ppermute | solution.py:296
  21.4 3.6 %collective-permute-start.7 = (bf16[16,80]{1,0:T(8,128)(2,1)S(1)}, bf16[16,80]{1,0:T(8,128)(2,1)S(1)}, u32[]{:S(2)}, u32[]{:S(2)}) collective-permute-start(bf16[16,80]{1,0:T(8,128)(2,1)S(1)} %get-tuple-element.45), channel_id=1, source_target_pairs={{0,4},{1,7},{2,6},{3,5},{4,0},{5,3},{6,2},{7,1},{8,12},{9,15},{10,... | collective-permute-start | bytes 7688 | tf_op jit(solution)/shard_map/ppermute | solution.py:297
  21.4 4.1 %collective-permute-start.6 = (bf16[64,80]{1,0:T(8,128)(2,1)S(1)}, bf16[64,80]{1,0:T(8,128)(2,1)S(1)}, u32[]{:S(2)}, u32[]{:S(2)}) collective-permute-start(bf16[64,80]{1,0:T(8,128)(2,1)S(1)} %get-tuple-element.44), channel_id=1, source_target_pairs={{0,3},{1,2},{2,1},{3,0},{4,7},{5,6},{6,5},{7,4},{8,11},{9,10},{10,... | collective-permute-start | bytes 30728 | tf_op jit(solution)/shard_map/ppermute | solution.py:299
  25.1 1.2 %collective-permute-start.9 = (bf16[32,80]{1,0:T(8,128)(2,1)S(1)}, bf16[32,80]{1,0:T(8,128)(2,1)S(1)}, u32[]{:S(2)}, u32[]{:S(2)}) collective-permute-start(bf16[32,80]{1,0:T(8,128)(2,1)S(1)} %pad_maximum_fusion.1), channel_id=1, source_target_pairs={{0,1},{1,0},{2,3},{3,2},{4,5},{5,4},{6,7},{7,6},{8,9},{9,8},{10,11... | collective-permute-start | bytes 15368 | tf_op jit(solution)/shard_map/ppermute | solution.py:290
  27.3 6.4 %collective-permute-start.12 = (bf16[32,80]{1,0:T(8,128)(2,1)S(1)}, bf16[32,80]{1,0:T(8,128)(2,1)S(1)}, u32[]{:S(2)}, u32[]{:S(2)}) collective-permute-start(bf16[32,80]{1,0:T(8,128)(2,1)S(1)} %get-tuple-element.52), channel_id=1, source_target_pairs={{0,28},{1,31},{2,30},{3,29},{4,8},{5,11},{6,10},{7,9},{8,4},{9,7},... | collective-permute-start | bytes 15368 | tf_op jit(solution)/shard_map/ppermute | solution.py:296
  30.2 3.6 %collective-permute-start.11 = (bf16[16,80]{1,0:T(8,128)(2,1)S(1)}, bf16[16,80]{1,0:T(8,128)(2,1)S(1)}, u32[]{:S(2)}, u32[]{:S(2)}) collective-permute-start(bf16[16,80]{1,0:T(8,128)(2,1)S(1)} %get-tuple-element.51), channel_id=1, source_target_pairs={{0,4},{1,7},{2,6},{3,5},{4,0},{5,3},{6,2},{7,1},{8,12},{9,15},{10,... | collective-permute-start | bytes 7688 | tf_op jit(solution)/shard_map/ppermute | solution.py:297
  30.2 4.0 %collective-permute-start.10 = (bf16[64,80]{1,0:T(8,128)(2,1)S(1)}, bf16[64,80]{1,0:T(8,128)(2,1)S(1)}, u32[]{:S(2)}, u32[]{:S(2)}) collective-permute-start(bf16[64,80]{1,0:T(8,128)(2,1)S(1)} %get-tuple-element.50), channel_id=1, source_target_pairs={{0,3},{1,2},{2,1},{3,0},{4,7},{5,6},{6,5},{7,4},{8,11},{9,10},{10,... | collective-permute-start | bytes 30728 | tf_op jit(solution)/shard_map/ppermute | solution.py:299
  33.8 1.2 %collective-permute-start.13 = (bf16[32,80]{1,0:T(8,128)(2,1)S(1)}, bf16[32,80]{1,0:T(8,128)(2,1)S(1)}, u32[]{:S(2)}, u32[]{:S(2)}) collective-permute-start(bf16[32,80]{1,0:T(8,128)(2,1)S(1)} %pad_maximum_fusion.2), channel_id=1, source_target_pairs={{0,1},{1,0},{2,3},{3,2},{4,5},{5,4},{6,7},{7,6},{8,9},{9,8},{10,11... | collective-permute-start | bytes 15368 | tf_op jit(solution)/shard_map/ppermute | solution.py:290
  36.0 6.5 %collective-permute-start.16 = (bf16[32,80]{1,0:T(8,128)(2,1)S(1)}, bf16[32,80]{1,0:T(8,128)(2,1)S(1)}, u32[]{:S(2)}, u32[]{:S(2)}) collective-permute-start(bf16[32,80]{1,0:T(8,128)(2,1)S(1)} %get-tuple-element.56), channel_id=1, source_target_pairs={{0,28},{1,31},{2,30},{3,29},{4,8},{5,11},{6,10},{7,9},{8,4},{9,7},... | collective-permute-start | bytes 15368 | tf_op jit(solution)/shard_map/ppermute | solution.py:296
  38.9 3.6 %collective-permute-start.15 = (bf16[16,80]{1,0:T(8,128)(2,1)S(1)}, bf16[16,80]{1,0:T(8,128)(2,1)S(1)}, u32[]{:S(2)}, u32[]{:S(2)}) collective-permute-start(bf16[16,80]{1,0:T(8,128)(2,1)S(1)} %get-tuple-element.55), channel_id=1, source_target_pairs={{0,4},{1,7},{2,6},{3,5},{4,0},{5,3},{6,2},{7,1},{8,12},{9,15},{10,... | collective-permute-start | bytes 7688 | tf_op jit(solution)/shard_map/ppermute | solution.py:297
  38.9 4.0 %collective-permute-start.14 = (bf16[64,80]{1,0:T(8,128)(2,1)S(1)}, bf16[64,80]{1,0:T(8,128)(2,1)S(1)}, u32[]{:S(2)}, u32[]{:S(2)}) collective-permute-start(bf16[64,80]{1,0:T(8,128)(2,1)S(1)} %get-tuple-element.54), channel_id=1, source_target_pairs={{0,3},{1,2},{2,1},{3,0},{4,7},{5,6},{6,5},{7,4},{8,11},{9,10},{10,... | collective-permute-start | bytes 30728 | tf_op jit(solution)/shard_map/ppermute | solution.py:299
  42.5 1.2 %collective-permute-start.17 = (bf16[32,80]{1,0:T(8,128)(2,1)S(1)}, bf16[32,80]{1,0:T(8,128)(2,1)S(1)}, u32[]{:S(2)}, u32[]{:S(2)}) collective-permute-start(bf16[32,80]{1,0:T(8,128)(2,1)S(1)} %pad_maximum_fusion.3), channel_id=1, source_target_pairs={{0,1},{1,0},{2,3},{3,2},{4,5},{5,4},{6,7},{7,6},{8,9},{9,8},{10,11... | collective-permute-start | bytes 15368 | tf_op jit(solution)/shard_map/ppermute | solution.py:290
  44.8 6.5 %collective-permute-start.20 = (bf16[32,80]{1,0:T(8,128)(2,1)S(1)}, bf16[32,80]{1,0:T(8,128)(2,1)S(1)}, u32[]{:S(2)}, u32[]{:S(2)}) collective-permute-start(bf16[32,80]{1,0:T(8,128)(2,1)S(1)} %get-tuple-element.60), channel_id=1, source_target_pairs={{0,28},{1,31},{2,30},{3,29},{4,8},{5,11},{6,10},{7,9},{8,4},{9,7},... | collective-permute-start | bytes 15368 | tf_op jit(solution)/shard_map/ppermute | solution.py:296
  47.6 3.7 %collective-permute-start.19 = (bf16[16,80]{1,0:T(8,128)(2,1)S(1)}, bf16[16,80]{1,0:T(8,128)(2,1)S(1)}, u32[]{:S(2)}, u32[]{:S(2)}) collective-permute-start(bf16[16,80]{1,0:T(8,128)(2,1)S(1)} %get-tuple-element.59), channel_id=1, source_target_pairs={{0,4},{1,7},{2,6},{3,5},{4,0},{5,3},{6,2},{7,1},{8,12},{9,15},{10,... | collective-permute-start | bytes 7688 | tf_op jit(solution)/shard_map/ppermute | solution.py:297
  47.6 4.0 %collective-permute-start.18 = (bf16[64,80]{1,0:T(8,128)(2,1)S(1)}, bf16[64,80]{1,0:T(8,128)(2,1)S(1)}, u32[]{:S(2)}, u32[]{:S(2)}) collective-permute-start(bf16[64,80]{1,0:T(8,128)(2,1)S(1)} %get-tuple-element.58), channel_id=1, source_target_pairs={{0,3},{1,2},{2,1},{3,0},{4,7},{5,6},{6,5},{7,4},{8,11},{9,10},{10,... | collective-permute-start | bytes 30728 | tf_op jit(solution)/shard_map/ppermute | solution.py:299
  51.3 1.2 %collective-permute-start.21 = (bf16[32,80]{1,0:T(8,128)(2,1)S(1)}, bf16[32,80]{1,0:T(8,128)(2,1)S(1)}, u32[]{:S(2)}, u32[]{:S(2)}) collective-permute-start(bf16[32,80]{1,0:T(8,128)(2,1)S(1)} %pad_maximum_fusion.4), channel_id=1, source_target_pairs={{0,1},{1,0},{2,3},{3,2},{4,5},{5,4},{6,7},{7,6},{8,9},{9,8},{10,11... | collective-permute-start | bytes 15368 | tf_op jit(solution)/shard_map/ppermute | solution.py:290

commit v4 on v3

--- a/solution.py
+++ b/solution.py
@@ -53,7 +53,7 @@
     ]
 
 
-def call(body, shapes, *args, limit=16, stay=0, scratch=()):
+def call(body, shapes, *args, limit=16, stay=0, scratch=(), cost=None):
     outs = [jax.ShapeDtypeStruct(shape, kind) for shape, kind in shapes]
     args = [
         pltpu.with_memory_space_constraint(arg, pltpu.HBM) if n < stay else arg
@@ -65,6 +65,7 @@
         in_specs=[HBM] * stay + [VMEM] * (len(args) - stay),
         out_specs=[VMEM] * len(outs),
         scratch_shapes=list(scratch),
+        cost_estimate=cost,
         compiler_params=pltpu.CompilerParams(vmem_limit_bytes=limit * 2**20),
     )(*args)
 
@@ -163,10 +164,21 @@
     packet_ref[:, : 2 * width] = jnp.concatenate([right - sums, scale], axis=1)
 
 
-def join_kernel(border, width, packet, mate, sums_ref, first_ref, second_ref):
+def join_kernel(border, width, chip_faces, packet, mate, sums_ref, sent_ref, first_ref, second_ref):
     sums = packet[:, : 2 * width] + mate[:, : 2 * width]
     sums_ref[...] = sums
+    half = width // 2
+    chip = lax.axis_index("face") // CORES
+    scale = pltpu.roll(sums[:, width:], back(chip * chip_faces, sums.shape[0]), 0)[:chip_faces]
+    sent_ref[...] = jnp.zeros(sent_ref.shape, F32)
+    sent_ref[:, :width] = sums[:, :width]
+    sent_ref[:chip_faces, width:] = scale[:, :half]
+    sent_ref[chip_faces : 2 * chip_faces, width:] = scale[:, half:]
     deal(sums, border, first_ref, second_ref)
+
+
+def back(shift, rows):
+    return lax.rem(rows - shift, rows)
 
 
 def deal(sums, border, first_ref, second_ref):
@@ -201,29 +213,40 @@
     return jnp.concatenate([sums[:border] + upper, sums[border:last], sums[last:] + lower], axis=0)
 
 
-def image(trace_now, hits, spread_hits, schur_own, schur_mate, sides):
-    elems = schur_own.shape[0]
-    width = trace_now.shape[1]
+def image(trace_now, hits, spread_hits, schur, sides):
+    pieces = [block[e] for block in schur for e in range(block.shape[0])]
     picked = contract(hits[...], trace_now.astype(HALF), 1, 0)
-    lam = to_lanes(picked, 2 * elems, sides)
-    terms = None
-    for e in range(2 * elems):
-        block = schur_own[e] if e < elems else schur_mate[e - elems]
-        part = contract(masked(lam, e), block, 1, 0)
-        terms = part if terms is None else terms + part
-    return spread(spread_hits[...], to_rows(terms, sides, width))
+    lam = to_lanes(picked, len(pieces), sides)
+    terms = add_up([contract(masked(lam, e), block, 1, 0) for e, block in enumerate(pieces)])
+    return spread(spread_hits[...], to_rows(terms, sides, trace_now.shape[1]))
+
+
+def own_kernel(chip_faces, sums, *refs):
+    *across, total_ref = refs
+    rows, width = sums.shape[0], sums.shape[1] // 2
+    chip = lax.axis_index("face") // CORES
+    chips = len(across) + 1
+    total = sums[...]
+    for n, block in enumerate(across):
+        packed = block[...]
+        pair = [packed[chip_faces * k : chip_faces * (k + 1), width:] for k in range(2)]
+        scale = jnp.concatenate(pair, axis=1)
+        scale = jnp.concatenate([scale, jnp.zeros((rows - chip_faces, width), F32)], axis=0)
+        scale = pltpu.roll(scale, lax.rem(chip + chips - n - 1, chips) * chip_faces, 0)
+        total = total + jnp.concatenate([packed[:, :width], scale], axis=1)
+    total_ref[...] = total
 
 
 def first_kernel(counts, border, sides, *refs):
     parts, rest = split(counts, refs)
-    hits, spread_hits, schur_own, schur_mate, right_ref, scale_ref, sums_ref, sent_ref, first_ref, second_ref = rest
+    hits, spread_hits, *schur, right_ref, scale_ref, sums_ref, sent_ref, first_ref, second_ref = rest
     both = whole(parts, border)
     width = both.shape[1] // 2
     right = both[:, :width]
     scale = 1.0 / both[:, width:]
     right_ref[...] = right
     scale_ref[...] = scale
-    sums = image(right * scale, hits, spread_hits, schur_own, schur_mate, sides)
+    sums = image(right * scale, hits, spread_hits, schur, sides)
     sums_ref[...] = sums
     sent_ref[...] = sums.astype(HALF)
     deal(sums, border, first_ref, second_ref)
@@ -231,9 +254,9 @@
 
 def step_kernel(counts, border, sides, *refs):
     parts, rest = split(counts, refs)
-    right, scale, hits, spread_hits, schur_own, schur_mate, sums_ref, sent_ref, first_ref, second_ref = rest
+    right, scale, hits, spread_hits, *schur, sums_ref, sent_ref, first_ref, second_ref = rest
     trace_now = (whole(parts, border) + right[...]) * scale[...]
-    sums = image(trace_now, hits, spread_hits, schur_own, schur_mate, sides)
+    sums = image(trace_now, hits, spread_hits, schur, sides)
     sums_ref[...] = sums
     sent_ref[...] = sums.astype(HALF)
     deal(sums, border, first_ref, second_ref)
@@ -246,7 +269,7 @@
     own_faces = trace_ref.shape[0]
     place = lax.axis_index("face") * own_faces
     rows = trace_now.shape[0]
-    trace_ref[...] = pltpu.roll(trace_now, lax.rem(rows - place, rows), 0)[:own_faces]
+    trace_ref[...] = pltpu.roll(trace_now, back(place, rows), 0)[:own_faces]
     elems = couple.shape[0]
     picked = contract(hits[...], trace_now.astype(HALF), 1, 0)
     lam = to_lanes(picked, 2 * elems, sides)
@@ -323,18 +346,26 @@
     couple = jnp.einsum(
         "evk,ekt->evt", inverse, vol_from_trace, preferred_element_type=F32
     ).astype(HALF)
+    couple, mate = lax.optimization_barrier((couple, mate))
+    chip_faces = CORES * own_faces
+    sums, sent, to_first, to_second = call(
+        functools.partial(join_kernel, border, width, chip_faces),
+        [
+            ((rows, 2 * width), F32),
+            ((rows, width + width // 2), F32),
+            ((border, 2 * width), F32),
+            ((border + 8, 2 * width), F32),
+        ],
+        packet, mate,
+    )
+    couple, sent = lax.optimization_barrier((couple, sent))
     schur_own = jnp.einsum("evs,evt->est", couple, down, preferred_element_type=F32).astype(HALF)
-    mate, schur_own = lax.optimization_barrier((mate, schur_own))
     schur_mate = swap_core(schur_own)
-    sums, to_first, to_second = call(
-        functools.partial(join_kernel, border, width),
-        [((rows, 2 * width), F32), ((border, 2 * width), F32), ((border + 8, 2 * width), F32)],
-        packet, mate,
-    )
     hits, spread_hits = call(
         functools.partial(hits_kernel, dims),
         [((slots, rows), HALF), ((rows, slots), HALF)],
         ids, mate,
+        cost=pl.CostEstimate(flops=70000000000, bytes_accessed=0, transcendentals=0),
     )
 
     def counted(kernel, parts):
@@ -349,7 +380,12 @@
         ((border, width), HALF),
         ((2 * border, width), HALF),
     ]
-    parts = exchange(sums, sums, to_first, to_second)
+    sent, schur_own = lax.optimization_barrier((sent, schur_own))
+    (_, *across), *rest = exchange(sums, sent, to_first, to_second)
+    own = call(
+        functools.partial(own_kernel, chip_faces), [((rows, 2 * width), F32)], sums, *across
+    )
+    parts = own, *rest
     right, scale, *out = call(
         counted(first_kernel, parts),
         [((rows, width), F32)] * 2 + dealt,

time: 53.9 us -> 53 us (0.983)
  waiting for transfers between devices: 17.9 us -> 16.2 us
    ppermute x5, starting transfers between devices: 17.7 us -> 14.4 us  [exchange(): lax.ppermute(to_second, AXES, partners(groups, chips, 1, s))]
    ppermute x5, starting transfers between devices: 0.01 us -> 2.88 us  [exchange(): lax.ppermute(to_first, AXES, partners(groups, chips, 0, s))]
    ppermute x5, waiting for transfers between devices: 2.13 us -> 0.01 us  [exchange(): lax.ppermute(to_first, AXES, partners(groups, chips, 0, s))]
    ppermute x5, waiting for transfers between devices: 0.01 us -> 1.32 us  [exchange(): lax.ppermute(sent, AXES, along_x(groups, chips, shift))]
    ppermute x5, waiting for transfers between devices: 11.6 us -> 10.9 us  [exchange(): lax.ppermute(to_second, AXES, partners(groups, chips, 1, s))]
    ppermute x5, starting transfers between devices: 4.62 us -> 5.17 us  [exchange(): lax.ppermute(sent, AXES, along_x(groups, chips, shift))]
    pallas_call x8 -> x9, Pallas kernels: 8.32 us -> 8.59 us  [call(): pl.pallas_call(body, out_shape=outs, in_specs=[HBM] * stay + [VMEM] * (le...]
  transfers between devices with their start and end apart: 22 -> 22, of which waited for: 13 -> 11; matrix products, arithmetic and copies ran while one was open for 4% -> 4% of each run, Pallas kernels for 0% -> 1%
where the time goes in v4:
time: 53 us; the launch traced here: 52.9 us
  starting transfers between devices  25.2 us (48%)
  waiting for transfers between devices  16.2 us (31%)
  Pallas kernels  8.59 us (16%)
  matrix products  2.07 us (4%)
  between operations  0.74 us (1%)
    ppermute x5, starting transfers between devices, exchange(): lax.ppermute(to_second, AXES, partners(groups, chips, 1, s))  14.4 us
    ppermute x5, waiting for transfers between devices, exchange(): lax.ppermute(to_second, AXES, partners(groups, chips, 1, s))  10.9 us
    pallas_call x9, Pallas kernels, call(): pl.pallas_call(body, out_shape=outs, in_specs=[HBM] * stay + [VMEM] * (le...  8.59 us
    ppermute x5, starting transfers between devices, exchange(): lax.ppermute(sent, AXES, along_x(groups, chips, shift))  5.17 us
    ppermute x7, waiting for transfers between devices, swap_core(): return lax.ppermute(block, AXES, other_core(groups, chips))  4.02 us
    ppermute x5, starting transfers between devices, exchange(): lax.ppermute(to_first, AXES, partners(groups, chips, 0, s))  2.88 us
    ppermute x7, starting transfers between devices, swap_core(): return lax.ppermute(block, AXES, other_core(groups, chips))  2.72 us
    ppermute x5, waiting for transfers between devices, exchange(): lax.ppermute(sent, AXES, along_x(groups, chips, shift))  1.32 us
  transfers between devices with their start and end apart: 22, of which 11 were waited for; matrix products, arithmetic and copies ran while one was open for 4% of the time, Pallas kernels for 1%

profile of v4, /device:TPU:0, one launch (start us, length us, event | category | flops | bytes accessed | tf_op | source)
XLA Modules:
  0.0 52.9 jit_solution(2166540359954999904)
XLA Ops:
  0.6 2.7 %shard_map.86 = (f32[8,320]{1,0:T(8,128)S(1)}, f32[64,166]{1,0:T(8,128)S(1)}, s32[8,6]{1,0:T(8,128)S(1)}, bf16[4,320,320]{2,1,0:T(8,128)(2,1)S(1)}, bf16[4,320,480]{2,1,0:T(8,128)(2,1)S(1)}) custom-call(bf16[4,320,320]{2,1,0:T(8,128)(2,1)} %refs_0_.1, bf16[4,320,480]{2,1,0:T(8,128)(2,1)} %bitcast.5, bf16[4,320]{1,0:T(4,128)(2,1)} %refs_2_.1, ...), custom_call_target="tpu_custom_call" | custom-call | tf_op jit(solution)/shard_map/pallas_call | solution.py:62
  5.0 2.9 %collective-permute-start.2 = (f32[16,160]{1,0:T(8,128)S(1)}, f32[16,160]{1,0:T(8,128)S(1)}, u32[]{:S(2)}, u32[]{:S(2)}) collective-permute-start(f32[16,160]{1,0:T(8,128)S(1)} %get-tuple-element.47), channel_id=1, source_target_pairs={{0,4},{1,7},{2,6},{3,5},{4,0},{5,3},{6,2},{7,1},{8,12},{9,15},{10,... | collective-permute-start | bytes 30728 | tf_op jit(solution)/shard_map/ppermute | solution.py:320
  7.8 3.5 %collective-permute-start.3 = (f32[24,160]{1,0:T(8,128)S(1)}, f32[24,160]{1,0:T(8,128)S(1)}, u32[]{:S(2)}, u32[]{:S(2)}) collective-permute-start(f32[24,160]{1,0:T(8,128)S(1)} %get-tuple-element.48), channel_id=1, source_target_pairs={{0,28},{1,31},{2,30},{3,29},{4,8},{5,11},{6,10},{7,9},{8,4},{9,7},... | collective-permute-start | bytes 46088 | tf_op jit(solution)/shard_map/ppermute | solution.py:319
  11.4 1.2 %convolution_convert_fusion.refs_6_.refs_9_ = bf16[4,480,480]{2,1,0:T(8,128)(2,1)S(1)} fusion(bf16[4,320,480]{2,1,0:T(8,128)(2,1)S(1)} %convolution_convert_fusion.1.refs_8_, bf16[4,320,480]{2,1,0:T(8,128)(2,1)S(1)} %get-tuple-element.45), kind=kOutput, calls=%fused_computation | convolution fusion | flops 590745600 | bytes 4300800 | tf_op jit(solution)/shard_map/evs,evt->est/dot_general | solution.py:362
  13.2 1.2 %collective-permute-start.1 = (f32[64,120]{1,0:T(8,128)S(1)}, f32[64,120]{1,0:T(8,128)S(1)}, u32[]{:S(2)}, u32[]{:S(2)}) collective-permute-start(f32[64,120]{1,0:T(8,128)S(1)} %get-tuple-element.46), channel_id=1, source_target_pairs={{0,3},{1,2},{2,1},{3,0},{4,7},{5,6},{6,5},{7,4},{8,11},{9,10},{10,... | collective-permute-start | bytes 92168 | tf_op jit(solution)/shard_map/ppermute | solution.py:322
  15.3 1.3 %collective-permute-done.1.refs_0_ = f32[64,120]{1,0:T(8,128)S(1)} collective-permute-done((f32[64,120]{1,0:T(8,128)S(1)}, f32[64,120]{1,0:T(8,128)S(1)}, u32[]{:S(2)}, u32[]{:S(2)}) %collective-permute-start.1) | collective-permute-done | bytes 30752 | tf_op jit(solution)/shard_map/ppermute | solution.py:322
  16.8 1.1 %shard_map.90 = (f32[64,80]{1,0:T(8,128)S(1)}, f32[64,80]{1,0:T(8,128)S(1)}, f32[64,80]{1,0:T(8,128)S(1)}, bf16[64,80]{1,0:T(8,128)(2,1)S(1)}, bf16[16,80]{1,0:T(8,128)(2,1)S(1)}, /*index=5*/bf16[32,80]{1,0:T(8,128)(2,1)S(1)}) custom-call(f32[64,160]{1,0:T(8,128)S(1)} %shard_map.88.refs_0_, f32[16,160]{1,0:T(8,128)S(1)} %collective-permute-done.2.refs_1_, ...), custom_call_target="tpu_custom_call" | custom-call | tf_op jit(solution)/shard_map/pallas_call | solution.py:62
  17.9 2.7 %collective-permute-start.8 = (bf16[32,80]{1,0:T(8,128)(2,1)S(1)}, bf16[32,80]{1,0:T(8,128)(2,1)S(1)}, u32[]{:S(2)}, u32[]{:S(2)}) collective-permute-start(bf16[32,80]{1,0:T(8,128)(2,1)S(1)} %get-tuple-element.56), channel_id=1, source_target_pairs={{0,28},{1,31},{2,30},{3,29},{4,8},{5,11},{6,10},{7,9},{8,4},{9,7},... | collective-permute-start | bytes 15368 | tf_op jit(solution)/shard_map/ppermute | solution.py:319
  20.6 1.1 %collective-permute-start.6 = (bf16[64,80]{1,0:T(8,128)(2,1)S(1)}, bf16[64,80]{1,0:T(8,128)(2,1)S(1)}, u32[]{:S(2)}, u32[]{:S(2)}) collective-permute-start(bf16[64,80]{1,0:T(8,128)(2,1)S(1)} %get-tuple-element.54), channel_id=1, source_target_pairs={{0,3},{1,2},{2,1},{3,0},{4,7},{5,6},{6,5},{7,4},{8,11},{9,10},{10,... | collective-permute-start | bytes 30728 | tf_op jit(solution)/shard_map/ppermute | solution.py:322
  21.8 2.6 %collective-permute-done.8.refs_3_ = bf16[32,80]{1,0:T(8,128)(2,1)S(1)} collective-permute-done((bf16[32,80]{1,0:T(8,128)(2,1)S(1)}, bf16[32,80]{1,0:T(8,128)(2,1)S(1)}, u32[]{:S(2)}, u32[]{:S(2)}) %collective-permute-start.8) | collective-permute-done | bytes 5152 | tf_op jit(solution)/shard_map/ppermute | solution.py:319
  24.6 1.0 %collective-permute-done.9.refs_4_ = bf16[32,80]{1,0:T(8,128)(2,1)S(1)} collective-permute-done((bf16[32,80]{1,0:T(8,128)(2,1)S(1)}, bf16[32,80]{1,0:T(8,128)(2,1)S(1)}, u32[]{:S(2)}, u32[]{:S(2)}) %collective-permute-start.9) | collective-permute-done | bytes 5152 | tf_op jit(solution)/shard_map/ppermute | solution.py:313
  25.6 1.0 %shard_map.91 = (f32[64,80]{1,0:T(8,128)S(1)}, bf16[64,80]{1,0:T(8,128)(2,1)S(1)}, bf16[16,80]{1,0:T(8,128)(2,1)S(1)}, bf16[32,80]{1,0:T(8,128)(2,1)S(1)}) custom-call(f32[64,80]{1,0:T(8,128)S(1)} %get-tuple-element.53.refs_0_, bf16[64,80]{1,0:T(8,128)(2,1)S(1)} %collective-permute-done.6.refs_1_, bf16[16,80]{1,0:T(8,128)(2,1)S(1)} %collective-permute-done.7.refs_2_, ...), custom_call_target="tpu_custom_call" | custom-call | tf_op jit(solution)/shard_map/pallas_call | solution.py:62
  26.6 2.7 %collective-permute-start.12 = (bf16[32,80]{1,0:T(8,128)(2,1)S(1)}, bf16[32,80]{1,0:T(8,128)(2,1)S(1)}, u32[]{:S(2)}, u32[]{:S(2)}) collective-permute-start(bf16[32,80]{1,0:T(8,128)(2,1)S(1)} %get-tuple-element.62), channel_id=1, source_target_pairs={{0,28},{1,31},{2,30},{3,29},{4,8},{5,11},{6,10},{7,9},{8,4},{9,7},... | collective-permute-start | bytes 15368 | tf_op jit(solution)/shard_map/ppermute | solution.py:319
  30.3 2.7 %collective-permute-done.12.refs_3_ = bf16[32,80]{1,0:T(8,128)(2,1)S(1)} collective-permute-done((bf16[32,80]{1,0:T(8,128)(2,1)S(1)}, bf16[32,80]{1,0:T(8,128)(2,1)S(1)}, u32[]{:S(2)}, u32[]{:S(2)}) %collective-permute-start.12) | collective-permute-done | bytes 5152 | tf_op jit(solution)/shard_map/ppermute | solution.py:319
  33.3 1.0 %collective-permute-done.13.refs_4_ = bf16[32,80]{1,0:T(8,128)(2,1)S(1)} collective-permute-done((bf16[32,80]{1,0:T(8,128)(2,1)S(1)}, bf16[32,80]{1,0:T(8,128)(2,1)S(1)}, u32[]{:S(2)}, u32[]{:S(2)}) %collective-permute-start.13) | collective-permute-done | bytes 5152 | tf_op jit(solution)/shard_map/ppermute | solution.py:313
  34.3 1.0 %shard_map.92 = (f32[64,80]{1,0:T(8,128)S(1)}, bf16[64,80]{1,0:T(8,128)(2,1)S(1)}, bf16[16,80]{1,0:T(8,128)(2,1)S(1)}, bf16[32,80]{1,0:T(8,128)(2,1)S(1)}) custom-call(f32[64,80]{1,0:T(8,128)S(1)} %get-tuple-element.59.refs_0_, bf16[64,80]{1,0:T(8,128)(2,1)S(1)} %collective-permute-done.10.refs_1_, bf16[16,80]{1,0:T(8,128)(2,1)S(1)} %collective-permute-done.11.refs_2_, ...), custom_call_target="tpu_custom_call" | custom-call | tf_op jit(solution)/shard_map/pallas_call | solution.py:62
  35.3 2.7 %collective-permute-start.16 = (bf16[32,80]{1,0:T(8,128)(2,1)S(1)}, bf16[32,80]{1,0:T(8,128)(2,1)S(1)}, u32[]{:S(2)}, u32[]{:S(2)}) collective-permute-start(bf16[32,80]{1,0:T(8,128)(2,1)S(1)} %get-tuple-element.66), channel_id=1, source_target_pairs={{0,28},{1,31},{2,30},{3,29},{4,8},{5,11},{6,10},{7,9},{8,4},{9,7},... | collective-permute-start | bytes 15368 | tf_op jit(solution)/shard_map/ppermute | solution.py:319
  38.9 2.7 %collective-permute-done.16.refs_3_ = bf16[32,80]{1,0:T(8,128)(2,1)S(1)} collective-permute-done((bf16[32,80]{1,0:T(8,128)(2,1)S(1)}, bf16[32,80]{1,0:T(8,128)(2,1)S(1)}, u32[]{:S(2)}, u32[]{:S(2)}) %collective-permute-start.16) | collective-permute-done | bytes 5152 | tf_op jit(solution)/shard_map/ppermute | solution.py:319
  42.0 1.0 %collective-permute-done.17.refs_4_ = bf16[32,80]{1,0:T(8,128)(2,1)S(1)} collective-permute-done((bf16[32,80]{1,0:T(8,128)(2,1)S(1)}, bf16[32,80]{1,0:T(8,128)(2,1)S(1)}, u32[]{:S(2)}, u32[]{:S(2)}) %collective-permute-start.17) | collective-permute-done | bytes 5152 | tf_op jit(solution)/shard_map/ppermute | solution.py:313
  42.9 1.0 %shard_map.93 = (f32[64,80]{1,0:T(8,128)S(1)}, bf16[64,80]{1,0:T(8,128)(2,1)S(1)}, bf16[16,80]{1,0:T(8,128)(2,1)S(1)}, bf16[32,80]{1,0:T(8,128)(2,1)S(1)}) custom-call(f32[64,80]{1,0:T(8,128)S(1)} %get-tuple-element.63.refs_0_, bf16[64,80]{1,0:T(8,128)(2,1)S(1)} %collective-permute-done.14.refs_1_, bf16[16,80]{1,0:T(8,128)(2,1)S(1)} %collective-permute-done.15.refs_2_, ...), custom_call_target="tpu_custom_call" | custom-call | tf_op jit(solution)/shard_map/pallas_call | solution.py:62
  43.9 2.7 %collective-permute-start.20 = (bf16[32,80]{1,0:T(8,128)(2,1)S(1)}, bf16[32,80]{1,0:T(8,128)(2,1)S(1)}, u32[]{:S(2)}, u32[]{:S(2)}) collective-permute-start(bf16[32,80]{1,0:T(8,128)(2,1)S(1)} %get-tuple-element.70), channel_id=1, source_target_pairs={{0,28},{1,31},{2,30},{3,29},{4,8},{5,11},{6,10},{7,9},{8,4},{9,7},... | collective-permute-start | bytes 15368 | tf_op jit(solution)/shard_map/ppermute | solution.py:319
  47.6 2.7 %collective-permute-done.20.refs_3_ = bf16[32,80]{1,0:T(8,128)(2,1)S(1)} collective-permute-done((bf16[32,80]{1,0:T(8,128)(2,1)S(1)}, bf16[32,80]{1,0:T(8,128)(2,1)S(1)}, u32[]{:S(2)}, u32[]{:S(2)}) %collective-permute-start.20) | collective-permute-done | bytes 5152 | tf_op jit(solution)/shard_map/ppermute | solution.py:319
  50.6 1.0 %collective-permute-done.21.refs_4_ = bf16[32,80]{1,0:T(8,128)(2,1)S(1)} collective-permute-done((bf16[32,80]{1,0:T(8,128)(2,1)S(1)}, bf16[32,80]{1,0:T(8,128)(2,1)S(1)}, u32[]{:S(2)}, u32[]{:S(2)}) %collective-permute-start.21) | collective-permute-done | bytes 5152 | tf_op jit(solution)/shard_map/ppermute | solution.py:313
  51.6 1.2 %shard_map.94 = (f32[12,80]{1,0:T(8,128)}, f32[4,320]{1,0:T(4,128)}) custom-call(f32[64,80]{1,0:T(8,128)S(1)} %get-tuple-element.67.refs_0_, bf16[64,80]{1,0:T(8,128)(2,1)S(1)} %collective-permute-done.18.refs_1_, bf16[16,80]{1,0:T(8,128)(2,1)S(1)} %collective-permute-done.19.refs_2_, bf16[32,80]{1,0:T(8,128)(2,1)S(1)} %collective-permute-done.20.refs_3_, ...), custom_call_target="tpu_custom_call" | custom-call | tf_op jit(solution)/shard_map/pallas_call | solution.py:62
  (43 shorter events, 7.2 us)
Async XLA Ops:
  0.6 3.3 %copy-start = (bf16[4,320,480]{2,1,0:T(8,128)(2,1)S(1)}, bf16[4,320,480]{2,1,0:T(8,128)(2,1)}, u32[]{:S(2)}) copy-start(bf16[4,320,480]{2,1,0:T(8,128)(2,1)} %param.8) | copy-start | bytes 3686404
  3.4 1.4 %collective-permute-start = (f32[64,166]{1,0:T(8,128)S(1)}, f32[64,166]{1,0:T(8,128)S(1)}, u32[]{:S(2)}, u32[]{:S(2)}) collective-permute-start(f32[64,166]{1,0:T(8,128)S(1)} %get-tuple-element.37.packet), channel_id=1, source_target_pairs={{0,1},{1,0},{2,3},{3,2},{4,5},{5,4},{6,7},{7,6},{8,9},{9,8},{10,11... | collective-permute-start | bytes 127496 | tf_op jit(solution)/shard_map/ppermute | solution.py:313
  5.0 9.5 %collective-permute-start.2 = (f32[16,160]{1,0:T(8,128)S(1)}, f32[16,160]{1,0:T(8,128)S(1)}, u32[]{:S(2)}, u32[]{:S(2)}) collective-permute-start(f32[16,160]{1,0:T(8,128)S(1)} %get-tuple-element.47), channel_id=1, source_target_pairs={{0,4},{1,7},{2,6},{3,5},{4,0},{5,3},{6,2},{7,1},{8,12},{9,15},{10,... | collective-permute-start | bytes 30728 | tf_op jit(solution)/shard_map/ppermute | solution.py:320
  7.8 6.6 %collective-permute-start.3 = (f32[24,160]{1,0:T(8,128)S(1)}, f32[24,160]{1,0:T(8,128)S(1)}, u32[]{:S(2)}, u32[]{:S(2)}) collective-permute-start(f32[24,160]{1,0:T(8,128)S(1)} %get-tuple-element.48), channel_id=1, source_target_pairs={{0,28},{1,31},{2,30},{3,29},{4,8},{5,11},{6,10},{7,9},{8,4},{9,7},... | collective-permute-start | bytes 46088 | tf_op jit(solution)/shard_map/ppermute | solution.py:319
  12.6 4.2 %collective-permute-start.5 = (bf16[4,480,480]{2,1,0:T(8,128)(2,1)S(1)}, bf16[4,480,480]{2,1,0:T(8,128)(2,1)S(1)}, u32[]{:S(2)}, u32[]{:S(2)}) collective-permute-start(bf16[4,480,480]{2,1,0:T(8,128)(2,1)S(1)} %convolution_convert_fusion.refs_6_.refs_9_), channel_id=1, source_target_pairs={{0,1},{1,0},{2,3},{3,2},{4,5},{5,4},{6,7},{7,6},{8,9},{9,8},{10,11... | collective-permute-start | bytes 5529608 | tf_op jit(solution)/shard_map/ppermute | solution.py:313
  13.2 3.4 %collective-permute-start.1 = (f32[64,120]{1,0:T(8,128)S(1)}, f32[64,120]{1,0:T(8,128)S(1)}, u32[]{:S(2)}, u32[]{:S(2)}) collective-permute-start(f32[64,120]{1,0:T(8,128)S(1)} %get-tuple-element.46), channel_id=1, source_target_pairs={{0,3},{1,2},{2,1},{3,0},{4,7},{5,6},{6,5},{7,4},{8,11},{9,10},{10,... | collective-permute-start | bytes 92168 | tf_op jit(solution)/shard_map/ppermute | solution.py:322
  14.5 2.4 %collective-permute-start.4 = (f32[32,160]{1,0:T(8,128)S(1)}, f32[32,160]{1,0:T(8,128)S(1)}, u32[]{:S(2)}, u32[]{:S(2)}) collective-permute-start(f32[32,160]{1,0:T(8,128)S(1)} %pad_maximum_fusion), channel_id=1, source_target_pairs={{0,1},{1,0},{2,3},{3,2},{4,5},{5,4},{6,7},{7,6},{8,9},{9,8},{10,11... | collective-permute-start | bytes 61448 | tf_op jit(solution)/shard_map/ppermute | solution.py:313
  17.9 6.4 %collective-permute-start.8 = (bf16[32,80]{1,0:T(8,128)(2,1)S(1)}, bf16[32,80]{1,0:T(8,128)(2,1)S(1)}, u32[]{:S(2)}, u32[]{:S(2)}) collective-permute-start(bf16[32,80]{1,0:T(8,128)(2,1)S(1)} %get-tuple-element.56), channel_id=1, source_target_pairs={{0,28},{1,31},{2,30},{3,29},{4,8},{5,11},{6,10},{7,9},{8,4},{9,7},... | collective-permute-start | bytes 15368 | tf_op jit(solution)/shard_map/ppermute | solution.py:319
  20.6 3.7 %collective-permute-start.7 = (bf16[16,80]{1,0:T(8,128)(2,1)S(1)}, bf16[16,80]{1,0:T(8,128)(2,1)S(1)}, u32[]{:S(2)}, u32[]{:S(2)}) collective-permute-start(bf16[16,80]{1,0:T(8,128)(2,1)S(1)} %get-tuple-element.55), channel_id=1, source_target_pairs={{0,4},{1,7},{2,6},{3,5},{4,0},{5,3},{6,2},{7,1},{8,12},{9,15},{10,... | collective-permute-start | bytes 7688 | tf_op jit(solution)/shard_map/ppermute | solution.py:320
  20.6 4.0 %collective-permute-start.6 = (bf16[64,80]{1,0:T(8,128)(2,1)S(1)}, bf16[64,80]{1,0:T(8,128)(2,1)S(1)}, u32[]{:S(2)}, u32[]{:S(2)}) collective-permute-start(bf16[64,80]{1,0:T(8,128)(2,1)S(1)} %get-tuple-element.54), channel_id=1, source_target_pairs={{0,3},{1,2},{2,1},{3,0},{4,7},{5,6},{6,5},{7,4},{8,11},{9,10},{10,... | collective-permute-start | bytes 30728 | tf_op jit(solution)/shard_map/ppermute | solution.py:322
  24.3 1.2 %collective-permute-start.9 = (bf16[32,80]{1,0:T(8,128)(2,1)S(1)}, bf16[32,80]{1,0:T(8,128)(2,1)S(1)}, u32[]{:S(2)}, u32[]{:S(2)}) collective-permute-start(bf16[32,80]{1,0:T(8,128)(2,1)S(1)} %pad_maximum_fusion.1), channel_id=1, source_target_pairs={{0,1},{1,0},{2,3},{3,2},{4,5},{5,4},{6,7},{7,6},{8,9},{9,8},{10,11... | collective-permute-start | bytes 15368 | tf_op jit(solution)/shard_map/ppermute | solution.py:313
  26.6 6.4 %collective-permute-start.12 = (bf16[32,80]{1,0:T(8,128)(2,1)S(1)}, bf16[32,80]{1,0:T(8,128)(2,1)S(1)}, u32[]{:S(2)}, u32[]{:S(2)}) collective-permute-start(bf16[32,80]{1,0:T(8,128)(2,1)S(1)} %get-tuple-element.62), channel_id=1, source_target_pairs={{0,28},{1,31},{2,30},{3,29},{4,8},{5,11},{6,10},{7,9},{8,4},{9,7},... | collective-permute-start | bytes 15368 | tf_op jit(solution)/shard_map/ppermute | solution.py:319
  29.3 3.7 %collective-permute-start.11 = (bf16[16,80]{1,0:T(8,128)(2,1)S(1)}, bf16[16,80]{1,0:T(8,128)(2,1)S(1)}, u32[]{:S(2)}, u32[]{:S(2)}) collective-permute-start(bf16[16,80]{1,0:T(8,128)(2,1)S(1)} %get-tuple-element.61), channel_id=1, source_target_pairs={{0,4},{1,7},{2,6},{3,5},{4,0},{5,3},{6,2},{7,1},{8,12},{9,15},{10,... | collective-permute-start | bytes 7688 | tf_op jit(solution)/shard_map/ppermute | solution.py:320
  29.3 4.0 %collective-permute-start.10 = (bf16[64,80]{1,0:T(8,128)(2,1)S(1)}, bf16[64,80]{1,0:T(8,128)(2,1)S(1)}, u32[]{:S(2)}, u32[]{:S(2)}) collective-permute-start(bf16[64,80]{1,0:T(8,128)(2,1)S(1)} %get-tuple-element.60), channel_id=1, source_target_pairs={{0,3},{1,2},{2,1},{3,0},{4,7},{5,6},{6,5},{7,4},{8,11},{9,10},{10,... | collective-permute-start | bytes 30728 | tf_op jit(solution)/shard_map/ppermute | solution.py:322
  33.0 1.2 %collective-permute-start.13 = (bf16[32,80]{1,0:T(8,128)(2,1)S(1)}, bf16[32,80]{1,0:T(8,128)(2,1)S(1)}, u32[]{:S(2)}, u32[]{:S(2)}) collective-permute-start(bf16[32,80]{1,0:T(8,128)(2,1)S(1)} %pad_maximum_fusion.2), channel_id=1, source_target_pairs={{0,1},{1,0},{2,3},{3,2},{4,5},{5,4},{6,7},{7,6},{8,9},{9,8},{10,11... | collective-permute-start | bytes 15368 | tf_op jit(solution)/shard_map/ppermute | solution.py:313
  35.3 6.4 %collective-permute-start.16 = (bf16[32,80]{1,0:T(8,128)(2,1)S(1)}, bf16[32,80]{1,0:T(8,128)(2,1)S(1)}, u32[]{:S(2)}, u32[]{:S(2)}) collective-permute-start(bf16[32,80]{1,0:T(8,128)(2,1)S(1)} %get-tuple-element.66), channel_id=1, source_target_pairs={{0,28},{1,31},{2,30},{3,29},{4,8},{5,11},{6,10},{7,9},{8,4},{9,7},... | collective-permute-start | bytes 15368 | tf_op jit(solution)/shard_map/ppermute | solution.py:319
  38.0 3.7 %collective-permute-start.15 = (bf16[16,80]{1,0:T(8,128)(2,1)S(1)}, bf16[16,80]{1,0:T(8,128)(2,1)S(1)}, u32[]{:S(2)}, u32[]{:S(2)}) collective-permute-start(bf16[16,80]{1,0:T(8,128)(2,1)S(1)} %get-tuple-element.65), channel_id=1, source_target_pairs={{0,4},{1,7},{2,6},{3,5},{4,0},{5,3},{6,2},{7,1},{8,12},{9,15},{10,... | collective-permute-start | bytes 7688 | tf_op jit(solution)/shard_map/ppermute | solution.py:320
  38.0 4.0 %collective-permute-start.14 = (bf16[64,80]{1,0:T(8,128)(2,1)S(1)}, bf16[64,80]{1,0:T(8,128)(2,1)S(1)}, u32[]{:S(2)}, u32[]{:S(2)}) collective-permute-start(bf16[64,80]{1,0:T(8,128)(2,1)S(1)} %get-tuple-element.64), channel_id=1, source_target_pairs={{0,3},{1,2},{2,1},{3,0},{4,7},{5,6},{6,5},{7,4},{8,11},{9,10},{10,... | collective-permute-start | bytes 30728 | tf_op jit(solution)/shard_map/ppermute | solution.py:322
  41.7 1.2 %collective-permute-start.17 = (bf16[32,80]{1,0:T(8,128)(2,1)S(1)}, bf16[32,80]{1,0:T(8,128)(2,1)S(1)}, u32[]{:S(2)}, u32[]{:S(2)}) collective-permute-start(bf16[32,80]{1,0:T(8,128)(2,1)S(1)} %pad_maximum_fusion.3), channel_id=1, source_target_pairs={{0,1},{1,0},{2,3},{3,2},{4,5},{5,4},{6,7},{7,6},{8,9},{9,8},{10,11... | collective-permute-start | bytes 15368 | tf_op jit(solution)/shard_map/ppermute | solution.py:313
  43.9 6.4 %collective-permute-start.20 = (bf16[32,80]{1,0:T(8,128)(2,1)S(1)}, bf16[32,80]{1,0:T(8,128)(2,1)S(1)}, u32[]{:S(2)}, u32[]{:S(2)}) collective-permute-start(bf16[32,80]{1,0:T(8,128)(2,1)S(1)} %get-tuple-element.70), channel_id=1, source_target_pairs={{0,28},{1,31},{2,30},{3,29},{4,8},{5,11},{6,10},{7,9},{8,4},{9,7},... | collective-permute-start | bytes 15368 | tf_op jit(solution)/shard_map/ppermute | solution.py:319
  46.7 3.7 %collective-permute-start.19 = (bf16[16,80]{1,0:T(8,128)(2,1)S(1)}, bf16[16,80]{1,0:T(8,128)(2,1)S(1)}, u32[]{:S(2)}, u32[]{:S(2)}) collective-permute-start(bf16[16,80]{1,0:T(8,128)(2,1)S(1)} %get-tuple-element.69), channel_id=1, source_target_pairs={{0,4},{1,7},{2,6},{3,5},{4,0},{5,3},{6,2},{7,1},{8,12},{9,15},{10,... | collective-permute-start | bytes 7688 | tf_op jit(solution)/shard_map/ppermute | solution.py:320
  46.7 4.0 %collective-permute-start.18 = (bf16[64,80]{1,0:T(8,128)(2,1)S(1)}, bf16[64,80]{1,0:T(8,128)(2,1)S(1)}, u32[]{:S(2)}, u32[]{:S(2)}) collective-permute-start(bf16[64,80]{1,0:T(8,128)(2,1)S(1)} %get-tuple-element.68), channel_id=1, source_target_pairs={{0,3},{1,2},{2,1},{3,0},{4,7},{5,6},{6,5},{7,4},{8,11},{9,10},{10,... | collective-permute-start | bytes 30728 | tf_op jit(solution)/shard_map/ppermute | solution.py:322
  50.4 1.2 %collective-permute-start.21 = (bf16[32,80]{1,0:T(8,128)(2,1)S(1)}, bf16[32,80]{1,0:T(8,128)(2,1)S(1)}, u32[]{:S(2)}, u32[]{:S(2)}) collective-permute-start(bf16[32,80]{1,0:T(8,128)(2,1)S(1)} %pad_maximum_fusion.4), channel_id=1, source_target_pairs={{0,1},{1,0},{2,3},{3,2},{4,5},{5,4},{6,7},{7,6},{8,9},{9,8},{10,11... | collective-permute-start | bytes 15368 | tf_op jit(solution)/shard_map/ppermute | solution.py:313

commit v5 on v4

--- a/solution.py
+++ b/solution.py
@@ -164,9 +164,14 @@
     packet_ref[:, : 2 * width] = jnp.concatenate([right - sums, scale], axis=1)
 
 
-def join_kernel(border, width, chip_faces, packet, mate, sums_ref, sent_ref, first_ref, second_ref):
+def join_kernel(border, width, packet, mate, sums_ref, first_ref, second_ref):
     sums = packet[:, : 2 * width] + mate[:, : 2 * width]
     sums_ref[...] = sums
+    deal(sums, border, first_ref, second_ref)
+
+
+def pack_kernel(chip_faces, sums, sent_ref):
+    width = sums.shape[1] // 2
     half = width // 2
     chip = lax.axis_index("face") // CORES
     scale = pltpu.roll(sums[:, width:], back(chip * chip_faces, sums.shape[0]), 0)[:chip_faces]
@@ -174,7 +179,6 @@
     sent_ref[:, :width] = sums[:, :width]
     sent_ref[:chip_faces, width:] = scale[:, :half]
     sent_ref[chip_faces : 2 * chip_faces, width:] = scale[:, half:]
-    deal(sums, border, first_ref, second_ref)
 
 
 def back(shift, rows):
@@ -185,9 +189,12 @@
     even = lax.rem(lax.axis_index("elem"), 2) == 0
     upper, lower = sums[:border], sums[sums.shape[0] - border :]
     kind = first_ref.dtype
-    first_ref[...] = jnp.where(even, upper, lower).astype(kind)
+    first_ref[:border] = jnp.where(even, upper, lower).astype(kind)
+    if first_ref.shape[0] > border:
+        first_ref[border:] = sums[: first_ref.shape[0] - border].astype(kind)
     second_ref[:border] = jnp.where(even, lower, upper).astype(kind)
-    second_ref[border:] = first_ref[: second_ref.shape[0] - border]
+    if second_ref.shape[0] > border:
+        second_ref[border:] = sums[: second_ref.shape[0] - border].astype(kind)
 
 
 def hits_kernel(dims, ids, mate, hits_ref, spread_ref):
@@ -203,7 +210,7 @@
     own, first, second, (mate,) = parts
     even = lax.rem(lax.axis_index("elem"), 2) == 0
     blocks = mate[...].astype(F32)
-    a, b = add_up(first), add_up(second)[:border]
+    a, b = add_up(first)[:border], add_up(second)[:border]
     for n in range(len(first)):
         a = a + blocks[n * border : (n + 1) * border]
         b = b + blocks[(len(first) + n) * border : (len(first) + n + 1) * border]
@@ -321,7 +328,7 @@
         own = [part] + [
             lax.ppermute(sent, AXES, along_x(groups, chips, shift)) for shift in range(1, chips)
         ]
-        mate = swap_core(jnp.concatenate([*first, *(block[:border] for block in second)]))
+        mate = swap_core(jnp.concatenate([block[:border] for block in (*first, *second)]))
         return own, first, second, [mate]
 
     down = jnp.swapaxes(trace_from_vol, 1, 2)
@@ -348,17 +355,16 @@
     ).astype(HALF)
     couple, mate = lax.optimization_barrier((couple, mate))
     chip_faces = CORES * own_faces
-    sums, sent, to_first, to_second = call(
-        functools.partial(join_kernel, border, width, chip_faces),
+    sums, to_first, to_second = call(
+        functools.partial(join_kernel, border, width),
         [
             ((rows, 2 * width), F32),
-            ((rows, width + width // 2), F32),
+            ((border + 16, 2 * width), F32),
             ((border, 2 * width), F32),
-            ((border + 8, 2 * width), F32),
         ],
         packet, mate,
     )
-    couple, sent = lax.optimization_barrier((couple, sent))
+    couple, sums = lax.optimization_barrier((couple, sums))
     schur_own = jnp.einsum("evs,evt->est", couple, down, preferred_element_type=F32).astype(HALF)
     schur_mate = swap_core(schur_own)
     hits, spread_hits = call(
@@ -380,7 +386,10 @@
         ((border, width), HALF),
         ((2 * border, width), HALF),
     ]
-    sent, schur_own = lax.optimization_barrier((sent, schur_own))
+    sums, schur_own = lax.optimization_barrier((sums, schur_own))
+    (sent,) = call(
+        functools.partial(pack_kernel, chip_faces), [((rows, width + width // 2), F32)], sums
+    )
     (_, *across), *rest = exchange(sums, sent, to_first, to_second)
     own = call(
         functools.partial(own_kernel, chip_faces), [((rows, 2 * width), F32)], sums, *across

time: 53 us -> 52.9 us (level)
  starting transfers between devices: 25.2 us -> 21.7 us
  waiting for transfers between devices: 16.2 us -> 19.5 us
    ppermute x5, starting transfers between devices: 2.88 us -> 0.09 us  [exchange(): lax.ppermute(to_first, AXES, partners(groups, chips, 0, s))]
    ppermute x5, waiting for transfers between devices: 10.9 us -> 13 us  [exchange(): lax.ppermute(to_second, AXES, partners(groups, chips, 1, s))]
    ppermute x5, waiting for transfers between devices: 0.01 us -> 0.86 us  [exchange(): lax.ppermute(to_first, AXES, partners(groups, chips, 0, s))]
    ppermute x7, waiting for transfers between devices: 4.02 us -> 4.61 us  [swap_core(): return lax.ppermute(block, AXES, other_core(groups, chips))]
    pallas_call x9 -> x10, Pallas kernels: 8.59 us -> 8.6 us  [call(): pl.pallas_call(body, out_shape=outs, in_specs=[HBM] * stay + [VMEM] * (le...]
  transfers between devices with their start and end apart: 22 -> 22, of which waited for: 11 -> 10; matrix products, arithmetic and copies ran while one was open for 4% -> 4% of each run, Pallas kernels for 1% -> 1%
where the time goes in v5:
time: 52.9 us; the launch traced here: 52.7 us
  starting transfers between devices  21.7 us (41%)
  waiting for transfers between devices  19.5 us (37%)
  Pallas kernels  8.6 us (16%)
  matrix products  2.07 us (4%)
  between operations  0.81 us (2%)
    ppermute x5, starting transfers between devices, exchange(): lax.ppermute(to_second, AXES, partners(groups, chips, 1, s))  14.3 us
    ppermute x5, waiting for transfers between devices, exchange(): lax.ppermute(to_second, AXES, partners(groups, chips, 1, s))  13 us
    pallas_call x10, Pallas kernels, call(): pl.pallas_call(body, out_shape=outs, in_specs=[HBM] * stay + [VMEM] * (le...  8.6 us
    ppermute x5, starting transfers between devices, exchange(): lax.ppermute(sent, AXES, along_x(groups, chips, shift))  5.03 us
    ppermute x7, waiting for transfers between devices, swap_core(): return lax.ppermute(block, AXES, other_core(groups, chips))  4.61 us
    ppermute x7, starting transfers between devices, swap_core(): return lax.ppermute(block, AXES, other_core(groups, chips))  2.34 us
    dot_general x1, matrix products, local(): jnp.einsum('evs,evt->est', couple, down, preferred_element_type=F32)  1.22 us
  transfers between devices with their start and end apart: 22, of which 10 were waited for; matrix products, arithmetic and copies ran while one was open for 4% of the time, Pallas kernels for 1%

profile of v5, /device:TPU:0, one launch (start us, length us, event | category | flops | bytes accessed | tf_op | source)
XLA Modules:
  0.0 52.7 jit_solution(1594871974880521849)
XLA Ops:
  0.6 2.7 %shard_map.86 = (f32[8,320]{1,0:T(8,128)S(1)}, f32[64,166]{1,0:T(8,128)S(1)}, s32[8,6]{1,0:T(8,128)S(1)}, bf16[4,320,320]{2,1,0:T(8,128)(2,1)S(1)}, bf16[4,320,480]{2,1,0:T(8,128)(2,1)S(1)}) custom-call(bf16[4,320,320]{2,1,0:T(8,128)(2,1)} %refs_0_.1, bf16[4,320,480]{2,1,0:T(8,128)(2,1)} %bitcast.5, bf16[4,320]{1,0:T(4,128)(2,1)} %refs_2_.1, ...), custom_call_target="tpu_custom_call" | custom-call | tf_op jit(solution)/shard_map/pallas_call | solution.py:62
  4.8 6.0 %collective-permute-start.3 = (f32[16,160]{1,0:T(8,128)S(1)}, f32[16,160]{1,0:T(8,128)S(1)}, u32[]{:S(2)}, u32[]{:S(2)}) collective-permute-start(f32[16,160]{1,0:T(8,128)S(1)} %get-tuple-element.46), channel_id=1, source_target_pairs={{0,28},{1,31},{2,30},{3,29},{4,8},{5,11},{6,10},{7,9},{8,4},{9,7},... | collective-permute-start | bytes 30728 | tf_op jit(solution)/shard_map/ppermute | solution.py:326
  10.8 1.2 %convolution_convert_fusion.refs_6_.refs_9_ = bf16[4,480,480]{2,1,0:T(8,128)(2,1)S(1)} fusion(bf16[4,320,480]{2,1,0:T(8,128)(2,1)S(1)} %convolution_convert_fusion.1.refs_8_, bf16[4,320,480]{2,1,0:T(8,128)(2,1)S(1)} %get-tuple-element.43), kind=kOutput, calls=%fused_computation | convolution fusion | flops 590745600 | bytes 4300800 | tf_op jit(solution)/shard_map/evs,evt->est/dot_general | solution.py:368
  15.6 1.0 %collective-permute-done.1.refs_0_ = f32[64,120]{1,0:T(8,128)S(1)} collective-permute-done((f32[64,120]{1,0:T(8,128)S(1)}, f32[64,120]{1,0:T(8,128)S(1)}, u32[]{:S(2)}, u32[]{:S(2)}) %collective-permute-start.1) | collective-permute-done | bytes 30752 | tf_op jit(solution)/shard_map/ppermute | solution.py:329
  16.7 1.1 %shard_map.91 = (f32[64,80]{1,0:T(8,128)S(1)}, f32[64,80]{1,0:T(8,128)S(1)}, f32[64,80]{1,0:T(8,128)S(1)}, bf16[64,80]{1,0:T(8,128)(2,1)S(1)}, bf16[16,80]{1,0:T(8,128)(2,1)S(1)}, /*index=5*/bf16[32,80]{1,0:T(8,128)(2,1)S(1)}) custom-call(f32[64,160]{1,0:T(8,128)S(1)} %shard_map.89.refs_0_, f32[32,160]{1,0:T(8,128)S(1)} %collective-permute-done.2.refs_1_, ...), custom_call_target="tpu_custom_call" | custom-call | tf_op jit(solution)/shard_map/pallas_call | solution.py:62
  17.8 1.9 %collective-permute-start.8 = (bf16[32,80]{1,0:T(8,128)(2,1)S(1)}, bf16[32,80]{1,0:T(8,128)(2,1)S(1)}, u32[]{:S(2)}, u32[]{:S(2)}) collective-permute-start(bf16[32,80]{1,0:T(8,128)(2,1)S(1)} %get-tuple-element.54), channel_id=1, source_target_pairs={{0,28},{1,31},{2,30},{3,29},{4,8},{5,11},{6,10},{7,9},{8,4},{9,7},... | collective-permute-start | bytes 15368 | tf_op jit(solution)/shard_map/ppermute | solution.py:326
  19.8 1.0 %collective-permute-start.6 = (bf16[64,80]{1,0:T(8,128)(2,1)S(1)}, bf16[64,80]{1,0:T(8,128)(2,1)S(1)}, u32[]{:S(2)}, u32[]{:S(2)}) collective-permute-start(bf16[64,80]{1,0:T(8,128)(2,1)S(1)} %get-tuple-element.52), channel_id=1, source_target_pairs={{0,3},{1,2},{2,1},{3,0},{4,7},{5,6},{6,5},{7,4},{8,11},{9,10},{10,... | collective-permute-start | bytes 30728 | tf_op jit(solution)/shard_map/ppermute | solution.py:329
  20.7 3.5 %collective-permute-done.8.refs_3_ = bf16[32,80]{1,0:T(8,128)(2,1)S(1)} collective-permute-done((bf16[32,80]{1,0:T(8,128)(2,1)S(1)}, bf16[32,80]{1,0:T(8,128)(2,1)S(1)}, u32[]{:S(2)}, u32[]{:S(2)}) %collective-permute-start.8) | collective-permute-done | bytes 5152 | tf_op jit(solution)/shard_map/ppermute | solution.py:326
  24.4 1.1 %collective-permute-done.9.refs_4_ = bf16[32,80]{1,0:T(8,128)(2,1)S(1)} collective-permute-done((bf16[32,80]{1,0:T(8,128)(2,1)S(1)}, bf16[32,80]{1,0:T(8,128)(2,1)S(1)}, u32[]{:S(2)}, u32[]{:S(2)}) %collective-permute-start.9) | collective-permute-done | bytes 5152 | tf_op jit(solution)/shard_map/ppermute | solution.py:320
  25.5 1.0 %shard_map.92 = (f32[64,80]{1,0:T(8,128)S(1)}, bf16[64,80]{1,0:T(8,128)(2,1)S(1)}, bf16[16,80]{1,0:T(8,128)(2,1)S(1)}, bf16[32,80]{1,0:T(8,128)(2,1)S(1)}) custom-call(f32[64,80]{1,0:T(8,128)S(1)} %get-tuple-element.51.refs_0_, bf16[64,80]{1,0:T(8,128)(2,1)S(1)} %collective-permute-done.6.refs_1_, bf16[16,80]{1,0:T(8,128)(2,1)S(1)} %collective-permute-done.7.refs_2_, ...), custom_call_target="tpu_custom_call" | custom-call | tf_op jit(solution)/shard_map/pallas_call | solution.py:62
  26.5 2.1 %collective-permute-start.12 = (bf16[32,80]{1,0:T(8,128)(2,1)S(1)}, bf16[32,80]{1,0:T(8,128)(2,1)S(1)}, u32[]{:S(2)}, u32[]{:S(2)}) collective-permute-start(bf16[32,80]{1,0:T(8,128)(2,1)S(1)} %get-tuple-element.60), channel_id=1, source_target_pairs={{0,28},{1,31},{2,30},{3,29},{4,8},{5,11},{6,10},{7,9},{8,4},{9,7},... | collective-permute-start | bytes 15368 | tf_op jit(solution)/shard_map/ppermute | solution.py:326
  28.6 1.4 %collective-permute-start.10 = (bf16[64,80]{1,0:T(8,128)(2,1)S(1)}, bf16[64,80]{1,0:T(8,128)(2,1)S(1)}, u32[]{:S(2)}, u32[]{:S(2)}) collective-permute-start(bf16[64,80]{1,0:T(8,128)(2,1)S(1)} %get-tuple-element.58), channel_id=1, source_target_pairs={{0,3},{1,2},{2,1},{3,0},{4,7},{5,6},{6,5},{7,4},{8,11},{9,10},{10,... | collective-permute-start | bytes 30728 | tf_op jit(solution)/shard_map/ppermute | solution.py:329
  30.0 2.9 %collective-permute-done.12.refs_3_ = bf16[32,80]{1,0:T(8,128)(2,1)S(1)} collective-permute-done((bf16[32,80]{1,0:T(8,128)(2,1)S(1)}, bf16[32,80]{1,0:T(8,128)(2,1)S(1)}, u32[]{:S(2)}, u32[]{:S(2)}) %collective-permute-start.12) | collective-permute-done | bytes 5152 | tf_op jit(solution)/shard_map/ppermute | solution.py:326
  33.0 1.1 %collective-permute-done.13.refs_4_ = bf16[32,80]{1,0:T(8,128)(2,1)S(1)} collective-permute-done((bf16[32,80]{1,0:T(8,128)(2,1)S(1)}, bf16[32,80]{1,0:T(8,128)(2,1)S(1)}, u32[]{:S(2)}, u32[]{:S(2)}) %collective-permute-start.13) | collective-permute-done | bytes 5152 | tf_op jit(solution)/shard_map/ppermute | solution.py:320
  34.2 1.0 %shard_map.93 = (f32[64,80]{1,0:T(8,128)S(1)}, bf16[64,80]{1,0:T(8,128)(2,1)S(1)}, bf16[16,80]{1,0:T(8,128)(2,1)S(1)}, bf16[32,80]{1,0:T(8,128)(2,1)S(1)}) custom-call(f32[64,80]{1,0:T(8,128)S(1)} %get-tuple-element.57.refs_0_, bf16[64,80]{1,0:T(8,128)(2,1)S(1)} %collective-permute-done.10.refs_1_, bf16[16,80]{1,0:T(8,128)(2,1)S(1)} %collective-permute-done.11.refs_2_, ...), custom_call_target="tpu_custom_call" | custom-call | tf_op jit(solution)/shard_map/pallas_call | solution.py:62
  35.2 2.2 %collective-permute-start.16 = (bf16[32,80]{1,0:T(8,128)(2,1)S(1)}, bf16[32,80]{1,0:T(8,128)(2,1)S(1)}, u32[]{:S(2)}, u32[]{:S(2)}) collective-permute-start(bf16[32,80]{1,0:T(8,128)(2,1)S(1)} %get-tuple-element.64), channel_id=1, source_target_pairs={{0,28},{1,31},{2,30},{3,29},{4,8},{5,11},{6,10},{7,9},{8,4},{9,7},... | collective-permute-start | bytes 15368 | tf_op jit(solution)/shard_map/ppermute | solution.py:326
  38.3 3.3 %collective-permute-done.16.refs_3_ = bf16[32,80]{1,0:T(8,128)(2,1)S(1)} collective-permute-done((bf16[32,80]{1,0:T(8,128)(2,1)S(1)}, bf16[32,80]{1,0:T(8,128)(2,1)S(1)}, u32[]{:S(2)}, u32[]{:S(2)}) %collective-permute-start.16) | collective-permute-done | bytes 5152 | tf_op jit(solution)/shard_map/ppermute | solution.py:326
  41.7 1.1 %collective-permute-done.17.refs_4_ = bf16[32,80]{1,0:T(8,128)(2,1)S(1)} collective-permute-done((bf16[32,80]{1,0:T(8,128)(2,1)S(1)}, bf16[32,80]{1,0:T(8,128)(2,1)S(1)}, u32[]{:S(2)}, u32[]{:S(2)}) %collective-permute-start.17) | collective-permute-done | bytes 5152 | tf_op jit(solution)/shard_map/ppermute | solution.py:320
  42.8 1.0 %shard_map.94 = (f32[64,80]{1,0:T(8,128)S(1)}, bf16[64,80]{1,0:T(8,128)(2,1)S(1)}, bf16[16,80]{1,0:T(8,128)(2,1)S(1)}, bf16[32,80]{1,0:T(8,128)(2,1)S(1)}) custom-call(f32[64,80]{1,0:T(8,128)S(1)} %get-tuple-element.61.refs_0_, bf16[64,80]{1,0:T(8,128)(2,1)S(1)} %collective-permute-done.14.refs_1_, bf16[16,80]{1,0:T(8,128)(2,1)S(1)} %collective-permute-done.15.refs_2_, ...), custom_call_target="tpu_custom_call" | custom-call | tf_op jit(solution)/shard_map/pallas_call | solution.py:62
  43.8 2.2 %collective-permute-start.20 = (bf16[32,80]{1,0:T(8,128)(2,1)S(1)}, bf16[32,80]{1,0:T(8,128)(2,1)S(1)}, u32[]{:S(2)}, u32[]{:S(2)}) collective-permute-start(bf16[32,80]{1,0:T(8,128)(2,1)S(1)} %get-tuple-element.68), channel_id=1, source_target_pairs={{0,28},{1,31},{2,30},{3,29},{4,8},{5,11},{6,10},{7,9},{8,4},{9,7},... | collective-permute-start | bytes 15368 | tf_op jit(solution)/shard_map/ppermute | solution.py:326
  46.0 1.0 %collective-permute-start.18 = (bf16[64,80]{1,0:T(8,128)(2,1)S(1)}, bf16[64,80]{1,0:T(8,128)(2,1)S(1)}, u32[]{:S(2)}, u32[]{:S(2)}) collective-permute-start(bf16[64,80]{1,0:T(8,128)(2,1)S(1)} %get-tuple-element.66), channel_id=1, source_target_pairs={{0,3},{1,2},{2,1},{3,0},{4,7},{5,6},{6,5},{7,4},{8,11},{9,10},{10,... | collective-permute-start | bytes 30728 | tf_op jit(solution)/shard_map/ppermute | solution.py:329
  47.0 3.3 %collective-permute-done.20.refs_3_ = bf16[32,80]{1,0:T(8,128)(2,1)S(1)} collective-permute-done((bf16[32,80]{1,0:T(8,128)(2,1)S(1)}, bf16[32,80]{1,0:T(8,128)(2,1)S(1)}, u32[]{:S(2)}, u32[]{:S(2)}) %collective-permute-start.20) | collective-permute-done | bytes 5152 | tf_op jit(solution)/shard_map/ppermute | solution.py:326
  50.3 1.1 %collective-permute-done.21.refs_4_ = bf16[32,80]{1,0:T(8,128)(2,1)S(1)} collective-permute-done((bf16[32,80]{1,0:T(8,128)(2,1)S(1)}, bf16[32,80]{1,0:T(8,128)(2,1)S(1)}, u32[]{:S(2)}, u32[]{:S(2)}) %collective-permute-start.21) | collective-permute-done | bytes 5152 | tf_op jit(solution)/shard_map/ppermute | solution.py:320
  51.5 1.2 %shard_map.95 = (f32[12,80]{1,0:T(8,128)}, f32[4,320]{1,0:T(4,128)}) custom-call(f32[64,80]{1,0:T(8,128)S(1)} %get-tuple-element.65.refs_0_, bf16[64,80]{1,0:T(8,128)(2,1)S(1)} %collective-permute-done.18.refs_1_, bf16[16,80]{1,0:T(8,128)(2,1)S(1)} %collective-permute-done.19.refs_2_, bf16[32,80]{1,0:T(8,128)(2,1)S(1)} %collective-permute-done.20.refs_3_, ...), custom_call_target="tpu_custom_call" | custom-call | tf_op jit(solution)/shard_map/pallas_call | solution.py:62
  (44 shorter events, 6.6 us)
Async XLA Ops:
  0.6 3.3 %copy-start = (bf16[4,320,480]{2,1,0:T(8,128)(2,1)S(1)}, bf16[4,320,480]{2,1,0:T(8,128)(2,1)}, u32[]{:S(2)}) copy-start(bf16[4,320,480]{2,1,0:T(8,128)(2,1)} %param.8) | copy-start | bytes 3686404
  3.4 1.4 %collective-permute-start = (f32[64,166]{1,0:T(8,128)S(1)}, f32[64,166]{1,0:T(8,128)S(1)}, u32[]{:S(2)}, u32[]{:S(2)}) collective-permute-start(f32[64,166]{1,0:T(8,128)S(1)} %get-tuple-element.37.packet), channel_id=1, source_target_pairs={{0,1},{1,0},{2,3},{3,2},{4,5},{5,4},{6,7},{7,6},{8,9},{9,8},{10,11... | collective-permute-start | bytes 127496 | tf_op jit(solution)/shard_map/ppermute | solution.py:320
  4.8 9.9 %collective-permute-start.3 = (f32[16,160]{1,0:T(8,128)S(1)}, f32[16,160]{1,0:T(8,128)S(1)}, u32[]{:S(2)}, u32[]{:S(2)}) collective-permute-start(f32[16,160]{1,0:T(8,128)S(1)} %get-tuple-element.46), channel_id=1, source_target_pairs={{0,28},{1,31},{2,30},{3,29},{4,8},{5,11},{6,10},{7,9},{8,4},{9,7},... | collective-permute-start | bytes 30728 | tf_op jit(solution)/shard_map/ppermute | solution.py:326
  10.8 3.9 %collective-permute-start.2 = (f32[32,160]{1,0:T(8,128)S(1)}, f32[32,160]{1,0:T(8,128)S(1)}, u32[]{:S(2)}, u32[]{:S(2)}) collective-permute-start(f32[32,160]{1,0:T(8,128)S(1)} %get-tuple-element.45), channel_id=1, source_target_pairs={{0,4},{1,7},{2,6},{3,5},{4,0},{5,3},{6,2},{7,1},{8,12},{9,15},{10,... | collective-permute-start | bytes 61448 | tf_op jit(solution)/shard_map/ppermute | solution.py:327
  12.0 4.7 %collective-permute-start.5 = (bf16[4,480,480]{2,1,0:T(8,128)(2,1)S(1)}, bf16[4,480,480]{2,1,0:T(8,128)(2,1)S(1)}, u32[]{:S(2)}, u32[]{:S(2)}) collective-permute-start(bf16[4,480,480]{2,1,0:T(8,128)(2,1)S(1)} %convolution_convert_fusion.refs_6_.refs_9_), channel_id=1, source_target_pairs={{0,1},{1,0},{2,3},{3,2},{4,5},{5,4},{6,7},{7,6},{8,9},{9,8},{10,11... | collective-permute-start | bytes 5529608 | tf_op jit(solution)/shard_map/ppermute | solution.py:320
  13.1 3.5 %collective-permute-start.1 = (f32[64,120]{1,0:T(8,128)S(1)}, f32[64,120]{1,0:T(8,128)S(1)}, u32[]{:S(2)}, u32[]{:S(2)}) collective-permute-start(f32[64,120]{1,0:T(8,128)S(1)} %shard_map.88), channel_id=1, source_target_pairs={{0,3},{1,2},{2,1},{3,0},{4,7},{5,6},{6,5},{7,4},{8,11},{9,10},{10,... | collective-permute-start | bytes 92168 | tf_op jit(solution)/shard_map/ppermute | solution.py:329
  14.7 2.0 %collective-permute-start.4 = (f32[32,160]{1,0:T(8,128)S(1)}, f32[32,160]{1,0:T(8,128)S(1)}, u32[]{:S(2)}, u32[]{:S(2)}) collective-permute-start(f32[32,160]{1,0:T(8,128)S(1)} %pad_maximum_fusion), channel_id=1, source_target_pairs={{0,1},{1,0},{2,3},{3,2},{4,5},{5,4},{6,7},{7,6},{8,9},{9,8},{10,11... | collective-permute-start | bytes 61448 | tf_op jit(solution)/shard_map/ppermute | solution.py:320
  17.8 6.4 %collective-permute-start.8 = (bf16[32,80]{1,0:T(8,128)(2,1)S(1)}, bf16[32,80]{1,0:T(8,128)(2,1)S(1)}, u32[]{:S(2)}, u32[]{:S(2)}) collective-permute-start(bf16[32,80]{1,0:T(8,128)(2,1)S(1)} %get-tuple-element.54), channel_id=1, source_target_pairs={{0,28},{1,31},{2,30},{3,29},{4,8},{5,11},{6,10},{7,9},{8,4},{9,7},... | collective-permute-start | bytes 15368 | tf_op jit(solution)/shard_map/ppermute | solution.py:326
  19.8 4.5 %collective-permute-start.7 = (bf16[16,80]{1,0:T(8,128)(2,1)S(1)}, bf16[16,80]{1,0:T(8,128)(2,1)S(1)}, u32[]{:S(2)}, u32[]{:S(2)}) collective-permute-start(bf16[16,80]{1,0:T(8,128)(2,1)S(1)} %get-tuple-element.53), channel_id=1, source_target_pairs={{0,4},{1,7},{2,6},{3,5},{4,0},{5,3},{6,2},{7,1},{8,12},{9,15},{10,... | collective-permute-start | bytes 7688 | tf_op jit(solution)/shard_map/ppermute | solution.py:327
  19.8 4.6 %collective-permute-start.6 = (bf16[64,80]{1,0:T(8,128)(2,1)S(1)}, bf16[64,80]{1,0:T(8,128)(2,1)S(1)}, u32[]{:S(2)}, u32[]{:S(2)}) collective-permute-start(bf16[64,80]{1,0:T(8,128)(2,1)S(1)} %get-tuple-element.52), channel_id=1, source_target_pairs={{0,3},{1,2},{2,1},{3,0},{4,7},{5,6},{6,5},{7,4},{8,11},{9,10},{10,... | collective-permute-start | bytes 30728 | tf_op jit(solution)/shard_map/ppermute | solution.py:329
  24.2 1.2 %collective-permute-start.9 = (bf16[32,80]{1,0:T(8,128)(2,1)S(1)}, bf16[32,80]{1,0:T(8,128)(2,1)S(1)}, u32[]{:S(2)}, u32[]{:S(2)}) collective-permute-start(bf16[32,80]{1,0:T(8,128)(2,1)S(1)} %pad_maximum_fusion.1), channel_id=1, source_target_pairs={{0,1},{1,0},{2,3},{3,2},{4,5},{5,4},{6,7},{7,6},{8,9},{9,8},{10,11... | collective-permute-start | bytes 15368 | tf_op jit(solution)/shard_map/ppermute | solution.py:320
  26.5 6.4 %collective-permute-start.12 = (bf16[32,80]{1,0:T(8,128)(2,1)S(1)}, bf16[32,80]{1,0:T(8,128)(2,1)S(1)}, u32[]{:S(2)}, u32[]{:S(2)}) collective-permute-start(bf16[32,80]{1,0:T(8,128)(2,1)S(1)} %get-tuple-element.60), channel_id=1, source_target_pairs={{0,28},{1,31},{2,30},{3,29},{4,8},{5,11},{6,10},{7,9},{8,4},{9,7},... | collective-permute-start | bytes 15368 | tf_op jit(solution)/shard_map/ppermute | solution.py:326
  28.5 4.4 %collective-permute-start.11 = (bf16[16,80]{1,0:T(8,128)(2,1)S(1)}, bf16[16,80]{1,0:T(8,128)(2,1)S(1)}, u32[]{:S(2)}, u32[]{:S(2)}) collective-permute-start(bf16[16,80]{1,0:T(8,128)(2,1)S(1)} %get-tuple-element.59), channel_id=1, source_target_pairs={{0,4},{1,7},{2,6},{3,5},{4,0},{5,3},{6,2},{7,1},{8,12},{9,15},{10,... | collective-permute-start | bytes 7688 | tf_op jit(solution)/shard_map/ppermute | solution.py:327
  28.6 4.4 %collective-permute-start.10 = (bf16[64,80]{1,0:T(8,128)(2,1)S(1)}, bf16[64,80]{1,0:T(8,128)(2,1)S(1)}, u32[]{:S(2)}, u32[]{:S(2)}) collective-permute-start(bf16[64,80]{1,0:T(8,128)(2,1)S(1)} %get-tuple-element.58), channel_id=1, source_target_pairs={{0,3},{1,2},{2,1},{3,0},{4,7},{5,6},{6,5},{7,4},{8,11},{9,10},{10,... | collective-permute-start | bytes 30728 | tf_op jit(solution)/shard_map/ppermute | solution.py:329
  32.9 1.2 %collective-permute-start.13 = (bf16[32,80]{1,0:T(8,128)(2,1)S(1)}, bf16[32,80]{1,0:T(8,128)(2,1)S(1)}, u32[]{:S(2)}, u32[]{:S(2)}) collective-permute-start(bf16[32,80]{1,0:T(8,128)(2,1)S(1)} %pad_maximum_fusion.2), channel_id=1, source_target_pairs={{0,1},{1,0},{2,3},{3,2},{4,5},{5,4},{6,7},{7,6},{8,9},{9,8},{10,11... | collective-permute-start | bytes 15368 | tf_op jit(solution)/shard_map/ppermute | solution.py:320
  35.2 6.4 %collective-permute-start.16 = (bf16[32,80]{1,0:T(8,128)(2,1)S(1)}, bf16[32,80]{1,0:T(8,128)(2,1)S(1)}, u32[]{:S(2)}, u32[]{:S(2)}) collective-permute-start(bf16[32,80]{1,0:T(8,128)(2,1)S(1)} %get-tuple-element.64), channel_id=1, source_target_pairs={{0,28},{1,31},{2,30},{3,29},{4,8},{5,11},{6,10},{7,9},{8,4},{9,7},... | collective-permute-start | bytes 15368 | tf_op jit(solution)/shard_map/ppermute | solution.py:326
  37.3 4.3 %collective-permute-start.15 = (bf16[16,80]{1,0:T(8,128)(2,1)S(1)}, bf16[16,80]{1,0:T(8,128)(2,1)S(1)}, u32[]{:S(2)}, u32[]{:S(2)}) collective-permute-start(bf16[16,80]{1,0:T(8,128)(2,1)S(1)} %get-tuple-element.63), channel_id=1, source_target_pairs={{0,4},{1,7},{2,6},{3,5},{4,0},{5,3},{6,2},{7,1},{8,12},{9,15},{10,... | collective-permute-start | bytes 7688 | tf_op jit(solution)/shard_map/ppermute | solution.py:327
  37.3 4.3 %collective-permute-start.14 = (bf16[64,80]{1,0:T(8,128)(2,1)S(1)}, bf16[64,80]{1,0:T(8,128)(2,1)S(1)}, u32[]{:S(2)}, u32[]{:S(2)}) collective-permute-start(bf16[64,80]{1,0:T(8,128)(2,1)S(1)} %get-tuple-element.62), channel_id=1, source_target_pairs={{0,3},{1,2},{2,1},{3,0},{4,7},{5,6},{6,5},{7,4},{8,11},{9,10},{10,... | collective-permute-start | bytes 30728 | tf_op jit(solution)/shard_map/ppermute | solution.py:329
  41.6 1.2 %collective-permute-start.17 = (bf16[32,80]{1,0:T(8,128)(2,1)S(1)}, bf16[32,80]{1,0:T(8,128)(2,1)S(1)}, u32[]{:S(2)}, u32[]{:S(2)}) collective-permute-start(bf16[32,80]{1,0:T(8,128)(2,1)S(1)} %pad_maximum_fusion.3), channel_id=1, source_target_pairs={{0,1},{1,0},{2,3},{3,2},{4,5},{5,4},{6,7},{7,6},{8,9},{9,8},{10,11... | collective-permute-start | bytes 15368 | tf_op jit(solution)/shard_map/ppermute | solution.py:320
  43.8 6.4 %collective-permute-start.20 = (bf16[32,80]{1,0:T(8,128)(2,1)S(1)}, bf16[32,80]{1,0:T(8,128)(2,1)S(1)}, u32[]{:S(2)}, u32[]{:S(2)}) collective-permute-start(bf16[32,80]{1,0:T(8,128)(2,1)S(1)} %get-tuple-element.68), channel_id=1, source_target_pairs={{0,28},{1,31},{2,30},{3,29},{4,8},{5,11},{6,10},{7,9},{8,4},{9,7},... | collective-permute-start | bytes 15368 | tf_op jit(solution)/shard_map/ppermute | solution.py:326
  46.0 4.3 %collective-permute-start.19 = (bf16[16,80]{1,0:T(8,128)(2,1)S(1)}, bf16[16,80]{1,0:T(8,128)(2,1)S(1)}, u32[]{:S(2)}, u32[]{:S(2)}) collective-permute-start(bf16[16,80]{1,0:T(8,128)(2,1)S(1)} %get-tuple-element.67), channel_id=1, source_target_pairs={{0,4},{1,7},{2,6},{3,5},{4,0},{5,3},{6,2},{7,1},{8,12},{9,15},{10,... | collective-permute-start | bytes 7688 | tf_op jit(solution)/shard_map/ppermute | solution.py:327
  46.0 4.3 %collective-permute-start.18 = (bf16[64,80]{1,0:T(8,128)(2,1)S(1)}, bf16[64,80]{1,0:T(8,128)(2,1)S(1)}, u32[]{:S(2)}, u32[]{:S(2)}) collective-permute-start(bf16[64,80]{1,0:T(8,128)(2,1)S(1)} %get-tuple-element.66), channel_id=1, source_target_pairs={{0,3},{1,2},{2,1},{3,0},{4,7},{5,6},{6,5},{7,4},{8,11},{9,10},{10,... | collective-permute-start | bytes 30728 | tf_op jit(solution)/shard_map/ppermute | solution.py:329
  50.3 1.2 %collective-permute-start.21 = (bf16[32,80]{1,0:T(8,128)(2,1)S(1)}, bf16[32,80]{1,0:T(8,128)(2,1)S(1)}, u32[]{:S(2)}, u32[]{:S(2)}) collective-permute-start(bf16[32,80]{1,0:T(8,128)(2,1)S(1)} %pad_maximum_fusion.4), channel_id=1, source_target_pairs={{0,1},{1,0},{2,3},{3,2},{4,5},{5,4},{6,7},{7,6},{8,9},{9,8},{10,11... | collective-permute-start | bytes 15368 | tf_op jit(solution)/shard_map/ppermute | solution.py:320

commit v6 on v5

--- a/solution.py
+++ b/solution.py
@@ -8,6 +8,7 @@
 from jax.sharding import PartitionSpec as P
 
 SWEEPS = 5
+WAIT = pl.CostEstimate(flops=70 * 10**9, bytes_accessed=0, transcendentals=0)
 AXES = ("elem", "face")
 CORES = 2
 F32 = jnp.float32
@@ -117,8 +118,8 @@
 
 def load_kernel(dims, *refs):
     groups, elems, sides, width, group_faces, border = dims
-    sources, (local_ref, packet_ref, ids_ref, inverse, down) = refs[:6], refs[6:11]
-    residual, ids, residual_rows, stab_rows, sems = refs[11:]
+    sources, (local_ref, packet_ref, ids_ref, inverse, down, up) = refs[:7], refs[7:13]
+    residual, ids, residual_rows, stab_rows, sems = refs[13:]
     rows = group_faces + border
     lines = 2 * elems
 
@@ -128,16 +129,16 @@
         copy.start()
         return copy
 
-    inverse_hbm, down_hbm, residual_hbm, ids_hbm, residual_rows_hbm, stab_rows_hbm = range(6)
+    inverse_hbm, down_hbm, up_hbm, residual_hbm, ids_hbm, residual_rows_hbm, stab_rows_hbm = range(7)
     own_faces = residual_rows.shape[0]
     first = [fetch(residual_hbm, residual, 0, elems, 0), fetch(inverse_hbm, inverse, 0, elems, 1)]
-    half = elems // 1
-    pieces = [fetch(down_hbm, down, half * n, half, 2 + n) for n in range(1)]
+    down_copy = fetch(down_hbm, down, 0, elems, 2)
     small = [
-        fetch(ids_hbm, ids, 0, elems, 2 + 1),
-        fetch(residual_rows_hbm, residual_rows, 0, own_faces, 3 + 1),
-        fetch(stab_rows_hbm, stab_rows, 0, own_faces, 4 + 1),
+        fetch(ids_hbm, ids, 0, elems, 3),
+        fetch(residual_rows_hbm, residual_rows, 0, own_faces, 4),
+        fetch(stab_rows_hbm, stab_rows, 0, own_faces, 5),
     ]
+    up_copy = fetch(up_hbm, up, 0, elems, 6)
     for copy in first:
         copy.wait()
     source = residual[...].astype(F32)
@@ -155,13 +156,11 @@
     right = pltpu.roll(jnp.concatenate([residual_rows[...], blank], axis=0), place, 0)
     scale = pltpu.roll(jnp.concatenate([stab_rows[...], blank], axis=0), place, 0)
     packet_ref[:lines, 2 * width :] = ids_ref[...].astype(F32)
-    load = []
-    for n in range(1):
-        pieces[n].wait()
-        for e in range(half * n, half * (n + 1)):
-            load.append(contract(masked(local, e), down[e], 1, 0))
+    down_copy.wait()
+    load = [contract(masked(local, e), down[e], 1, 0) for e in range(elems)]
     sums = spread(spread_hits, to_rows(add_up(load), sides, width))
     packet_ref[:, : 2 * width] = jnp.concatenate([right - sums, scale], axis=1)
+    up_copy.wait()
 
 
 def join_kernel(border, width, packet, mate, sums_ref, first_ref, second_ref):
@@ -332,9 +331,9 @@
         return own, first, second, [mate]
 
     down = jnp.swapaxes(trace_from_vol, 1, 2)
-    large = (vol_inverse, down)
+    large = (vol_inverse, down, vol_from_trace)
     small = (vol_residual, face_ids, trace_residual, stabilization)
-    local_part, packet, ids, inverse, down = call(
+    local_part, packet, ids, inverse, down, up = call(
         functools.partial(load_kernel, dims),
         [
             ((2 * elems, volume), F32),
@@ -343,15 +342,15 @@
             *((array.shape, array.dtype) for array in large),
         ],
         *large, *small,
-        stay=6,
+        stay=7,
         scratch=[
             *(pltpu.VMEM(array.shape, array.dtype) for array in small),
-            pltpu.SemaphoreType.DMA((6,)),
+            pltpu.SemaphoreType.DMA((7,)),
         ],
     )
     mate = swap_core(packet)
     couple = jnp.einsum(
-        "evk,ekt->evt", inverse, vol_from_trace, preferred_element_type=F32
+        "evk,ekt->evt", inverse, up, preferred_element_type=F32
     ).astype(HALF)
     couple, mate = lax.optimization_barrier((couple, mate))
     chip_faces = CORES * own_faces
@@ -371,7 +370,7 @@
         functools.partial(hits_kernel, dims),
         [((slots, rows), HALF), ((rows, slots), HALF)],
         ids, mate,
-        cost=pl.CostEstimate(flops=70000000000, bytes_accessed=0, transcendentals=0),
+        cost=WAIT,
     )
 
     def counted(kernel, parts):

time: 52.9 us -> 52.8 us (level)
  no operation moved by 1% of the time
where the time goes in v6:
time: 52.8 us; the launch traced here: 52.6 us
  starting transfers between devices  21.7 us (41%)
  waiting for transfers between devices  19.5 us (37%)
  Pallas kernels  8.5 us (16%)
  matrix products  2.07 us (4%)
  between operations  0.8 us (2%)
    ppermute x5, starting transfers between devices, exchange(): lax.ppermute(to_second, AXES, partners(groups, chips, 1, s))  14.3 us
    ppermute x5, waiting for transfers between devices, exchange(): lax.ppermute(to_second, AXES, partners(groups, chips, 1, s))  13 us
    pallas_call x10, Pallas kernels, call(): pl.pallas_call(body, out_shape=outs, in_specs=[HBM] * stay + [VMEM] * (le...  8.5 us
    ppermute x5, starting transfers between devices, exchange(): lax.ppermute(sent, AXES, along_x(groups, chips, shift))  5.03 us
    ppermute x7, waiting for transfers between devices, swap_core(): return lax.ppermute(block, AXES, other_core(groups, chips))  4.62 us
    ppermute x7, starting transfers between devices, swap_core(): return lax.ppermute(block, AXES, other_core(groups, chips))  2.34 us
    dot_general x1, matrix products, local(): jnp.einsum('evs,evt->est', couple, down, preferred_element_type=F32)  1.22 us
  transfers between devices with their start and end apart: 22, of which 10 were waited for; matrix products, arithmetic and copies ran while one was open for 4% of the time, Pallas kernels for 1%

profile of v6, /device:TPU:0, one launch (start us, length us, event | category | flops | bytes accessed | tf_op | source)
XLA Modules:
  0.0 52.6 jit_solution(7040269800425710101)
XLA Ops:
  0.6 2.6 %shard_map.86 = (f32[8,320]{1,0:T(8,128)S(1)}, f32[64,166]{1,0:T(8,128)S(1)}, s32[8,6]{1,0:T(8,128)S(1)}, bf16[4,320,320]{2,1,0:T(8,128)(2,1)S(1)}, bf16[4,320,4...) custom-call(bf16[4,320,320]{2,1,0:T(8,128)(2,1)} %refs_0_.1, bf16[4,320,480]{2,1,0:T(8,128)(2,1)} %bitcast.5, ...), custom_call_target="tpu_custom_call" | custom-call | tf_op jit(solution)/shard_map/pallas_call | solution.py:63
  4.7 6.0 %collective-permute-start.3 = (f32[16,160]{1,0:T(8,128)S(1)}, f32[16,160]{1,0:T(8,128)S(1)}, u32[]{:S(2)}, u32[]{:S(2)}) collective-permute-start(f32[16,160]{1,0:T(8,128)S(1)} %get-tuple-element.48), channel_id=1, source_target_pairs={{0,28},{1,31},{2,30},{3,29},{4,8},{5,11},{6,10},{7,9},{8,4},{9,7},... | collective-permute-start | bytes 30728 | tf_op jit(solution)/shard_map/ppermute | solution.py:325
  10.7 1.2 %convolution_convert_fusion.refs_6_.refs_9_ = bf16[4,480,480]{2,1,0:T(8,128)(2,1)S(1)} fusion(bf16[4,320,480]{2,1,0:T(8,128)(2,1)S(1)} %convolution_convert_fusion.1.refs_8_, bf16[4,320,480]{2,1,0:T(8,128)(2,1)S(1)} %get-tuple-element.45), kind=kOutput, calls=%fused_computation | convolution fusion | flops 590745600 | bytes 4300800 | tf_op jit(solution)/shard_map/evs,evt->est/dot_general | solution.py:367
  15.5 1.0 %collective-permute-done.1.refs_0_ = f32[64,120]{1,0:T(8,128)S(1)} collective-permute-done((f32[64,120]{1,0:T(8,128)S(1)}, f32[64,120]{1,0:T(8,128)S(1)}, u32[]{:S(2)}, u32[]{:S(2)}) %collective-permute-start.1) | collective-permute-done | bytes 30752 | tf_op jit(solution)/shard_map/ppermute | solution.py:328
  16.6 1.1 %shard_map.91 = (f32[64,80]{1,0:T(8,128)S(1)}, f32[64,80]{1,0:T(8,128)S(1)}, f32[64,80]{1,0:T(8,128)S(1)}, bf16[64,80]{1,0:T(8,128)(2,1)S(1)}, bf16[16,80]{1,0:T(8,128)(2,1)S(1)}, /*index=5*/bf16[32,80]{1,0:T(8,128)(2,1)S(1)}) custom-call(f32[64,160]{1,0:T(8,128)S(1)} %shard_map.89.refs_0_, f32[32,160]{1,0:T(8,128)S(1)} %collective-permute-done.2.refs_1_, ...), custom_call_target="tpu_custom_call" | custom-call | tf_op jit(solution)/shard_map/pallas_call | solution.py:63
  17.7 1.9 %collective-permute-start.8 = (bf16[32,80]{1,0:T(8,128)(2,1)S(1)}, bf16[32,80]{1,0:T(8,128)(2,1)S(1)}, u32[]{:S(2)}, u32[]{:S(2)}) collective-permute-start(bf16[32,80]{1,0:T(8,128)(2,1)S(1)} %get-tuple-element.56), channel_id=1, source_target_pairs={{0,28},{1,31},{2,30},{3,29},{4,8},{5,11},{6,10},{7,9},{8,4},{9,7},... | collective-permute-start | bytes 15368 | tf_op jit(solution)/shard_map/ppermute | solution.py:325
  19.6 1.0 %collective-permute-start.6 = (bf16[64,80]{1,0:T(8,128)(2,1)S(1)}, bf16[64,80]{1,0:T(8,128)(2,1)S(1)}, u32[]{:S(2)}, u32[]{:S(2)}) collective-permute-start(bf16[64,80]{1,0:T(8,128)(2,1)S(1)} %get-tuple-element.54), channel_id=1, source_target_pairs={{0,3},{1,2},{2,1},{3,0},{4,7},{5,6},{6,5},{7,4},{8,11},{9,10},{10,... | collective-permute-start | bytes 30728 | tf_op jit(solution)/shard_map/ppermute | solution.py:328
  20.6 3.5 %collective-permute-done.8.refs_3_ = bf16[32,80]{1,0:T(8,128)(2,1)S(1)} collective-permute-done((bf16[32,80]{1,0:T(8,128)(2,1)S(1)}, bf16[32,80]{1,0:T(8,128)(2,1)S(1)}, u32[]{:S(2)}, u32[]{:S(2)}) %collective-permute-start.8) | collective-permute-done | bytes 5152 | tf_op jit(solution)/shard_map/ppermute | solution.py:325
  24.3 1.1 %collective-permute-done.9.refs_4_ = bf16[32,80]{1,0:T(8,128)(2,1)S(1)} collective-permute-done((bf16[32,80]{1,0:T(8,128)(2,1)S(1)}, bf16[32,80]{1,0:T(8,128)(2,1)S(1)}, u32[]{:S(2)}, u32[]{:S(2)}) %collective-permute-start.9) | collective-permute-done | bytes 5152 | tf_op jit(solution)/shard_map/ppermute | solution.py:319
  25.4 1.0 %shard_map.92 = (f32[64,80]{1,0:T(8,128)S(1)}, bf16[64,80]{1,0:T(8,128)(2,1)S(1)}, bf16[16,80]{1,0:T(8,128)(2,1)S(1)}, bf16[32,80]{1,0:T(8,128)(2,1)S(1)}) custom-call(f32[64,80]{1,0:T(8,128)S(1)} %get-tuple-element.53.refs_0_, bf16[64,80]{1,0:T(8,128)(2,1)S(1)} %collective-permute-done.6.refs_1_, bf16[16,80]{1,0:T(8,128)(2,1)S(1)} %collective-permute-done.7.refs_2_, ...), custom_call_target="tpu_custom_call" | custom-call | tf_op jit(solution)/shard_map/pallas_call | solution.py:63
  26.4 2.1 %collective-permute-start.12 = (bf16[32,80]{1,0:T(8,128)(2,1)S(1)}, bf16[32,80]{1,0:T(8,128)(2,1)S(1)}, u32[]{:S(2)}, u32[]{:S(2)}) collective-permute-start(bf16[32,80]{1,0:T(8,128)(2,1)S(1)} %get-tuple-element.62), channel_id=1, source_target_pairs={{0,28},{1,31},{2,30},{3,29},{4,8},{5,11},{6,10},{7,9},{8,4},{9,7},... | collective-permute-start | bytes 15368 | tf_op jit(solution)/shard_map/ppermute | solution.py:325
  28.5 1.4 %collective-permute-start.10 = (bf16[64,80]{1,0:T(8,128)(2,1)S(1)}, bf16[64,80]{1,0:T(8,128)(2,1)S(1)}, u32[]{:S(2)}, u32[]{:S(2)}) collective-permute-start(bf16[64,80]{1,0:T(8,128)(2,1)S(1)} %get-tuple-element.60), channel_id=1, source_target_pairs={{0,3},{1,2},{2,1},{3,0},{4,7},{5,6},{6,5},{7,4},{8,11},{9,10},{10,... | collective-permute-start | bytes 30728 | tf_op jit(solution)/shard_map/ppermute | solution.py:328
  29.9 2.9 %collective-permute-done.12.refs_3_ = bf16[32,80]{1,0:T(8,128)(2,1)S(1)} collective-permute-done((bf16[32,80]{1,0:T(8,128)(2,1)S(1)}, bf16[32,80]{1,0:T(8,128)(2,1)S(1)}, u32[]{:S(2)}, u32[]{:S(2)}) %collective-permute-start.12) | collective-permute-done | bytes 5152 | tf_op jit(solution)/shard_map/ppermute | solution.py:325
  32.9 1.1 %collective-permute-done.13.refs_4_ = bf16[32,80]{1,0:T(8,128)(2,1)S(1)} collective-permute-done((bf16[32,80]{1,0:T(8,128)(2,1)S(1)}, bf16[32,80]{1,0:T(8,128)(2,1)S(1)}, u32[]{:S(2)}, u32[]{:S(2)}) %collective-permute-start.13) | collective-permute-done | bytes 5152 | tf_op jit(solution)/shard_map/ppermute | solution.py:319
  34.0 1.0 %shard_map.93 = (f32[64,80]{1,0:T(8,128)S(1)}, bf16[64,80]{1,0:T(8,128)(2,1)S(1)}, bf16[16,80]{1,0:T(8,128)(2,1)S(1)}, bf16[32,80]{1,0:T(8,128)(2,1)S(1)}) custom-call(f32[64,80]{1,0:T(8,128)S(1)} %get-tuple-element.59.refs_0_, bf16[64,80]{1,0:T(8,128)(2,1)S(1)} %collective-permute-done.10.refs_1_, bf16[16,80]{1,0:T(8,128)(2,1)S(1)} %collective-permute-done.11.refs_2_, ...), custom_call_target="tpu_custom_call" | custom-call | tf_op jit(solution)/shard_map/pallas_call | solution.py:63
  35.1 2.2 %collective-permute-start.16 = (bf16[32,80]{1,0:T(8,128)(2,1)S(1)}, bf16[32,80]{1,0:T(8,128)(2,1)S(1)}, u32[]{:S(2)}, u32[]{:S(2)}) collective-permute-start(bf16[32,80]{1,0:T(8,128)(2,1)S(1)} %get-tuple-element.66), channel_id=1, source_target_pairs={{0,28},{1,31},{2,30},{3,29},{4,8},{5,11},{6,10},{7,9},{8,4},{9,7},... | collective-permute-start | bytes 15368 | tf_op jit(solution)/shard_map/ppermute | solution.py:325
  37.2 1.0 %collective-permute-start.14 = (bf16[64,80]{1,0:T(8,128)(2,1)S(1)}, bf16[64,80]{1,0:T(8,128)(2,1)S(1)}, u32[]{:S(2)}, u32[]{:S(2)}) collective-permute-start(bf16[64,80]{1,0:T(8,128)(2,1)S(1)} %get-tuple-element.64), channel_id=1, source_target_pairs={{0,3},{1,2},{2,1},{3,0},{4,7},{5,6},{6,5},{7,4},{8,11},{9,10},{10,... | collective-permute-start | bytes 30728 | tf_op jit(solution)/shard_map/ppermute | solution.py:328
  38.2 3.3 %collective-permute-done.16.refs_3_ = bf16[32,80]{1,0:T(8,128)(2,1)S(1)} collective-permute-done((bf16[32,80]{1,0:T(8,128)(2,1)S(1)}, bf16[32,80]{1,0:T(8,128)(2,1)S(1)}, u32[]{:S(2)}, u32[]{:S(2)}) %collective-permute-start.16) | collective-permute-done | bytes 5152 | tf_op jit(solution)/shard_map/ppermute | solution.py:325
  41.6 1.1 %collective-permute-done.17.refs_4_ = bf16[32,80]{1,0:T(8,128)(2,1)S(1)} collective-permute-done((bf16[32,80]{1,0:T(8,128)(2,1)S(1)}, bf16[32,80]{1,0:T(8,128)(2,1)S(1)}, u32[]{:S(2)}, u32[]{:S(2)}) %collective-permute-start.17) | collective-permute-done | bytes 5152 | tf_op jit(solution)/shard_map/ppermute | solution.py:319
  42.7 1.0 %shard_map.94 = (f32[64,80]{1,0:T(8,128)S(1)}, bf16[64,80]{1,0:T(8,128)(2,1)S(1)}, bf16[16,80]{1,0:T(8,128)(2,1)S(1)}, bf16[32,80]{1,0:T(8,128)(2,1)S(1)}) custom-call(f32[64,80]{1,0:T(8,128)S(1)} %get-tuple-element.63.refs_0_, bf16[64,80]{1,0:T(8,128)(2,1)S(1)} %collective-permute-done.14.refs_1_, bf16[16,80]{1,0:T(8,128)(2,1)S(1)} %collective-permute-done.15.refs_2_, ...), custom_call_target="tpu_custom_call" | custom-call | tf_op jit(solution)/shard_map/pallas_call | solution.py:63
  43.7 2.2 %collective-permute-start.20 = (bf16[32,80]{1,0:T(8,128)(2,1)S(1)}, bf16[32,80]{1,0:T(8,128)(2,1)S(1)}, u32[]{:S(2)}, u32[]{:S(2)}) collective-permute-start(bf16[32,80]{1,0:T(8,128)(2,1)S(1)} %get-tuple-element.70), channel_id=1, source_target_pairs={{0,28},{1,31},{2,30},{3,29},{4,8},{5,11},{6,10},{7,9},{8,4},{9,7},... | collective-permute-start | bytes 15368 | tf_op jit(solution)/shard_map/ppermute | solution.py:325
  46.8 3.3 %collective-permute-done.20.refs_3_ = bf16[32,80]{1,0:T(8,128)(2,1)S(1)} collective-permute-done((bf16[32,80]{1,0:T(8,128)(2,1)S(1)}, bf16[32,80]{1,0:T(8,128)(2,1)S(1)}, u32[]{:S(2)}, u32[]{:S(2)}) %collective-permute-start.20) | collective-permute-done | bytes 5152 | tf_op jit(solution)/shard_map/ppermute | solution.py:325
  50.2 1.1 %collective-permute-done.21.refs_4_ = bf16[32,80]{1,0:T(8,128)(2,1)S(1)} collective-permute-done((bf16[32,80]{1,0:T(8,128)(2,1)S(1)}, bf16[32,80]{1,0:T(8,128)(2,1)S(1)}, u32[]{:S(2)}, u32[]{:S(2)}) %collective-permute-start.21) | collective-permute-done | bytes 5152 | tf_op jit(solution)/shard_map/ppermute | solution.py:319
  51.4 1.2 %shard_map.95 = (f32[12,80]{1,0:T(8,128)}, f32[4,320]{1,0:T(4,128)}) custom-call(f32[64,80]{1,0:T(8,128)S(1)} %get-tuple-element.67.refs_0_, bf16[64,80]{1,0:T(8,128)(2,1)S(1)} %collective-permute-done.18.refs_1_, bf16[16,80]{1,0:T(8,128)(2,1)S(1)} %collective-permute-done.19.refs_2_, bf16[32,80]{1,0:T(8,128)(2,1)S(1)} %collective-permute-done.20.refs_3_, ...), custom_call_target="tpu_custom_call" | custom-call | tf_op jit(solution)/shard_map/pallas_call | solution.py:63
  (42 shorter events, 6.5 us)
Async XLA Ops:
  3.3 1.4 %collective-permute-start = (f32[64,166]{1,0:T(8,128)S(1)}, f32[64,166]{1,0:T(8,128)S(1)}, u32[]{:S(2)}, u32[]{:S(2)}) collective-permute-start(f32[64,166]{1,0:T(8,128)S(1)} %get-tuple-element.39.packet), channel_id=1, source_target_pairs={{0,1},{1,0},{2,3},{3,2},{4,5},{5,4},{6,7},{7,6},{8,9},{9,8},{10,11... | collective-permute-start | bytes 127496 | tf_op jit(solution)/shard_map/ppermute | solution.py:319
  4.7 9.9 %collective-permute-start.3 = (f32[16,160]{1,0:T(8,128)S(1)}, f32[16,160]{1,0:T(8,128)S(1)}, u32[]{:S(2)}, u32[]{:S(2)}) collective-permute-start(f32[16,160]{1,0:T(8,128)S(1)} %get-tuple-element.48), channel_id=1, source_target_pairs={{0,28},{1,31},{2,30},{3,29},{4,8},{5,11},{6,10},{7,9},{8,4},{9,7},... | collective-permute-start | bytes 30728 | tf_op jit(solution)/shard_map/ppermute | solution.py:325
  10.7 3.9 %collective-permute-start.2 = (f32[32,160]{1,0:T(8,128)S(1)}, f32[32,160]{1,0:T(8,128)S(1)}, u32[]{:S(2)}, u32[]{:S(2)}) collective-permute-start(f32[32,160]{1,0:T(8,128)S(1)} %get-tuple-element.47), channel_id=1, source_target_pairs={{0,4},{1,7},{2,6},{3,5},{4,0},{5,3},{6,2},{7,1},{8,12},{9,15},{10,... | collective-permute-start | bytes 61448 | tf_op jit(solution)/shard_map/ppermute | solution.py:326
  11.9 4.7 %collective-permute-start.5 = (bf16[4,480,480]{2,1,0:T(8,128)(2,1)S(1)}, bf16[4,480,480]{2,1,0:T(8,128)(2,1)S(1)}, u32[]{:S(2)}, u32[]{:S(2)}) collective-permute-start(bf16[4,480,480]{2,1,0:T(8,128)(2,1)S(1)} %convolution_convert_fusion.refs_6_.refs_9_), channel_id=1, source_target_pairs={{0,1},{1,0},{2,3},{3,2},{4,5},{5,4},{6,7},{7,6},{8,9},{9,8},{10,11... | collective-permute-start | bytes 5529608 | tf_op jit(solution)/shard_map/ppermute | solution.py:319
  13.0 3.5 %collective-permute-start.1 = (f32[64,120]{1,0:T(8,128)S(1)}, f32[64,120]{1,0:T(8,128)S(1)}, u32[]{:S(2)}, u32[]{:S(2)}) collective-permute-start(f32[64,120]{1,0:T(8,128)S(1)} %shard_map.88), channel_id=1, source_target_pairs={{0,3},{1,2},{2,1},{3,0},{4,7},{5,6},{6,5},{7,4},{8,11},{9,10},{10,... | collective-permute-start | bytes 92168 | tf_op jit(solution)/shard_map/ppermute | solution.py:328
  14.6 2.0 %collective-permute-start.4 = (f32[32,160]{1,0:T(8,128)S(1)}, f32[32,160]{1,0:T(8,128)S(1)}, u32[]{:S(2)}, u32[]{:S(2)}) collective-permute-start(f32[32,160]{1,0:T(8,128)S(1)} %pad_maximum_fusion), channel_id=1, source_target_pairs={{0,1},{1,0},{2,3},{3,2},{4,5},{5,4},{6,7},{7,6},{8,9},{9,8},{10,11... | collective-permute-start | bytes 61448 | tf_op jit(solution)/shard_map/ppermute | solution.py:319
  17.7 6.4 %collective-permute-start.8 = (bf16[32,80]{1,0:T(8,128)(2,1)S(1)}, bf16[32,80]{1,0:T(8,128)(2,1)S(1)}, u32[]{:S(2)}, u32[]{:S(2)}) collective-permute-start(bf16[32,80]{1,0:T(8,128)(2,1)S(1)} %get-tuple-element.56), channel_id=1, source_target_pairs={{0,28},{1,31},{2,30},{3,29},{4,8},{5,11},{6,10},{7,9},{8,4},{9,7},... | collective-permute-start | bytes 15368 | tf_op jit(solution)/shard_map/ppermute | solution.py:325
  19.6 4.5 %collective-permute-start.7 = (bf16[16,80]{1,0:T(8,128)(2,1)S(1)}, bf16[16,80]{1,0:T(8,128)(2,1)S(1)}, u32[]{:S(2)}, u32[]{:S(2)}) collective-permute-start(bf16[16,80]{1,0:T(8,128)(2,1)S(1)} %get-tuple-element.55), channel_id=1, source_target_pairs={{0,4},{1,7},{2,6},{3,5},{4,0},{5,3},{6,2},{7,1},{8,12},{9,15},{10,... | collective-permute-start | bytes 7688 | tf_op jit(solution)/shard_map/ppermute | solution.py:326
  19.6 4.6 %collective-permute-start.6 = (bf16[64,80]{1,0:T(8,128)(2,1)S(1)}, bf16[64,80]{1,0:T(8,128)(2,1)S(1)}, u32[]{:S(2)}, u32[]{:S(2)}) collective-permute-start(bf16[64,80]{1,0:T(8,128)(2,1)S(1)} %get-tuple-element.54), channel_id=1, source_target_pairs={{0,3},{1,2},{2,1},{3,0},{4,7},{5,6},{6,5},{7,4},{8,11},{9,10},{10,... | collective-permute-start | bytes 30728 | tf_op jit(solution)/shard_map/ppermute | solution.py:328
  24.1 1.2 %collective-permute-start.9 = (bf16[32,80]{1,0:T(8,128)(2,1)S(1)}, bf16[32,80]{1,0:T(8,128)(2,1)S(1)}, u32[]{:S(2)}, u32[]{:S(2)}) collective-permute-start(bf16[32,80]{1,0:T(8,128)(2,1)S(1)} %pad_maximum_fusion.1), channel_id=1, source_target_pairs={{0,1},{1,0},{2,3},{3,2},{4,5},{5,4},{6,7},{7,6},{8,9},{9,8},{10,11... | collective-permute-start | bytes 15368 | tf_op jit(solution)/shard_map/ppermute | solution.py:319
  26.4 6.4 %collective-permute-start.12 = (bf16[32,80]{1,0:T(8,128)(2,1)S(1)}, bf16[32,80]{1,0:T(8,128)(2,1)S(1)}, u32[]{:S(2)}, u32[]{:S(2)}) collective-permute-start(bf16[32,80]{1,0:T(8,128)(2,1)S(1)} %get-tuple-element.62), channel_id=1, source_target_pairs={{0,28},{1,31},{2,30},{3,29},{4,8},{5,11},{6,10},{7,9},{8,4},{9,7},... | collective-permute-start | bytes 15368 | tf_op jit(solution)/shard_map/ppermute | solution.py:325
  28.4 4.4 %collective-permute-start.11 = (bf16[16,80]{1,0:T(8,128)(2,1)S(1)}, bf16[16,80]{1,0:T(8,128)(2,1)S(1)}, u32[]{:S(2)}, u32[]{:S(2)}) collective-permute-start(bf16[16,80]{1,0:T(8,128)(2,1)S(1)} %get-tuple-element.61), channel_id=1, source_target_pairs={{0,4},{1,7},{2,6},{3,5},{4,0},{5,3},{6,2},{7,1},{8,12},{9,15},{10,... | collective-permute-start | bytes 7688 | tf_op jit(solution)/shard_map/ppermute | solution.py:326
  28.5 4.4 %collective-permute-start.10 = (bf16[64,80]{1,0:T(8,128)(2,1)S(1)}, bf16[64,80]{1,0:T(8,128)(2,1)S(1)}, u32[]{:S(2)}, u32[]{:S(2)}) collective-permute-start(bf16[64,80]{1,0:T(8,128)(2,1)S(1)} %get-tuple-element.60), channel_id=1, source_target_pairs={{0,3},{1,2},{2,1},{3,0},{4,7},{5,6},{6,5},{7,4},{8,11},{9,10},{10,... | collective-permute-start | bytes 30728 | tf_op jit(solution)/shard_map/ppermute | solution.py:328
  32.8 1.2 %collective-permute-start.13 = (bf16[32,80]{1,0:T(8,128)(2,1)S(1)}, bf16[32,80]{1,0:T(8,128)(2,1)S(1)}, u32[]{:S(2)}, u32[]{:S(2)}) collective-permute-start(bf16[32,80]{1,0:T(8,128)(2,1)S(1)} %pad_maximum_fusion.2), channel_id=1, source_target_pairs={{0,1},{1,0},{2,3},{3,2},{4,5},{5,4},{6,7},{7,6},{8,9},{9,8},{10,11... | collective-permute-start | bytes 15368 | tf_op jit(solution)/shard_map/ppermute | solution.py:319
  35.1 6.4 %collective-permute-start.16 = (bf16[32,80]{1,0:T(8,128)(2,1)S(1)}, bf16[32,80]{1,0:T(8,128)(2,1)S(1)}, u32[]{:S(2)}, u32[]{:S(2)}) collective-permute-start(bf16[32,80]{1,0:T(8,128)(2,1)S(1)} %get-tuple-element.66), channel_id=1, source_target_pairs={{0,28},{1,31},{2,30},{3,29},{4,8},{5,11},{6,10},{7,9},{8,4},{9,7},... | collective-permute-start | bytes 15368 | tf_op jit(solution)/shard_map/ppermute | solution.py:325
  37.2 4.3 %collective-permute-start.15 = (bf16[16,80]{1,0:T(8,128)(2,1)S(1)}, bf16[16,80]{1,0:T(8,128)(2,1)S(1)}, u32[]{:S(2)}, u32[]{:S(2)}) collective-permute-start(bf16[16,80]{1,0:T(8,128)(2,1)S(1)} %get-tuple-element.65), channel_id=1, source_target_pairs={{0,4},{1,7},{2,6},{3,5},{4,0},{5,3},{6,2},{7,1},{8,12},{9,15},{10,... | collective-permute-start | bytes 7688 | tf_op jit(solution)/shard_map/ppermute | solution.py:326
  37.2 4.3 %collective-permute-start.14 = (bf16[64,80]{1,0:T(8,128)(2,1)S(1)}, bf16[64,80]{1,0:T(8,128)(2,1)S(1)}, u32[]{:S(2)}, u32[]{:S(2)}) collective-permute-start(bf16[64,80]{1,0:T(8,128)(2,1)S(1)} %get-tuple-element.64), channel_id=1, source_target_pairs={{0,3},{1,2},{2,1},{3,0},{4,7},{5,6},{6,5},{7,4},{8,11},{9,10},{10,... | collective-permute-start | bytes 30728 | tf_op jit(solution)/shard_map/ppermute | solution.py:328
  41.5 1.2 %collective-permute-start.17 = (bf16[32,80]{1,0:T(8,128)(2,1)S(1)}, bf16[32,80]{1,0:T(8,128)(2,1)S(1)}, u32[]{:S(2)}, u32[]{:S(2)}) collective-permute-start(bf16[32,80]{1,0:T(8,128)(2,1)S(1)} %pad_maximum_fusion.3), channel_id=1, source_target_pairs={{0,1},{1,0},{2,3},{3,2},{4,5},{5,4},{6,7},{7,6},{8,9},{9,8},{10,11... | collective-permute-start | bytes 15368 | tf_op jit(solution)/shard_map/ppermute | solution.py:319
  43.7 6.4 %collective-permute-start.20 = (bf16[32,80]{1,0:T(8,128)(2,1)S(1)}, bf16[32,80]{1,0:T(8,128)(2,1)S(1)}, u32[]{:S(2)}, u32[]{:S(2)}) collective-permute-start(bf16[32,80]{1,0:T(8,128)(2,1)S(1)} %get-tuple-element.70), channel_id=1, source_target_pairs={{0,28},{1,31},{2,30},{3,29},{4,8},{5,11},{6,10},{7,9},{8,4},{9,7},... | collective-permute-start | bytes 15368 | tf_op jit(solution)/shard_map/ppermute | solution.py:325
  45.9 4.3 %collective-permute-start.19 = (bf16[16,80]{1,0:T(8,128)(2,1)S(1)}, bf16[16,80]{1,0:T(8,128)(2,1)S(1)}, u32[]{:S(2)}, u32[]{:S(2)}) collective-permute-start(bf16[16,80]{1,0:T(8,128)(2,1)S(1)} %get-tuple-element.69), channel_id=1, source_target_pairs={{0,4},{1,7},{2,6},{3,5},{4,0},{5,3},{6,2},{7,1},{8,12},{9,15},{10,... | collective-permute-start | bytes 7688 | tf_op jit(solution)/shard_map/ppermute | solution.py:326
  45.9 4.3 %collective-permute-start.18 = (bf16[64,80]{1,0:T(8,128)(2,1)S(1)}, bf16[64,80]{1,0:T(8,128)(2,1)S(1)}, u32[]{:S(2)}, u32[]{:S(2)}) collective-permute-start(bf16[64,80]{1,0:T(8,128)(2,1)S(1)} %get-tuple-element.68), channel_id=1, source_target_pairs={{0,3},{1,2},{2,1},{3,0},{4,7},{5,6},{6,5},{7,4},{8,11},{9,10},{10,... | collective-permute-start | bytes 30728 | tf_op jit(solution)/shard_map/ppermute | solution.py:328
  50.1 1.2 %collective-permute-start.21 = (bf16[32,80]{1,0:T(8,128)(2,1)S(1)}, bf16[32,80]{1,0:T(8,128)(2,1)S(1)}, u32[]{:S(2)}, u32[]{:S(2)}) collective-permute-start(bf16[32,80]{1,0:T(8,128)(2,1)S(1)} %pad_maximum_fusion.4), channel_id=1, source_target_pairs={{0,1},{1,0},{2,3},{3,2},{4,5},{5,4},{6,7},{7,6},{8,9},{9,8},{10,11... | collective-permute-start | bytes 15368 | tf_op jit(solution)/shard_map/ppermute | solution.py:319

commit v7 on v6

--- a/solution.py
+++ b/solution.py
@@ -268,6 +268,11 @@
     deal(sums, border, first_ref, second_ref)
 
 
+def turn_kernel(couple, after, turned_ref):
+    for e in range(couple.shape[0]):
+        turned_ref[e] = couple[e].T
+
+
 def last_kernel(counts, border, sides, *refs):
     parts, rest = split(counts, refs)
     right, scale, hits, couple, local, trace_ref, vol_ref = rest
@@ -281,7 +286,7 @@
     lam = to_lanes(picked, 2 * elems, sides)
     value = local[...]
     for e in range(elems):
-        value = value - contract(masked(lam, e), couple[e], 1, 1)
+        value = value - contract(masked(lam, e), couple[e], 1, 0)
     vol_ref[...] = value[:elems]
 
 
@@ -399,6 +404,10 @@
         [((rows, width), F32)] * 2 + dealt,
         *flat(parts), hits, spread_hits, schur_own, schur_mate,
     )
+    (turned,) = call(
+        turn_kernel, [((elems, trace, volume), HALF)], couple, right,
+        cost=pl.CostEstimate(flops=10**9, bytes_accessed=0, transcendentals=0),
+    )
     for _ in range(SWEEPS - 2):
         parts = exchange(*out)
         out = call(
@@ -409,7 +418,7 @@
     trace_update, vol_update = call(
         counted(last_kernel, parts),
         [((own_faces, width), F32), ((elems, volume), F32)],
-        *flat(parts), right, scale, hits, couple, local_part,
+        *flat(parts), right, scale, hits, turned, local_part,
     )
     return trace_update, vol_update
 

time: 52.8 us -> 52.7 us (level)
    pallas_call x10 -> x11, Pallas kernels: 8.5 us -> 8.84 us  [call(): pl.pallas_call(body, out_shape=outs, in_specs=[HBM] * stay + [VMEM] * (le...]
  transfers between devices with their start and end apart: 22 -> 22, of which waited for: 10 -> 10; matrix products, arithmetic and copies ran while one was open for 4% -> 4% of each run, Pallas kernels for 1% -> 2%
where the time goes in v7:
time: 52.7 us; the launch traced here: 52.5 us
  starting transfers between devices  21.7 us (41%)
  waiting for transfers between devices  19 us (36%)
  Pallas kernels  8.84 us (17%)
  matrix products  2.07 us (4%)
  between operations  0.81 us (2%)
    ppermute x5, starting transfers between devices, exchange(): lax.ppermute(to_second, AXES, partners(groups, chips, 1, s))  14.3 us
    ppermute x5, waiting for transfers between devices, exchange(): lax.ppermute(to_second, AXES, partners(groups, chips, 1, s))  13 us
    pallas_call x11, Pallas kernels, call(): pl.pallas_call(body, out_shape=outs, in_specs=[HBM] * stay + [VMEM] * (le...  8.84 us
    ppermute x5, starting transfers between devices, exchange(): lax.ppermute(sent, AXES, along_x(groups, chips, shift))  5.03 us
    ppermute x7, waiting for transfers between devices, swap_core(): return lax.ppermute(block, AXES, other_core(groups, chips))  4.16 us
    ppermute x7, starting transfers between devices, swap_core(): return lax.ppermute(block, AXES, other_core(groups, chips))  2.34 us
    dot_general x1, matrix products, local(): jnp.einsum('evs,evt->est', couple, down, preferred_element_type=F32)  1.22 us
  transfers between devices with their start and end apart: 22, of which 10 were waited for; matrix products, arithmetic and copies ran while one was open for 4% of the time, Pallas kernels for 2%

profile of v7, /device:TPU:0, one launch (start us, length us, event | category | flops | bytes accessed | tf_op | source)
XLA Modules:
  0.0 52.5 jit_solution(18419196929206391867)
XLA Ops:
  0.6 2.6 %shard_map.86 = (f32[8,320]{1,0:T(8,128)S(1)}, f32[64,166]{1,0:T(8,128)S(1)}, s32[8,6]{1,0:T(8,128)S(1)}, bf16[4,320,320]{2,1,0:T(8,128)(2,1)S(1)}, bf16[4,320,4...) custom-call(bf16[4,320,320]{2,1,0:T(8,128)(2,1)} %refs_0_.1, bf16[4,320,480]{2,1,0:T(8,128)(2,1)} %bitcast.5, ...), custom_call_target="tpu_custom_call" | custom-call | tf_op jit(solution)/shard_map/pallas_call | solution.py:63
  4.7 6.0 %collective-permute-start.3 = (f32[16,160]{1,0:T(8,128)S(1)}, f32[16,160]{1,0:T(8,128)S(1)}, u32[]{:S(2)}, u32[]{:S(2)}) collective-permute-start(f32[16,160]{1,0:T(8,128)S(1)} %get-tuple-element.48), channel_id=1, source_target_pairs={{0,28},{1,31},{2,30},{3,29},{4,8},{5,11},{6,10},{7,9},{8,4},{9,7},... | collective-permute-start | bytes 30728 | tf_op jit(solution)/shard_map/ppermute | solution.py:330
  10.7 1.2 %convolution_convert_fusion.refs_6_.refs_9_ = bf16[4,480,480]{2,1,0:T(8,128)(2,1)S(1)} fusion(bf16[4,320,480]{2,1,0:T(8,128)(2,1)S(1)} %convolution_convert_fusion.1.couple, bf16[4,320,480]{2,1,0:T(8,128)(2,1)S(1)} %get-tuple-element.45), kind=kOutput, calls=%fused_computation | convolution fusion | flops 590745600 | bytes 4300800 | tf_op jit(solution)/shard_map/evs,evt->est/dot_general | solution.py:372
  15.5 1.0 %collective-permute-done.1.refs_0_ = f32[64,120]{1,0:T(8,128)S(1)} collective-permute-done((f32[64,120]{1,0:T(8,128)S(1)}, f32[64,120]{1,0:T(8,128)S(1)}, u32[]{:S(2)}, u32[]{:S(2)}) %collective-permute-start.1) | collective-permute-done | bytes 30752 | tf_op jit(solution)/shard_map/ppermute | solution.py:333
  16.6 1.1 %shard_map.91 = (f32[64,80]{1,0:T(8,128)S(1)}, f32[64,80]{1,0:T(8,128)S(1)}, f32[64,80]{1,0:T(8,128)S(1)}, bf16[64,80]{1,0:T(8,128)(2,1)S(1)}, bf16[16,80]{1,0:T(8,128)(2,1)S(1)}, /*index=5*/bf16[32,80]{1,0:T(8,128)(2,1)S(1)}) custom-call(f32[64,160]{1,0:T(8,128)S(1)} %shard_map.89.refs_0_, f32[32,160]{1,0:T(8,128)S(1)} %collective-permute-done.2.refs_1_, ...), custom_call_target="tpu_custom_call" | custom-call | tf_op jit(solution)/shard_map/pallas_call | solution.py:63
  17.7 1.9 %collective-permute-start.8 = (bf16[32,80]{1,0:T(8,128)(2,1)S(1)}, bf16[32,80]{1,0:T(8,128)(2,1)S(1)}, u32[]{:S(2)}, u32[]{:S(2)}) collective-permute-start(bf16[32,80]{1,0:T(8,128)(2,1)S(1)} %get-tuple-element.56), channel_id=1, source_target_pairs={{0,28},{1,31},{2,30},{3,29},{4,8},{5,11},{6,10},{7,9},{8,4},{9,7},... | collective-permute-start | bytes 15368 | tf_op jit(solution)/shard_map/ppermute | solution.py:330
  19.6 1.0 %collective-permute-start.6 = (bf16[64,80]{1,0:T(8,128)(2,1)S(1)}, bf16[64,80]{1,0:T(8,128)(2,1)S(1)}, u32[]{:S(2)}, u32[]{:S(2)}) collective-permute-start(bf16[64,80]{1,0:T(8,128)(2,1)S(1)} %get-tuple-element.54), channel_id=1, source_target_pairs={{0,3},{1,2},{2,1},{3,0},{4,7},{5,6},{6,5},{7,4},{8,11},{9,10},{10,... | collective-permute-start | bytes 30728 | tf_op jit(solution)/shard_map/ppermute | solution.py:333
  20.6 3.5 %collective-permute-done.8.refs_3_ = bf16[32,80]{1,0:T(8,128)(2,1)S(1)} collective-permute-done((bf16[32,80]{1,0:T(8,128)(2,1)S(1)}, bf16[32,80]{1,0:T(8,128)(2,1)S(1)}, u32[]{:S(2)}, u32[]{:S(2)}) %collective-permute-start.8) | collective-permute-done | bytes 5152 | tf_op jit(solution)/shard_map/ppermute | solution.py:330
  24.3 1.1 %collective-permute-done.9.refs_4_ = bf16[32,80]{1,0:T(8,128)(2,1)S(1)} collective-permute-done((bf16[32,80]{1,0:T(8,128)(2,1)S(1)}, bf16[32,80]{1,0:T(8,128)(2,1)S(1)}, u32[]{:S(2)}, u32[]{:S(2)}) %collective-permute-start.9) | collective-permute-done | bytes 5152 | tf_op jit(solution)/shard_map/ppermute | solution.py:324
  25.4 1.0 %shard_map.92 = (f32[64,80]{1,0:T(8,128)S(1)}, bf16[64,80]{1,0:T(8,128)(2,1)S(1)}, bf16[16,80]{1,0:T(8,128)(2,1)S(1)}, bf16[32,80]{1,0:T(8,128)(2,1)S(1)}) custom-call(f32[64,80]{1,0:T(8,128)S(1)} %get-tuple-element.53.refs_0_, bf16[64,80]{1,0:T(8,128)(2,1)S(1)} %collective-permute-done.6.refs_1_, bf16[16,80]{1,0:T(8,128)(2,1)S(1)} %collective-permute-done.7.refs_2_, ...), custom_call_target="tpu_custom_call" | custom-call | tf_op jit(solution)/shard_map/pallas_call | solution.py:63
  26.4 2.1 %collective-permute-start.12 = (bf16[32,80]{1,0:T(8,128)(2,1)S(1)}, bf16[32,80]{1,0:T(8,128)(2,1)S(1)}, u32[]{:S(2)}, u32[]{:S(2)}) collective-permute-start(bf16[32,80]{1,0:T(8,128)(2,1)S(1)} %get-tuple-element.62), channel_id=1, source_target_pairs={{0,28},{1,31},{2,30},{3,29},{4,8},{5,11},{6,10},{7,9},{8,4},{9,7},... | collective-permute-start | bytes 15368 | tf_op jit(solution)/shard_map/ppermute | solution.py:330
  28.5 1.4 %collective-permute-start.10 = (bf16[64,80]{1,0:T(8,128)(2,1)S(1)}, bf16[64,80]{1,0:T(8,128)(2,1)S(1)}, u32[]{:S(2)}, u32[]{:S(2)}) collective-permute-start(bf16[64,80]{1,0:T(8,128)(2,1)S(1)} %get-tuple-element.60), channel_id=1, source_target_pairs={{0,3},{1,2},{2,1},{3,0},{4,7},{5,6},{6,5},{7,4},{8,11},{9,10},{10,... | collective-permute-start | bytes 30728 | tf_op jit(solution)/shard_map/ppermute | solution.py:333
  29.9 2.9 %collective-permute-done.12.refs_3_ = bf16[32,80]{1,0:T(8,128)(2,1)S(1)} collective-permute-done((bf16[32,80]{1,0:T(8,128)(2,1)S(1)}, bf16[32,80]{1,0:T(8,128)(2,1)S(1)}, u32[]{:S(2)}, u32[]{:S(2)}) %collective-permute-start.12) | collective-permute-done | bytes 5152 | tf_op jit(solution)/shard_map/ppermute | solution.py:330
  32.9 1.1 %collective-permute-done.13.refs_4_ = bf16[32,80]{1,0:T(8,128)(2,1)S(1)} collective-permute-done((bf16[32,80]{1,0:T(8,128)(2,1)S(1)}, bf16[32,80]{1,0:T(8,128)(2,1)S(1)}, u32[]{:S(2)}, u32[]{:S(2)}) %collective-permute-start.13) | collective-permute-done | bytes 5152 | tf_op jit(solution)/shard_map/ppermute | solution.py:324
  34.0 1.0 %shard_map.93 = (f32[64,80]{1,0:T(8,128)S(1)}, bf16[64,80]{1,0:T(8,128)(2,1)S(1)}, bf16[16,80]{1,0:T(8,128)(2,1)S(1)}, bf16[32,80]{1,0:T(8,128)(2,1)S(1)}) custom-call(f32[64,80]{1,0:T(8,128)S(1)} %get-tuple-element.59.refs_0_, bf16[64,80]{1,0:T(8,128)(2,1)S(1)} %collective-permute-done.10.refs_1_, bf16[16,80]{1,0:T(8,128)(2,1)S(1)} %collective-permute-done.11.refs_2_, ...), custom_call_target="tpu_custom_call" | custom-call | tf_op jit(solution)/shard_map/pallas_call | solution.py:63
  35.1 2.2 %collective-permute-start.16 = (bf16[32,80]{1,0:T(8,128)(2,1)S(1)}, bf16[32,80]{1,0:T(8,128)(2,1)S(1)}, u32[]{:S(2)}, u32[]{:S(2)}) collective-permute-start(bf16[32,80]{1,0:T(8,128)(2,1)S(1)} %get-tuple-element.66), channel_id=1, source_target_pairs={{0,28},{1,31},{2,30},{3,29},{4,8},{5,11},{6,10},{7,9},{8,4},{9,7},... | collective-permute-start | bytes 15368 | tf_op jit(solution)/shard_map/ppermute | solution.py:330
  37.2 1.0 %collective-permute-start.14 = (bf16[64,80]{1,0:T(8,128)(2,1)S(1)}, bf16[64,80]{1,0:T(8,128)(2,1)S(1)}, u32[]{:S(2)}, u32[]{:S(2)}) collective-permute-start(bf16[64,80]{1,0:T(8,128)(2,1)S(1)} %get-tuple-element.64), channel_id=1, source_target_pairs={{0,3},{1,2},{2,1},{3,0},{4,7},{5,6},{6,5},{7,4},{8,11},{9,10},{10,... | collective-permute-start | bytes 30728 | tf_op jit(solution)/shard_map/ppermute | solution.py:333
  38.2 3.3 %collective-permute-done.16.refs_3_ = bf16[32,80]{1,0:T(8,128)(2,1)S(1)} collective-permute-done((bf16[32,80]{1,0:T(8,128)(2,1)S(1)}, bf16[32,80]{1,0:T(8,128)(2,1)S(1)}, u32[]{:S(2)}, u32[]{:S(2)}) %collective-permute-start.16) | collective-permute-done | bytes 5152 | tf_op jit(solution)/shard_map/ppermute | solution.py:330
  41.6 1.1 %collective-permute-done.17.refs_4_ = bf16[32,80]{1,0:T(8,128)(2,1)S(1)} collective-permute-done((bf16[32,80]{1,0:T(8,128)(2,1)S(1)}, bf16[32,80]{1,0:T(8,128)(2,1)S(1)}, u32[]{:S(2)}, u32[]{:S(2)}) %collective-permute-start.17) | collective-permute-done | bytes 5152 | tf_op jit(solution)/shard_map/ppermute | solution.py:324
  42.7 1.0 %shard_map.94 = (f32[64,80]{1,0:T(8,128)S(1)}, bf16[64,80]{1,0:T(8,128)(2,1)S(1)}, bf16[16,80]{1,0:T(8,128)(2,1)S(1)}, bf16[32,80]{1,0:T(8,128)(2,1)S(1)}) custom-call(f32[64,80]{1,0:T(8,128)S(1)} %get-tuple-element.63.refs_0_, bf16[64,80]{1,0:T(8,128)(2,1)S(1)} %collective-permute-done.14.refs_1_, bf16[16,80]{1,0:T(8,128)(2,1)S(1)} %collective-permute-done.15.refs_2_, ...), custom_call_target="tpu_custom_call" | custom-call | tf_op jit(solution)/shard_map/pallas_call | solution.py:63
  43.7 2.2 %collective-permute-start.20 = (bf16[32,80]{1,0:T(8,128)(2,1)S(1)}, bf16[32,80]{1,0:T(8,128)(2,1)S(1)}, u32[]{:S(2)}, u32[]{:S(2)}) collective-permute-start(bf16[32,80]{1,0:T(8,128)(2,1)S(1)} %get-tuple-element.70), channel_id=1, source_target_pairs={{0,28},{1,31},{2,30},{3,29},{4,8},{5,11},{6,10},{7,9},{8,4},{9,7},... | collective-permute-start | bytes 15368 | tf_op jit(solution)/shard_map/ppermute | solution.py:330
  45.9 1.0 %collective-permute-start.18 = (bf16[64,80]{1,0:T(8,128)(2,1)S(1)}, bf16[64,80]{1,0:T(8,128)(2,1)S(1)}, u32[]{:S(2)}, u32[]{:S(2)}) collective-permute-start(bf16[64,80]{1,0:T(8,128)(2,1)S(1)} %get-tuple-element.68), channel_id=1, source_target_pairs={{0,3},{1,2},{2,1},{3,0},{4,7},{5,6},{6,5},{7,4},{8,11},{9,10},{10,... | collective-permute-start | bytes 30728 | tf_op jit(solution)/shard_map/ppermute | solution.py:333
  46.8 3.3 %collective-permute-done.20.refs_3_ = bf16[32,80]{1,0:T(8,128)(2,1)S(1)} collective-permute-done((bf16[32,80]{1,0:T(8,128)(2,1)S(1)}, bf16[32,80]{1,0:T(8,128)(2,1)S(1)}, u32[]{:S(2)}, u32[]{:S(2)}) %collective-permute-start.20) | collective-permute-done | bytes 5152 | tf_op jit(solution)/shard_map/ppermute | solution.py:330
  51.4 1.1 %shard_map.96 = (f32[12,80]{1,0:T(8,128)}, f32[4,320]{1,0:T(4,128)}) custom-call(f32[64,80]{1,0:T(8,128)S(1)} %get-tuple-element.67.refs_0_, bf16[64,80]{1,0:T(8,128)(2,1)S(1)} %collective-permute-done.18.refs_1_, bf16[16,80]{1,0:T(8,128)(2,1)S(1)} %collective-permute-done.19.refs_2_, bf16[32,80]{1,0:T(8,128)(2,1)S(1)} %collective-permute-done.20.refs_3_, ...), custom_call_target="tpu_custom_call" | custom-call | tf_op jit(solution)/shard_map/pallas_call | solution.py:63
  (43 shorter events, 6.7 us)
Async XLA Ops:
  3.3 1.4 %collective-permute-start = (f32[64,166]{1,0:T(8,128)S(1)}, f32[64,166]{1,0:T(8,128)S(1)}, u32[]{:S(2)}, u32[]{:S(2)}) collective-permute-start(f32[64,166]{1,0:T(8,128)S(1)} %get-tuple-element.39.packet), channel_id=1, source_target_pairs={{0,1},{1,0},{2,3},{3,2},{4,5},{5,4},{6,7},{7,6},{8,9},{9,8},{10,11... | collective-permute-start | bytes 127496 | tf_op jit(solution)/shard_map/ppermute | solution.py:324
  4.7 9.9 %collective-permute-start.3 = (f32[16,160]{1,0:T(8,128)S(1)}, f32[16,160]{1,0:T(8,128)S(1)}, u32[]{:S(2)}, u32[]{:S(2)}) collective-permute-start(f32[16,160]{1,0:T(8,128)S(1)} %get-tuple-element.48), channel_id=1, source_target_pairs={{0,28},{1,31},{2,30},{3,29},{4,8},{5,11},{6,10},{7,9},{8,4},{9,7},... | collective-permute-start | bytes 30728 | tf_op jit(solution)/shard_map/ppermute | solution.py:330
  10.7 3.9 %collective-permute-start.2 = (f32[32,160]{1,0:T(8,128)S(1)}, f32[32,160]{1,0:T(8,128)S(1)}, u32[]{:S(2)}, u32[]{:S(2)}) collective-permute-start(f32[32,160]{1,0:T(8,128)S(1)} %get-tuple-element.47), channel_id=1, source_target_pairs={{0,4},{1,7},{2,6},{3,5},{4,0},{5,3},{6,2},{7,1},{8,12},{9,15},{10,... | collective-permute-start | bytes 61448 | tf_op jit(solution)/shard_map/ppermute | solution.py:331
  11.9 4.7 %collective-permute-start.5 = (bf16[4,480,480]{2,1,0:T(8,128)(2,1)S(1)}, bf16[4,480,480]{2,1,0:T(8,128)(2,1)S(1)}, u32[]{:S(2)}, u32[]{:S(2)}) collective-permute-start(bf16[4,480,480]{2,1,0:T(8,128)(2,1)S(1)} %convolution_convert_fusion.refs_6_.refs_9_), channel_id=1, source_target_pairs={{0,1},{1,0},{2,3},{3,2},{4,5},{5,4},{6,7},{7,6},{8,9},{9,8},{10,11... | collective-permute-start | bytes 5529608 | tf_op jit(solution)/shard_map/ppermute | solution.py:324
  13.0 3.5 %collective-permute-start.1 = (f32[64,120]{1,0:T(8,128)S(1)}, f32[64,120]{1,0:T(8,128)S(1)}, u32[]{:S(2)}, u32[]{:S(2)}) collective-permute-start(f32[64,120]{1,0:T(8,128)S(1)} %shard_map.88), channel_id=1, source_target_pairs={{0,3},{1,2},{2,1},{3,0},{4,7},{5,6},{6,5},{7,4},{8,11},{9,10},{10,... | collective-permute-start | bytes 92168 | tf_op jit(solution)/shard_map/ppermute | solution.py:333
  14.6 2.0 %collective-permute-start.4 = (f32[32,160]{1,0:T(8,128)S(1)}, f32[32,160]{1,0:T(8,128)S(1)}, u32[]{:S(2)}, u32[]{:S(2)}) collective-permute-start(f32[32,160]{1,0:T(8,128)S(1)} %pad_maximum_fusion), channel_id=1, source_target_pairs={{0,1},{1,0},{2,3},{3,2},{4,5},{5,4},{6,7},{7,6},{8,9},{9,8},{10,11... | collective-permute-start | bytes 61448 | tf_op jit(solution)/shard_map/ppermute | solution.py:324
  17.7 6.4 %collective-permute-start.8 = (bf16[32,80]{1,0:T(8,128)(2,1)S(1)}, bf16[32,80]{1,0:T(8,128)(2,1)S(1)}, u32[]{:S(2)}, u32[]{:S(2)}) collective-permute-start(bf16[32,80]{1,0:T(8,128)(2,1)S(1)} %get-tuple-element.56), channel_id=1, source_target_pairs={{0,28},{1,31},{2,30},{3,29},{4,8},{5,11},{6,10},{7,9},{8,4},{9,7},... | collective-permute-start | bytes 15368 | tf_op jit(solution)/shard_map/ppermute | solution.py:330
  19.6 4.5 %collective-permute-start.7 = (bf16[16,80]{1,0:T(8,128)(2,1)S(1)}, bf16[16,80]{1,0:T(8,128)(2,1)S(1)}, u32[]{:S(2)}, u32[]{:S(2)}) collective-permute-start(bf16[16,80]{1,0:T(8,128)(2,1)S(1)} %get-tuple-element.55), channel_id=1, source_target_pairs={{0,4},{1,7},{2,6},{3,5},{4,0},{5,3},{6,2},{7,1},{8,12},{9,15},{10,... | collective-permute-start | bytes 7688 | tf_op jit(solution)/shard_map/ppermute | solution.py:331
  19.6 4.6 %collective-permute-start.6 = (bf16[64,80]{1,0:T(8,128)(2,1)S(1)}, bf16[64,80]{1,0:T(8,128)(2,1)S(1)}, u32[]{:S(2)}, u32[]{:S(2)}) collective-permute-start(bf16[64,80]{1,0:T(8,128)(2,1)S(1)} %get-tuple-element.54), channel_id=1, source_target_pairs={{0,3},{1,2},{2,1},{3,0},{4,7},{5,6},{6,5},{7,4},{8,11},{9,10},{10,... | collective-permute-start | bytes 30728 | tf_op jit(solution)/shard_map/ppermute | solution.py:333
  24.1 1.2 %collective-permute-start.9 = (bf16[32,80]{1,0:T(8,128)(2,1)S(1)}, bf16[32,80]{1,0:T(8,128)(2,1)S(1)}, u32[]{:S(2)}, u32[]{:S(2)}) collective-permute-start(bf16[32,80]{1,0:T(8,128)(2,1)S(1)} %pad_maximum_fusion.1), channel_id=1, source_target_pairs={{0,1},{1,0},{2,3},{3,2},{4,5},{5,4},{6,7},{7,6},{8,9},{9,8},{10,11... | collective-permute-start | bytes 15368 | tf_op jit(solution)/shard_map/ppermute | solution.py:324
  26.4 6.4 %collective-permute-start.12 = (bf16[32,80]{1,0:T(8,128)(2,1)S(1)}, bf16[32,80]{1,0:T(8,128)(2,1)S(1)}, u32[]{:S(2)}, u32[]{:S(2)}) collective-permute-start(bf16[32,80]{1,0:T(8,128)(2,1)S(1)} %get-tuple-element.62), channel_id=1, source_target_pairs={{0,28},{1,31},{2,30},{3,29},{4,8},{5,11},{6,10},{7,9},{8,4},{9,7},... | collective-permute-start | bytes 15368 | tf_op jit(solution)/shard_map/ppermute | solution.py:330
  28.4 4.4 %collective-permute-start.11 = (bf16[16,80]{1,0:T(8,128)(2,1)S(1)}, bf16[16,80]{1,0:T(8,128)(2,1)S(1)}, u32[]{:S(2)}, u32[]{:S(2)}) collective-permute-start(bf16[16,80]{1,0:T(8,128)(2,1)S(1)} %get-tuple-element.61), channel_id=1, source_target_pairs={{0,4},{1,7},{2,6},{3,5},{4,0},{5,3},{6,2},{7,1},{8,12},{9,15},{10,... | collective-permute-start | bytes 7688 | tf_op jit(solution)/shard_map/ppermute | solution.py:331
  28.5 4.4 %collective-permute-start.10 = (bf16[64,80]{1,0:T(8,128)(2,1)S(1)}, bf16[64,80]{1,0:T(8,128)(2,1)S(1)}, u32[]{:S(2)}, u32[]{:S(2)}) collective-permute-start(bf16[64,80]{1,0:T(8,128)(2,1)S(1)} %get-tuple-element.60), channel_id=1, source_target_pairs={{0,3},{1,2},{2,1},{3,0},{4,7},{5,6},{6,5},{7,4},{8,11},{9,10},{10,... | collective-permute-start | bytes 30728 | tf_op jit(solution)/shard_map/ppermute | solution.py:333
  32.8 1.2 %collective-permute-start.13 = (bf16[32,80]{1,0:T(8,128)(2,1)S(1)}, bf16[32,80]{1,0:T(8,128)(2,1)S(1)}, u32[]{:S(2)}, u32[]{:S(2)}) collective-permute-start(bf16[32,80]{1,0:T(8,128)(2,1)S(1)} %pad_maximum_fusion.2), channel_id=1, source_target_pairs={{0,1},{1,0},{2,3},{3,2},{4,5},{5,4},{6,7},{7,6},{8,9},{9,8},{10,11... | collective-permute-start | bytes 15368 | tf_op jit(solution)/shard_map/ppermute | solution.py:324
  35.1 6.4 %collective-permute-start.16 = (bf16[32,80]{1,0:T(8,128)(2,1)S(1)}, bf16[32,80]{1,0:T(8,128)(2,1)S(1)}, u32[]{:S(2)}, u32[]{:S(2)}) collective-permute-start(bf16[32,80]{1,0:T(8,128)(2,1)S(1)} %get-tuple-element.66), channel_id=1, source_target_pairs={{0,28},{1,31},{2,30},{3,29},{4,8},{5,11},{6,10},{7,9},{8,4},{9,7},... | collective-permute-start | bytes 15368 | tf_op jit(solution)/shard_map/ppermute | solution.py:330
  37.2 4.3 %collective-permute-start.15 = (bf16[16,80]{1,0:T(8,128)(2,1)S(1)}, bf16[16,80]{1,0:T(8,128)(2,1)S(1)}, u32[]{:S(2)}, u32[]{:S(2)}) collective-permute-start(bf16[16,80]{1,0:T(8,128)(2,1)S(1)} %get-tuple-element.65), channel_id=1, source_target_pairs={{0,4},{1,7},{2,6},{3,5},{4,0},{5,3},{6,2},{7,1},{8,12},{9,15},{10,... | collective-permute-start | bytes 7688 | tf_op jit(solution)/shard_map/ppermute | solution.py:331
  37.2 4.3 %collective-permute-start.14 = (bf16[64,80]{1,0:T(8,128)(2,1)S(1)}, bf16[64,80]{1,0:T(8,128)(2,1)S(1)}, u32[]{:S(2)}, u32[]{:S(2)}) collective-permute-start(bf16[64,80]{1,0:T(8,128)(2,1)S(1)} %get-tuple-element.64), channel_id=1, source_target_pairs={{0,3},{1,2},{2,1},{3,0},{4,7},{5,6},{6,5},{7,4},{8,11},{9,10},{10,... | collective-permute-start | bytes 30728 | tf_op jit(solution)/shard_map/ppermute | solution.py:333
  41.5 1.2 %collective-permute-start.17 = (bf16[32,80]{1,0:T(8,128)(2,1)S(1)}, bf16[32,80]{1,0:T(8,128)(2,1)S(1)}, u32[]{:S(2)}, u32[]{:S(2)}) collective-permute-start(bf16[32,80]{1,0:T(8,128)(2,1)S(1)} %pad_maximum_fusion.3), channel_id=1, source_target_pairs={{0,1},{1,0},{2,3},{3,2},{4,5},{5,4},{6,7},{7,6},{8,9},{9,8},{10,11... | collective-permute-start | bytes 15368 | tf_op jit(solution)/shard_map/ppermute | solution.py:324
  43.7 6.4 %collective-permute-start.20 = (bf16[32,80]{1,0:T(8,128)(2,1)S(1)}, bf16[32,80]{1,0:T(8,128)(2,1)S(1)}, u32[]{:S(2)}, u32[]{:S(2)}) collective-permute-start(bf16[32,80]{1,0:T(8,128)(2,1)S(1)} %get-tuple-element.70), channel_id=1, source_target_pairs={{0,28},{1,31},{2,30},{3,29},{4,8},{5,11},{6,10},{7,9},{8,4},{9,7},... | collective-permute-start | bytes 15368 | tf_op jit(solution)/shard_map/ppermute | solution.py:330
  45.9 4.3 %collective-permute-start.19 = (bf16[16,80]{1,0:T(8,128)(2,1)S(1)}, bf16[16,80]{1,0:T(8,128)(2,1)S(1)}, u32[]{:S(2)}, u32[]{:S(2)}) collective-permute-start(bf16[16,80]{1,0:T(8,128)(2,1)S(1)} %get-tuple-element.69), channel_id=1, source_target_pairs={{0,4},{1,7},{2,6},{3,5},{4,0},{5,3},{6,2},{7,1},{8,12},{9,15},{10,... | collective-permute-start | bytes 7688 | tf_op jit(solution)/shard_map/ppermute | solution.py:331
  45.9 4.8 %collective-permute-start.18 = (bf16[64,80]{1,0:T(8,128)(2,1)S(1)}, bf16[64,80]{1,0:T(8,128)(2,1)S(1)}, u32[]{:S(2)}, u32[]{:S(2)}) collective-permute-start(bf16[64,80]{1,0:T(8,128)(2,1)S(1)} %get-tuple-element.68), channel_id=1, source_target_pairs={{0,3},{1,2},{2,1},{3,0},{4,7},{5,6},{6,5},{7,4},{8,11},{9,10},{10,... | collective-permute-start | bytes 30728 | tf_op jit(solution)/shard_map/ppermute | solution.py:333
  50.1 1.2 %collective-permute-start.21 = (bf16[32,80]{1,0:T(8,128)(2,1)S(1)}, bf16[32,80]{1,0:T(8,128)(2,1)S(1)}, u32[]{:S(2)}, u32[]{:S(2)}) collective-permute-start(bf16[32,80]{1,0:T(8,128)(2,1)S(1)} %pad_maximum_fusion.4), channel_id=1, source_target_pairs={{0,1},{1,0},{2,3},{3,2},{4,5},{5,4},{6,7},{7,6},{8,9},{9,8},{10,11... | collective-permute-start | bytes 15368 | tf_op jit(solution)/shard_map/ppermute | solution.py:324

commit v8 on v7

--- a/solution.py
+++ b/solution.py
@@ -219,6 +219,30 @@
     return jnp.concatenate([sums[:border] + upper, sums[border:last], sums[last:] + lower], axis=0)
 
 
+def known_kernel(counts, border, *refs):
+    (own, first, second), (right, known_ref) = split(counts, refs)
+    even = lax.rem(lax.axis_index("elem"), 2) == 0
+    a, b = add_up(first)[:border], add_up(second)[:border]
+    upper, lower = jnp.where(even, a, b), jnp.where(even, b, a)
+    last = known_ref.shape[0] - border
+    known_ref[...] = add_up(own) + right[...]
+    known_ref[:border] += upper
+    known_ref[last:] += lower
+
+
+def completed(known, mate, border):
+    even = lax.rem(lax.axis_index("elem"), 2) == 0
+    half = mate.shape[0] // 2
+    a, b = (
+        add_up([mate.at[pl.ds(at + n * border, border)] for n in range(half // border)])
+        for at in (0, half)
+    )
+    upper, lower = jnp.where(even, a, b), jnp.where(even, b, a)
+    sums = known[...]
+    last = sums.shape[0] - border
+    return jnp.concatenate([sums[:border] + upper, sums[border:last], sums[last:] + lower], axis=0)
+
+
 def image(trace_now, hits, spread_hits, schur, sides):
     pieces = [block[e] for block in schur for e in range(block.shape[0])]
     picked = contract(hits[...], trace_now.astype(HALF), 1, 0)
@@ -258,10 +282,9 @@
     deal(sums, border, first_ref, second_ref)
 
 
-def step_kernel(counts, border, sides, *refs):
-    parts, rest = split(counts, refs)
-    right, scale, hits, spread_hits, *schur, sums_ref, sent_ref, first_ref, second_ref = rest
-    trace_now = (whole(parts, border) + right[...]) * scale[...]
+def step_kernel(border, sides, known, mate, *rest):
+    scale, hits, spread_hits, *schur, sums_ref, sent_ref, first_ref, second_ref = rest
+    trace_now = completed(known, mate, border) * scale[...]
     sums = image(trace_now, hits, spread_hits, schur, sides)
     sums_ref[...] = sums
     sent_ref[...] = sums.astype(HALF)
@@ -273,10 +296,9 @@
         turned_ref[e] = couple[e].T
 
 
-def last_kernel(counts, border, sides, *refs):
-    parts, rest = split(counts, refs)
-    right, scale, hits, couple, local, trace_ref, vol_ref = rest
-    trace_now = (whole(parts, border) + right[...]) * scale[...]
+def last_kernel(border, sides, known, mate, *rest):
+    scale, hits, couple, local, trace_ref, vol_ref = rest
+    trace_now = completed(known, mate, border) * scale[...]
     own_faces = trace_ref.shape[0]
     place = lax.axis_index("face") * own_faces
     rows = trace_now.shape[0]
@@ -408,17 +430,25 @@
         turn_kernel, [((elems, trace, volume), HALF)], couple, right,
         cost=pl.CostEstimate(flops=10**9, bytes_accessed=0, transcendentals=0),
     )
+
+    def gathered(*sent_parts):
+        *parts, (mate,) = exchange(*sent_parts)
+        counts = tuple(len(part) for part in parts)
+        (known,) = call(
+            functools.partial(known_kernel, counts, border), [((rows, width), F32)],
+            *flat(parts), right,
+        )
+        return known, mate
+
     for _ in range(SWEEPS - 2):
-        parts = exchange(*out)
         out = call(
-            counted(step_kernel, parts), dealt,
-            *flat(parts), right, scale, hits, spread_hits, schur_own, schur_mate,
+            functools.partial(step_kernel, border, sides), dealt,
+            *gathered(*out), scale, hits, spread_hits, schur_own, schur_mate,
         )
-    parts = exchange(*out)
     trace_update, vol_update = call(
-        counted(last_kernel, parts),
+        functools.partial(last_kernel, border, sides),
         [((own_faces, width), F32), ((elems, volume), F32)],
-        *flat(parts), right, scale, hits, turned, local_part,
+        *gathered(*out), scale, hits, turned, local_part,
     )
     return trace_update, vol_update
 

time: 52.7 us -> 52.7 us (level)
    pallas_call x11 -> x15, Pallas kernels: 8.84 us -> 8.9 us  [call(): pl.pallas_call(body, out_shape=outs, in_specs=[HBM] * stay + [VMEM] * (le...]
where the time goes in v8:
time: 52.7 us; the launch traced here: 52.5 us
  starting transfers between devices  21.7 us (41%)
  waiting for transfers between devices  18.9 us (36%)
  Pallas kernels  8.9 us (17%)
  matrix products  2.07 us (4%)
  between operations  0.83 us (2%)
    ppermute x5, starting transfers between devices, exchange(): lax.ppermute(to_second, AXES, partners(groups, chips, 1, s))  14.3 us
    ppermute x5, waiting for transfers between devices, exchange(): lax.ppermute(to_second, AXES, partners(groups, chips, 1, s))  13 us
    pallas_call x15, Pallas kernels, call(): pl.pallas_call(body, out_shape=outs, in_specs=[HBM] * stay + [VMEM] * (le...  8.9 us
    ppermute x5, starting transfers between devices, exchange(): lax.ppermute(sent, AXES, along_x(groups, chips, shift))  5.03 us
    ppermute x7, waiting for transfers between devices, swap_core(): return lax.ppermute(block, AXES, other_core(groups, chips))  4.06 us
    ppermute x7, starting transfers between devices, swap_core(): return lax.ppermute(block, AXES, other_core(groups, chips))  2.34 us
    dot_general x1, matrix products, local(): jnp.einsum('evs,evt->est', couple, down, preferred_element_type=F32)  1.22 us
  transfers between devices with their start and end apart: 22, of which 10 were waited for; matrix products, arithmetic and copies ran while one was open for 4% of the time, Pallas kernels for 2%

profile of v8, /device:TPU:0, one launch (start us, length us, event | category | flops | bytes accessed | tf_op | source)
XLA Modules:
  0.0 52.5 jit_solution(14360954736131371825)
XLA Ops:
  0.6 2.6 %shard_map.86 = (f32[8,320]{1,0:T(8,128)S(1)}, f32[64,166]{1,0:T(8,128)S(1)}, s32[8,6]{1,0:T(8,128)S(1)}, bf16[4,320,320]{2,1,0:T(8,128)(2,1)S(1)}, bf16[4,320,4...) custom-call(bf16[4,320,320]{2,1,0:T(8,128)(2,1)} %refs_0_.1, bf16[4,320,480]{2,1,0:T(8,128)(2,1)} %bitcast.5, ...), custom_call_target="tpu_custom_call" | custom-call | tf_op jit(solution)/shard_map/pallas_call | solution.py:63
  4.7 6.0 %collective-permute-start.3 = (f32[16,160]{1,0:T(8,128)S(1)}, f32[16,160]{1,0:T(8,128)S(1)}, u32[]{:S(2)}, u32[]{:S(2)}) collective-permute-start(f32[16,160]{1,0:T(8,128)S(1)} %get-tuple-element.48), channel_id=1, source_target_pairs={{0,28},{1,31},{2,30},{3,29},{4,8},{5,11},{6,10},{7,9},{8,4},{9,7},... | collective-permute-start | bytes 30728 | tf_op jit(solution)/shard_map/ppermute | solution.py:352
  10.7 1.2 %convolution_convert_fusion.refs_6_.rest_3_ = bf16[4,480,480]{2,1,0:T(8,128)(2,1)S(1)} fusion(bf16[4,320,480]{2,1,0:T(8,128)(2,1)S(1)} %convolution_convert_fusion.1.couple, bf16[4,320,480]{2,1,0:T(8,128)(2,1)S(1)} %get-tuple-element.45), kind=kOutput, calls=%fused_computation | convolution fusion | flops 590745600 | bytes 4300800 | tf_op jit(solution)/shard_map/evs,evt->est/dot_general | solution.py:394
  15.5 1.0 %collective-permute-done.1.refs_0_ = f32[64,120]{1,0:T(8,128)S(1)} collective-permute-done((f32[64,120]{1,0:T(8,128)S(1)}, f32[64,120]{1,0:T(8,128)S(1)}, u32[]{:S(2)}, u32[]{:S(2)}) %collective-permute-start.1) | collective-permute-done | bytes 30752 | tf_op jit(solution)/shard_map/ppermute | solution.py:355
  16.6 1.1 %shard_map.91 = (f32[64,80]{1,0:T(8,128)S(1)}, f32[64,80]{1,0:T(8,128)S(1)}, f32[64,80]{1,0:T(8,128)S(1)}, bf16[64,80]{1,0:T(8,128)(2,1)S(1)}, bf16[16,80]{1,0:T(8,128)(2,1)S(1)}, /*index=5*/bf16[32,80]{1,0:T(8,128)(2,1)S(1)}) custom-call(f32[64,160]{1,0:T(8,128)S(1)} %shard_map.89.refs_0_, f32[32,160]{1,0:T(8,128)S(1)} %collective-permute-done.2.refs_1_, ...), custom_call_target="tpu_custom_call" | custom-call | tf_op jit(solution)/shard_map/pallas_call | solution.py:63
  17.7 1.9 %collective-permute-start.8 = (bf16[32,80]{1,0:T(8,128)(2,1)S(1)}, bf16[32,80]{1,0:T(8,128)(2,1)S(1)}, u32[]{:S(2)}, u32[]{:S(2)}) collective-permute-start(bf16[32,80]{1,0:T(8,128)(2,1)S(1)} %get-tuple-element.56), channel_id=1, source_target_pairs={{0,28},{1,31},{2,30},{3,29},{4,8},{5,11},{6,10},{7,9},{8,4},{9,7},... | collective-permute-start | bytes 15368 | tf_op jit(solution)/shard_map/ppermute | solution.py:352
  19.7 1.0 %collective-permute-start.6 = (bf16[64,80]{1,0:T(8,128)(2,1)S(1)}, bf16[64,80]{1,0:T(8,128)(2,1)S(1)}, u32[]{:S(2)}, u32[]{:S(2)}) collective-permute-start(bf16[64,80]{1,0:T(8,128)(2,1)S(1)} %get-tuple-element.54), channel_id=1, source_target_pairs={{0,3},{1,2},{2,1},{3,0},{4,7},{5,6},{6,5},{7,4},{8,11},{9,10},{10,... | collective-permute-start | bytes 30728 | tf_op jit(solution)/shard_map/ppermute | solution.py:355
  20.6 3.5 %collective-permute-done.8.refs_3_ = bf16[32,80]{1,0:T(8,128)(2,1)S(1)} collective-permute-done((bf16[32,80]{1,0:T(8,128)(2,1)S(1)}, bf16[32,80]{1,0:T(8,128)(2,1)S(1)}, u32[]{:S(2)}, u32[]{:S(2)}) %collective-permute-start.8) | collective-permute-done | bytes 5152 | tf_op jit(solution)/shard_map/ppermute | solution.py:352
  24.3 1.1 %collective-permute-done.9.mate = bf16[32,80]{1,0:T(8,128)(2,1)S(1)} collective-permute-done((bf16[32,80]{1,0:T(8,128)(2,1)S(1)}, bf16[32,80]{1,0:T(8,128)(2,1)S(1)}, u32[]{:S(2)}, u32[]{:S(2)}) %collective-permute-start.9) | collective-permute-done | bytes 5152 | tf_op jit(solution)/shard_map/ppermute | solution.py:346
  25.4 1.0 %shard_map.93 = (f32[64,80]{1,0:T(8,128)S(1)}, bf16[64,80]{1,0:T(8,128)(2,1)S(1)}, bf16[16,80]{1,0:T(8,128)(2,1)S(1)}, bf16[32,80]{1,0:T(8,128)(2,1)S(1)}) custom-call(f32[64,80]{1,0:T(8,128)S(1)} %shard_map.92.known, bf16[32,80]{1,0:T(8,128)(2,1)S(1)} %collective-permute-done.9.mate, f32[64,80]{1,0:T(8,128)S(1)} %get-tuple-element.58.rest_0_, ...), custom_call_target="tpu_custom_call" | custom-call | tf_op jit(solution)/shard_map/pallas_call | solution.py:63
  26.4 2.1 %collective-permute-start.12 = (bf16[32,80]{1,0:T(8,128)(2,1)S(1)}, bf16[32,80]{1,0:T(8,128)(2,1)S(1)}, u32[]{:S(2)}, u32[]{:S(2)}) collective-permute-start(bf16[32,80]{1,0:T(8,128)(2,1)S(1)} %get-tuple-element.62), channel_id=1, source_target_pairs={{0,28},{1,31},{2,30},{3,29},{4,8},{5,11},{6,10},{7,9},{8,4},{9,7},... | collective-permute-start | bytes 15368 | tf_op jit(solution)/shard_map/ppermute | solution.py:352
  28.5 1.4 %collective-permute-start.10 = (bf16[64,80]{1,0:T(8,128)(2,1)S(1)}, bf16[64,80]{1,0:T(8,128)(2,1)S(1)}, u32[]{:S(2)}, u32[]{:S(2)}) collective-permute-start(bf16[64,80]{1,0:T(8,128)(2,1)S(1)} %get-tuple-element.60), channel_id=1, source_target_pairs={{0,3},{1,2},{2,1},{3,0},{4,7},{5,6},{6,5},{7,4},{8,11},{9,10},{10,... | collective-permute-start | bytes 30728 | tf_op jit(solution)/shard_map/ppermute | solution.py:355
  29.9 2.9 %collective-permute-done.12.refs_3_ = bf16[32,80]{1,0:T(8,128)(2,1)S(1)} collective-permute-done((bf16[32,80]{1,0:T(8,128)(2,1)S(1)}, bf16[32,80]{1,0:T(8,128)(2,1)S(1)}, u32[]{:S(2)}, u32[]{:S(2)}) %collective-permute-start.12) | collective-permute-done | bytes 5152 | tf_op jit(solution)/shard_map/ppermute | solution.py:352
  32.9 1.1 %collective-permute-done.13.mate = bf16[32,80]{1,0:T(8,128)(2,1)S(1)} collective-permute-done((bf16[32,80]{1,0:T(8,128)(2,1)S(1)}, bf16[32,80]{1,0:T(8,128)(2,1)S(1)}, u32[]{:S(2)}, u32[]{:S(2)}) %collective-permute-start.13) | collective-permute-done | bytes 5152 | tf_op jit(solution)/shard_map/ppermute | solution.py:346
  34.0 1.0 %shard_map.95 = (f32[64,80]{1,0:T(8,128)S(1)}, bf16[64,80]{1,0:T(8,128)(2,1)S(1)}, bf16[16,80]{1,0:T(8,128)(2,1)S(1)}, bf16[32,80]{1,0:T(8,128)(2,1)S(1)}) custom-call(f32[64,80]{1,0:T(8,128)S(1)} %shard_map.94.known, bf16[32,80]{1,0:T(8,128)(2,1)S(1)} %collective-permute-done.13.mate, f32[64,80]{1,0:T(8,128)S(1)} %get-tuple-element.58.rest_0_, ...), custom_call_target="tpu_custom_call" | custom-call | tf_op jit(solution)/shard_map/pallas_call | solution.py:63
  35.0 2.2 %collective-permute-start.16 = (bf16[32,80]{1,0:T(8,128)(2,1)S(1)}, bf16[32,80]{1,0:T(8,128)(2,1)S(1)}, u32[]{:S(2)}, u32[]{:S(2)}) collective-permute-start(bf16[32,80]{1,0:T(8,128)(2,1)S(1)} %get-tuple-element.66), channel_id=1, source_target_pairs={{0,28},{1,31},{2,30},{3,29},{4,8},{5,11},{6,10},{7,9},{8,4},{9,7},... | collective-permute-start | bytes 15368 | tf_op jit(solution)/shard_map/ppermute | solution.py:352
  37.2 1.0 %collective-permute-start.14 = (bf16[64,80]{1,0:T(8,128)(2,1)S(1)}, bf16[64,80]{1,0:T(8,128)(2,1)S(1)}, u32[]{:S(2)}, u32[]{:S(2)}) collective-permute-start(bf16[64,80]{1,0:T(8,128)(2,1)S(1)} %get-tuple-element.64), channel_id=1, source_target_pairs={{0,3},{1,2},{2,1},{3,0},{4,7},{5,6},{6,5},{7,4},{8,11},{9,10},{10,... | collective-permute-start | bytes 30728 | tf_op jit(solution)/shard_map/ppermute | solution.py:355
  38.2 3.3 %collective-permute-done.16.refs_3_ = bf16[32,80]{1,0:T(8,128)(2,1)S(1)} collective-permute-done((bf16[32,80]{1,0:T(8,128)(2,1)S(1)}, bf16[32,80]{1,0:T(8,128)(2,1)S(1)}, u32[]{:S(2)}, u32[]{:S(2)}) %collective-permute-start.16) | collective-permute-done | bytes 5152 | tf_op jit(solution)/shard_map/ppermute | solution.py:352
  41.6 1.1 %collective-permute-done.17.mate = bf16[32,80]{1,0:T(8,128)(2,1)S(1)} collective-permute-done((bf16[32,80]{1,0:T(8,128)(2,1)S(1)}, bf16[32,80]{1,0:T(8,128)(2,1)S(1)}, u32[]{:S(2)}, u32[]{:S(2)}) %collective-permute-start.17) | collective-permute-done | bytes 5152 | tf_op jit(solution)/shard_map/ppermute | solution.py:346
  42.7 1.0 %shard_map.97 = (f32[64,80]{1,0:T(8,128)S(1)}, bf16[64,80]{1,0:T(8,128)(2,1)S(1)}, bf16[16,80]{1,0:T(8,128)(2,1)S(1)}, bf16[32,80]{1,0:T(8,128)(2,1)S(1)}) custom-call(f32[64,80]{1,0:T(8,128)S(1)} %shard_map.96.known, bf16[32,80]{1,0:T(8,128)(2,1)S(1)} %collective-permute-done.17.mate, f32[64,80]{1,0:T(8,128)S(1)} %get-tuple-element.58.rest_0_, ...), custom_call_target="tpu_custom_call" | custom-call | tf_op jit(solution)/shard_map/pallas_call | solution.py:63
  43.7 2.2 %collective-permute-start.20 = (bf16[32,80]{1,0:T(8,128)(2,1)S(1)}, bf16[32,80]{1,0:T(8,128)(2,1)S(1)}, u32[]{:S(2)}, u32[]{:S(2)}) collective-permute-start(bf16[32,80]{1,0:T(8,128)(2,1)S(1)} %get-tuple-element.70), channel_id=1, source_target_pairs={{0,28},{1,31},{2,30},{3,29},{4,8},{5,11},{6,10},{7,9},{8,4},{9,7},... | collective-permute-start | bytes 15368 | tf_op jit(solution)/shard_map/ppermute | solution.py:352
  45.9 1.0 %collective-permute-start.18 = (bf16[64,80]{1,0:T(8,128)(2,1)S(1)}, bf16[64,80]{1,0:T(8,128)(2,1)S(1)}, u32[]{:S(2)}, u32[]{:S(2)}) collective-permute-start(bf16[64,80]{1,0:T(8,128)(2,1)S(1)} %get-tuple-element.68), channel_id=1, source_target_pairs={{0,3},{1,2},{2,1},{3,0},{4,7},{5,6},{6,5},{7,4},{8,11},{9,10},{10,... | collective-permute-start | bytes 30728 | tf_op jit(solution)/shard_map/ppermute | solution.py:355
  46.8 3.3 %collective-permute-done.20.refs_3_ = bf16[32,80]{1,0:T(8,128)(2,1)S(1)} collective-permute-done((bf16[32,80]{1,0:T(8,128)(2,1)S(1)}, bf16[32,80]{1,0:T(8,128)(2,1)S(1)}, u32[]{:S(2)}, u32[]{:S(2)}) %collective-permute-start.20) | collective-permute-done | bytes 5152 | tf_op jit(solution)/shard_map/ppermute | solution.py:352
  51.4 1.1 %shard_map.100 = (f32[12,80]{1,0:T(8,128)}, f32[4,320]{1,0:T(4,128)}) custom-call(f32[64,80]{1,0:T(8,128)S(1)} %shard_map.98.known, bf16[32,80]{1,0:T(8,128)(2,1)S(1)} %collective-permute-done.21.mate, f32[64,80]{1,0:T(8,128)S(1)} %get-tuple-element.58.rest_0_, bf16[48,64]{1,0:T(8,128)(2,1)S(1)} %get-tuple-element.50.refs_4_.rest_1_, ...), custom_call_target="tpu_custom_call" | custom-call | tf_op jit(solution)/shard_map/pallas_call | solution.py:63
  (47 shorter events, 6.8 us)
Async XLA Ops:
  3.3 1.4 %collective-permute-start = (f32[64,166]{1,0:T(8,128)S(1)}, f32[64,166]{1,0:T(8,128)S(1)}, u32[]{:S(2)}, u32[]{:S(2)}) collective-permute-start(f32[64,166]{1,0:T(8,128)S(1)} %get-tuple-element.39.packet), channel_id=1, source_target_pairs={{0,1},{1,0},{2,3},{3,2},{4,5},{5,4},{6,7},{7,6},{8,9},{9,8},{10,11... | collective-permute-start | bytes 127496 | tf_op jit(solution)/shard_map/ppermute | solution.py:346
  4.7 9.9 %collective-permute-start.3 = (f32[16,160]{1,0:T(8,128)S(1)}, f32[16,160]{1,0:T(8,128)S(1)}, u32[]{:S(2)}, u32[]{:S(2)}) collective-permute-start(f32[16,160]{1,0:T(8,128)S(1)} %get-tuple-element.48), channel_id=1, source_target_pairs={{0,28},{1,31},{2,30},{3,29},{4,8},{5,11},{6,10},{7,9},{8,4},{9,7},... | collective-permute-start | bytes 30728 | tf_op jit(solution)/shard_map/ppermute | solution.py:352
  10.7 3.9 %collective-permute-start.2 = (f32[32,160]{1,0:T(8,128)S(1)}, f32[32,160]{1,0:T(8,128)S(1)}, u32[]{:S(2)}, u32[]{:S(2)}) collective-permute-start(f32[32,160]{1,0:T(8,128)S(1)} %get-tuple-element.47), channel_id=1, source_target_pairs={{0,4},{1,7},{2,6},{3,5},{4,0},{5,3},{6,2},{7,1},{8,12},{9,15},{10,... | collective-permute-start | bytes 61448 | tf_op jit(solution)/shard_map/ppermute | solution.py:353
  11.9 4.7 %collective-permute-start.5 = (bf16[4,480,480]{2,1,0:T(8,128)(2,1)S(1)}, bf16[4,480,480]{2,1,0:T(8,128)(2,1)S(1)}, u32[]{:S(2)}, u32[]{:S(2)}) collective-permute-start(bf16[4,480,480]{2,1,0:T(8,128)(2,1)S(1)} %convolution_convert_fusion.refs_6_.rest_3_), channel_id=1, source_target_pairs={{0,1},{1,0},{2,3},{3,2},{4,5},{5,4},{6,7},{7,6},{8,9},{9,8},{10,11... | collective-permute-start | bytes 5529608 | tf_op jit(solution)/shard_map/ppermute | solution.py:346
  13.0 3.5 %collective-permute-start.1 = (f32[64,120]{1,0:T(8,128)S(1)}, f32[64,120]{1,0:T(8,128)S(1)}, u32[]{:S(2)}, u32[]{:S(2)}) collective-permute-start(f32[64,120]{1,0:T(8,128)S(1)} %shard_map.88), channel_id=1, source_target_pairs={{0,3},{1,2},{2,1},{3,0},{4,7},{5,6},{6,5},{7,4},{8,11},{9,10},{10,... | collective-permute-start | bytes 92168 | tf_op jit(solution)/shard_map/ppermute | solution.py:355
  14.6 2.0 %collective-permute-start.4 = (f32[32,160]{1,0:T(8,128)S(1)}, f32[32,160]{1,0:T(8,128)S(1)}, u32[]{:S(2)}, u32[]{:S(2)}) collective-permute-start(f32[32,160]{1,0:T(8,128)S(1)} %pad_maximum_fusion), channel_id=1, source_target_pairs={{0,1},{1,0},{2,3},{3,2},{4,5},{5,4},{6,7},{7,6},{8,9},{9,8},{10,11... | collective-permute-start | bytes 61448 | tf_op jit(solution)/shard_map/ppermute | solution.py:346
  17.7 6.4 %collective-permute-start.8 = (bf16[32,80]{1,0:T(8,128)(2,1)S(1)}, bf16[32,80]{1,0:T(8,128)(2,1)S(1)}, u32[]{:S(2)}, u32[]{:S(2)}) collective-permute-start(bf16[32,80]{1,0:T(8,128)(2,1)S(1)} %get-tuple-element.56), channel_id=1, source_target_pairs={{0,28},{1,31},{2,30},{3,29},{4,8},{5,11},{6,10},{7,9},{8,4},{9,7},... | collective-permute-start | bytes 15368 | tf_op jit(solution)/shard_map/ppermute | solution.py:352
  19.6 4.5 %collective-permute-start.7 = (bf16[16,80]{1,0:T(8,128)(2,1)S(1)}, bf16[16,80]{1,0:T(8,128)(2,1)S(1)}, u32[]{:S(2)}, u32[]{:S(2)}) collective-permute-start(bf16[16,80]{1,0:T(8,128)(2,1)S(1)} %get-tuple-element.55), channel_id=1, source_target_pairs={{0,4},{1,7},{2,6},{3,5},{4,0},{5,3},{6,2},{7,1},{8,12},{9,15},{10,... | collective-permute-start | bytes 7688 | tf_op jit(solution)/shard_map/ppermute | solution.py:353
  19.7 4.6 %collective-permute-start.6 = (bf16[64,80]{1,0:T(8,128)(2,1)S(1)}, bf16[64,80]{1,0:T(8,128)(2,1)S(1)}, u32[]{:S(2)}, u32[]{:S(2)}) collective-permute-start(bf16[64,80]{1,0:T(8,128)(2,1)S(1)} %get-tuple-element.54), channel_id=1, source_target_pairs={{0,3},{1,2},{2,1},{3,0},{4,7},{5,6},{6,5},{7,4},{8,11},{9,10},{10,... | collective-permute-start | bytes 30728 | tf_op jit(solution)/shard_map/ppermute | solution.py:355
  24.1 1.2 %collective-permute-start.9 = (bf16[32,80]{1,0:T(8,128)(2,1)S(1)}, bf16[32,80]{1,0:T(8,128)(2,1)S(1)}, u32[]{:S(2)}, u32[]{:S(2)}) collective-permute-start(bf16[32,80]{1,0:T(8,128)(2,1)S(1)} %pad_maximum_fusion.1), channel_id=1, source_target_pairs={{0,1},{1,0},{2,3},{3,2},{4,5},{5,4},{6,7},{7,6},{8,9},{9,8},{10,11... | collective-permute-start | bytes 15368 | tf_op jit(solution)/shard_map/ppermute | solution.py:346
  26.4 6.4 %collective-permute-start.12 = (bf16[32,80]{1,0:T(8,128)(2,1)S(1)}, bf16[32,80]{1,0:T(8,128)(2,1)S(1)}, u32[]{:S(2)}, u32[]{:S(2)}) collective-permute-start(bf16[32,80]{1,0:T(8,128)(2,1)S(1)} %get-tuple-element.62), channel_id=1, source_target_pairs={{0,28},{1,31},{2,30},{3,29},{4,8},{5,11},{6,10},{7,9},{8,4},{9,7},... | collective-permute-start | bytes 15368 | tf_op jit(solution)/shard_map/ppermute | solution.py:352
  28.4 4.4 %collective-permute-start.11 = (bf16[16,80]{1,0:T(8,128)(2,1)S(1)}, bf16[16,80]{1,0:T(8,128)(2,1)S(1)}, u32[]{:S(2)}, u32[]{:S(2)}) collective-permute-start(bf16[16,80]{1,0:T(8,128)(2,1)S(1)} %get-tuple-element.61), channel_id=1, source_target_pairs={{0,4},{1,7},{2,6},{3,5},{4,0},{5,3},{6,2},{7,1},{8,12},{9,15},{10,... | collective-permute-start | bytes 7688 | tf_op jit(solution)/shard_map/ppermute | solution.py:353
  28.5 4.4 %collective-permute-start.10 = (bf16[64,80]{1,0:T(8,128)(2,1)S(1)}, bf16[64,80]{1,0:T(8,128)(2,1)S(1)}, u32[]{:S(2)}, u32[]{:S(2)}) collective-permute-start(bf16[64,80]{1,0:T(8,128)(2,1)S(1)} %get-tuple-element.60), channel_id=1, source_target_pairs={{0,3},{1,2},{2,1},{3,0},{4,7},{5,6},{6,5},{7,4},{8,11},{9,10},{10,... | collective-permute-start | bytes 30728 | tf_op jit(solution)/shard_map/ppermute | solution.py:355
  32.8 1.2 %collective-permute-start.13 = (bf16[32,80]{1,0:T(8,128)(2,1)S(1)}, bf16[32,80]{1,0:T(8,128)(2,1)S(1)}, u32[]{:S(2)}, u32[]{:S(2)}) collective-permute-start(bf16[32,80]{1,0:T(8,128)(2,1)S(1)} %pad_maximum_fusion.2), channel_id=1, source_target_pairs={{0,1},{1,0},{2,3},{3,2},{4,5},{5,4},{6,7},{7,6},{8,9},{9,8},{10,11... | collective-permute-start | bytes 15368 | tf_op jit(solution)/shard_map/ppermute | solution.py:346
  35.0 6.4 %collective-permute-start.16 = (bf16[32,80]{1,0:T(8,128)(2,1)S(1)}, bf16[32,80]{1,0:T(8,128)(2,1)S(1)}, u32[]{:S(2)}, u32[]{:S(2)}) collective-permute-start(bf16[32,80]{1,0:T(8,128)(2,1)S(1)} %get-tuple-element.66), channel_id=1, source_target_pairs={{0,28},{1,31},{2,30},{3,29},{4,8},{5,11},{6,10},{7,9},{8,4},{9,7},... | collective-permute-start | bytes 15368 | tf_op jit(solution)/shard_map/ppermute | solution.py:352
  37.2 4.3 %collective-permute-start.15 = (bf16[16,80]{1,0:T(8,128)(2,1)S(1)}, bf16[16,80]{1,0:T(8,128)(2,1)S(1)}, u32[]{:S(2)}, u32[]{:S(2)}) collective-permute-start(bf16[16,80]{1,0:T(8,128)(2,1)S(1)} %get-tuple-element.65), channel_id=1, source_target_pairs={{0,4},{1,7},{2,6},{3,5},{4,0},{5,3},{6,2},{7,1},{8,12},{9,15},{10,... | collective-permute-start | bytes 7688 | tf_op jit(solution)/shard_map/ppermute | solution.py:353
  37.2 4.3 %collective-permute-start.14 = (bf16[64,80]{1,0:T(8,128)(2,1)S(1)}, bf16[64,80]{1,0:T(8,128)(2,1)S(1)}, u32[]{:S(2)}, u32[]{:S(2)}) collective-permute-start(bf16[64,80]{1,0:T(8,128)(2,1)S(1)} %get-tuple-element.64), channel_id=1, source_target_pairs={{0,3},{1,2},{2,1},{3,0},{4,7},{5,6},{6,5},{7,4},{8,11},{9,10},{10,... | collective-permute-start | bytes 30728 | tf_op jit(solution)/shard_map/ppermute | solution.py:355
  41.5 1.2 %collective-permute-start.17 = (bf16[32,80]{1,0:T(8,128)(2,1)S(1)}, bf16[32,80]{1,0:T(8,128)(2,1)S(1)}, u32[]{:S(2)}, u32[]{:S(2)}) collective-permute-start(bf16[32,80]{1,0:T(8,128)(2,1)S(1)} %pad_maximum_fusion.3), channel_id=1, source_target_pairs={{0,1},{1,0},{2,3},{3,2},{4,5},{5,4},{6,7},{7,6},{8,9},{9,8},{10,11... | collective-permute-start | bytes 15368 | tf_op jit(solution)/shard_map/ppermute | solution.py:346
  43.7 6.4 %collective-permute-start.20 = (bf16[32,80]{1,0:T(8,128)(2,1)S(1)}, bf16[32,80]{1,0:T(8,128)(2,1)S(1)}, u32[]{:S(2)}, u32[]{:S(2)}) collective-permute-start(bf16[32,80]{1,0:T(8,128)(2,1)S(1)} %get-tuple-element.70), channel_id=1, source_target_pairs={{0,28},{1,31},{2,30},{3,29},{4,8},{5,11},{6,10},{7,9},{8,4},{9,7},... | collective-permute-start | bytes 15368 | tf_op jit(solution)/shard_map/ppermute | solution.py:352
  45.9 4.3 %collective-permute-start.19 = (bf16[16,80]{1,0:T(8,128)(2,1)S(1)}, bf16[16,80]{1,0:T(8,128)(2,1)S(1)}, u32[]{:S(2)}, u32[]{:S(2)}) collective-permute-start(bf16[16,80]{1,0:T(8,128)(2,1)S(1)} %get-tuple-element.69), channel_id=1, source_target_pairs={{0,4},{1,7},{2,6},{3,5},{4,0},{5,3},{6,2},{7,1},{8,12},{9,15},{10,... | collective-permute-start | bytes 7688 | tf_op jit(solution)/shard_map/ppermute | solution.py:353
  45.9 4.8 %collective-permute-start.18 = (bf16[64,80]{1,0:T(8,128)(2,1)S(1)}, bf16[64,80]{1,0:T(8,128)(2,1)S(1)}, u32[]{:S(2)}, u32[]{:S(2)}) collective-permute-start(bf16[64,80]{1,0:T(8,128)(2,1)S(1)} %get-tuple-element.68), channel_id=1, source_target_pairs={{0,3},{1,2},{2,1},{3,0},{4,7},{5,6},{6,5},{7,4},{8,11},{9,10},{10,... | collective-permute-start | bytes 30728 | tf_op jit(solution)/shard_map/ppermute | solution.py:355
  50.1 1.2 %collective-permute-start.21 = (bf16[32,80]{1,0:T(8,128)(2,1)S(1)}, bf16[32,80]{1,0:T(8,128)(2,1)S(1)}, u32[]{:S(2)}, u32[]{:S(2)}) collective-permute-start(bf16[32,80]{1,0:T(8,128)(2,1)S(1)} %pad_maximum_fusion.4), channel_id=1, source_target_pairs={{0,1},{1,0},{2,3},{3,2},{4,5},{5,4},{6,7},{7,6},{8,9},{9,8},{10,11... | collective-permute-start | bytes 15368 | tf_op jit(solution)/shard_map/ppermute | solution.py:346

commit v9 on v7

--- a/solution.py
+++ b/solution.py
@@ -224,7 +224,7 @@
     picked = contract(hits[...], trace_now.astype(HALF), 1, 0)
     lam = to_lanes(picked, len(pieces), sides)
     terms = add_up([contract(masked(lam, e), block, 1, 0) for e, block in enumerate(pieces)])
-    return spread(spread_hits[...], to_rows(terms, sides, trace_now.shape[1]))
+    return contract(spread_hits[...], to_rows(terms, sides, trace_now.shape[1]).astype(HALF), 1, 0)
 
 
 def own_kernel(chip_faces, sums, *refs):

time: 52.7 us -> 52.5 us (level)
  no operation moved by 1% of the time
where the time goes in v9:
time: 52.5 us; the launch traced here: 52.4 us
  starting transfers between devices  21.7 us (41%)
  waiting for transfers between devices  19 us (36%)
  Pallas kernels  8.77 us (17%)
  matrix products  2.07 us (4%)
  between operations  0.78 us (1%)
    ppermute x5, starting transfers between devices, exchange(): lax.ppermute(to_second, AXES, partners(groups, chips, 1, s))  14.2 us
    ppermute x5, waiting for transfers between devices, exchange(): lax.ppermute(to_second, AXES, partners(groups, chips, 1, s))  13 us
    pallas_call x11, Pallas kernels, call(): pl.pallas_call(body, out_shape=outs, in_specs=[HBM] * stay + [VMEM] * (le...  8.77 us
    ppermute x5, starting transfers between devices, exchange(): lax.ppermute(sent, AXES, along_x(groups, chips, shift))  5.03 us
    ppermute x7, waiting for transfers between devices, swap_core(): return lax.ppermute(block, AXES, other_core(groups, chips))  4.16 us
    ppermute x7, starting transfers between devices, swap_core(): return lax.ppermute(block, AXES, other_core(groups, chips))  2.34 us
    dot_general x1, matrix products, local(): jnp.einsum('evs,evt->est', couple, down, preferred_element_type=F32)  1.22 us
  transfers between devices with their start and end apart: 22, of which 10 were waited for; matrix products, arithmetic and copies ran while one was open for 4% of the time, Pallas kernels for 2%

profile of v9, /device:TPU:0, one launch (start us, length us, event | category | flops | bytes accessed | tf_op | source)
XLA Modules:
  0.0 52.4 jit_solution(8856707531017935341)
XLA Ops:
  0.6 2.6 %shard_map.86 = (f32[8,320]{1,0:T(8,128)S(1)}, f32[64,166]{1,0:T(8,128)S(1)}, s32[8,6]{1,0:T(8,128)S(1)}, bf16[4,320,320]{2,1,0:T(8,128)(2,1)S(1)}, bf16[4,320,4...) custom-call(bf16[4,320,320]{2,1,0:T(8,128)(2,1)} %refs_0_.1, bf16[4,320,480]{2,1,0:T(8,128)(2,1)} %bitcast.5, ...), custom_call_target="tpu_custom_call" | custom-call | tf_op jit(solution)/shard_map/pallas_call | solution.py:63
  4.7 6.0 %collective-permute-start.3 = (f32[16,160]{1,0:T(8,128)S(1)}, f32[16,160]{1,0:T(8,128)S(1)}, u32[]{:S(2)}, u32[]{:S(2)}) collective-permute-start(f32[16,160]{1,0:T(8,128)S(1)} %get-tuple-element.48), channel_id=1, source_target_pairs={{0,28},{1,31},{2,30},{3,29},{4,8},{5,11},{6,10},{7,9},{8,4},{9,7},... | collective-permute-start | bytes 30728 | tf_op jit(solution)/shard_map/ppermute | solution.py:330
  10.7 1.2 %convolution_convert_fusion.refs_6_.refs_9_ = bf16[4,480,480]{2,1,0:T(8,128)(2,1)S(1)} fusion(bf16[4,320,480]{2,1,0:T(8,128)(2,1)S(1)} %convolution_convert_fusion.1.couple, bf16[4,320,480]{2,1,0:T(8,128)(2,1)S(1)} %get-tuple-element.45), kind=kOutput, calls=%fused_computation | convolution fusion | flops 590745600 | bytes 4300800 | tf_op jit(solution)/shard_map/evs,evt->est/dot_general | solution.py:372
  15.5 1.0 %collective-permute-done.1.refs_0_ = f32[64,120]{1,0:T(8,128)S(1)} collective-permute-done((f32[64,120]{1,0:T(8,128)S(1)}, f32[64,120]{1,0:T(8,128)S(1)}, u32[]{:S(2)}, u32[]{:S(2)}) %collective-permute-start.1) | collective-permute-done | bytes 30752 | tf_op jit(solution)/shard_map/ppermute | solution.py:333
  16.6 1.1 %shard_map.91 = (f32[64,80]{1,0:T(8,128)S(1)}, f32[64,80]{1,0:T(8,128)S(1)}, f32[64,80]{1,0:T(8,128)S(1)}, bf16[64,80]{1,0:T(8,128)(2,1)S(1)}, bf16[16,80]{1,0:T(8,128)(2,1)S(1)}, /*index=5*/bf16[32,80]{1,0:T(8,128)(2,1)S(1)}) custom-call(f32[64,160]{1,0:T(8,128)S(1)} %shard_map.89.refs_0_, f32[32,160]{1,0:T(8,128)S(1)} %collective-permute-done.2.refs_1_, ...), custom_call_target="tpu_custom_call" | custom-call | tf_op jit(solution)/shard_map/pallas_call | solution.py:63
  17.7 1.9 %collective-permute-start.8 = (bf16[32,80]{1,0:T(8,128)(2,1)S(1)}, bf16[32,80]{1,0:T(8,128)(2,1)S(1)}, u32[]{:S(2)}, u32[]{:S(2)}) collective-permute-start(bf16[32,80]{1,0:T(8,128)(2,1)S(1)} %get-tuple-element.56), channel_id=1, source_target_pairs={{0,28},{1,31},{2,30},{3,29},{4,8},{5,11},{6,10},{7,9},{8,4},{9,7},... | collective-permute-start | bytes 15368 | tf_op jit(solution)/shard_map/ppermute | solution.py:330
  19.6 1.0 %collective-permute-start.6 = (bf16[64,80]{1,0:T(8,128)(2,1)S(1)}, bf16[64,80]{1,0:T(8,128)(2,1)S(1)}, u32[]{:S(2)}, u32[]{:S(2)}) collective-permute-start(bf16[64,80]{1,0:T(8,128)(2,1)S(1)} %get-tuple-element.54), channel_id=1, source_target_pairs={{0,3},{1,2},{2,1},{3,0},{4,7},{5,6},{6,5},{7,4},{8,11},{9,10},{10,... | collective-permute-start | bytes 30728 | tf_op jit(solution)/shard_map/ppermute | solution.py:333
  20.6 3.5 %collective-permute-done.8.refs_3_ = bf16[32,80]{1,0:T(8,128)(2,1)S(1)} collective-permute-done((bf16[32,80]{1,0:T(8,128)(2,1)S(1)}, bf16[32,80]{1,0:T(8,128)(2,1)S(1)}, u32[]{:S(2)}, u32[]{:S(2)}) %collective-permute-start.8) | collective-permute-done | bytes 5152 | tf_op jit(solution)/shard_map/ppermute | solution.py:330
  24.2 1.1 %collective-permute-done.9.refs_4_ = bf16[32,80]{1,0:T(8,128)(2,1)S(1)} collective-permute-done((bf16[32,80]{1,0:T(8,128)(2,1)S(1)}, bf16[32,80]{1,0:T(8,128)(2,1)S(1)}, u32[]{:S(2)}, u32[]{:S(2)}) %collective-permute-start.9) | collective-permute-done | bytes 5152 | tf_op jit(solution)/shard_map/ppermute | solution.py:324
  25.3 1.0 %shard_map.92 = (f32[64,80]{1,0:T(8,128)S(1)}, bf16[64,80]{1,0:T(8,128)(2,1)S(1)}, bf16[16,80]{1,0:T(8,128)(2,1)S(1)}, bf16[32,80]{1,0:T(8,128)(2,1)S(1)}) custom-call(f32[64,80]{1,0:T(8,128)S(1)} %get-tuple-element.53.refs_0_, bf16[64,80]{1,0:T(8,128)(2,1)S(1)} %collective-permute-done.6.refs_1_, bf16[16,80]{1,0:T(8,128)(2,1)S(1)} %collective-permute-done.7.refs_2_, ...), custom_call_target="tpu_custom_call" | custom-call | tf_op jit(solution)/shard_map/pallas_call | solution.py:63
  26.3 2.0 %collective-permute-start.12 = (bf16[32,80]{1,0:T(8,128)(2,1)S(1)}, bf16[32,80]{1,0:T(8,128)(2,1)S(1)}, u32[]{:S(2)}, u32[]{:S(2)}) collective-permute-start(bf16[32,80]{1,0:T(8,128)(2,1)S(1)} %get-tuple-element.62), channel_id=1, source_target_pairs={{0,28},{1,31},{2,30},{3,29},{4,8},{5,11},{6,10},{7,9},{8,4},{9,7},... | collective-permute-start | bytes 15368 | tf_op jit(solution)/shard_map/ppermute | solution.py:330
  28.4 1.4 %collective-permute-start.10 = (bf16[64,80]{1,0:T(8,128)(2,1)S(1)}, bf16[64,80]{1,0:T(8,128)(2,1)S(1)}, u32[]{:S(2)}, u32[]{:S(2)}) collective-permute-start(bf16[64,80]{1,0:T(8,128)(2,1)S(1)} %get-tuple-element.60), channel_id=1, source_target_pairs={{0,3},{1,2},{2,1},{3,0},{4,7},{5,6},{6,5},{7,4},{8,11},{9,10},{10,... | collective-permute-start | bytes 30728 | tf_op jit(solution)/shard_map/ppermute | solution.py:333
  29.8 2.9 %collective-permute-done.12.refs_3_ = bf16[32,80]{1,0:T(8,128)(2,1)S(1)} collective-permute-done((bf16[32,80]{1,0:T(8,128)(2,1)S(1)}, bf16[32,80]{1,0:T(8,128)(2,1)S(1)}, u32[]{:S(2)}, u32[]{:S(2)}) %collective-permute-start.12) | collective-permute-done | bytes 5152 | tf_op jit(solution)/shard_map/ppermute | solution.py:330
  32.8 1.1 %collective-permute-done.13.refs_4_ = bf16[32,80]{1,0:T(8,128)(2,1)S(1)} collective-permute-done((bf16[32,80]{1,0:T(8,128)(2,1)S(1)}, bf16[32,80]{1,0:T(8,128)(2,1)S(1)}, u32[]{:S(2)}, u32[]{:S(2)}) %collective-permute-start.13) | collective-permute-done | bytes 5152 | tf_op jit(solution)/shard_map/ppermute | solution.py:324
  34.0 1.0 %shard_map.93 = (f32[64,80]{1,0:T(8,128)S(1)}, bf16[64,80]{1,0:T(8,128)(2,1)S(1)}, bf16[16,80]{1,0:T(8,128)(2,1)S(1)}, bf16[32,80]{1,0:T(8,128)(2,1)S(1)}) custom-call(f32[64,80]{1,0:T(8,128)S(1)} %get-tuple-element.59.refs_0_, bf16[64,80]{1,0:T(8,128)(2,1)S(1)} %collective-permute-done.10.refs_1_, bf16[16,80]{1,0:T(8,128)(2,1)S(1)} %collective-permute-done.11.refs_2_, ...), custom_call_target="tpu_custom_call" | custom-call | tf_op jit(solution)/shard_map/pallas_call | solution.py:63
  35.0 2.1 %collective-permute-start.16 = (bf16[32,80]{1,0:T(8,128)(2,1)S(1)}, bf16[32,80]{1,0:T(8,128)(2,1)S(1)}, u32[]{:S(2)}, u32[]{:S(2)}) collective-permute-start(bf16[32,80]{1,0:T(8,128)(2,1)S(1)} %get-tuple-element.66), channel_id=1, source_target_pairs={{0,28},{1,31},{2,30},{3,29},{4,8},{5,11},{6,10},{7,9},{8,4},{9,7},... | collective-permute-start | bytes 15368 | tf_op jit(solution)/shard_map/ppermute | solution.py:330
  37.1 1.0 %collective-permute-start.14 = (bf16[64,80]{1,0:T(8,128)(2,1)S(1)}, bf16[64,80]{1,0:T(8,128)(2,1)S(1)}, u32[]{:S(2)}, u32[]{:S(2)}) collective-permute-start(bf16[64,80]{1,0:T(8,128)(2,1)S(1)} %get-tuple-element.64), channel_id=1, source_target_pairs={{0,3},{1,2},{2,1},{3,0},{4,7},{5,6},{6,5},{7,4},{8,11},{9,10},{10,... | collective-permute-start | bytes 30728 | tf_op jit(solution)/shard_map/ppermute | solution.py:333
  38.1 3.3 %collective-permute-done.16.refs_3_ = bf16[32,80]{1,0:T(8,128)(2,1)S(1)} collective-permute-done((bf16[32,80]{1,0:T(8,128)(2,1)S(1)}, bf16[32,80]{1,0:T(8,128)(2,1)S(1)}, u32[]{:S(2)}, u32[]{:S(2)}) %collective-permute-start.16) | collective-permute-done | bytes 5152 | tf_op jit(solution)/shard_map/ppermute | solution.py:330
  41.5 1.1 %collective-permute-done.17.refs_4_ = bf16[32,80]{1,0:T(8,128)(2,1)S(1)} collective-permute-done((bf16[32,80]{1,0:T(8,128)(2,1)S(1)}, bf16[32,80]{1,0:T(8,128)(2,1)S(1)}, u32[]{:S(2)}, u32[]{:S(2)}) %collective-permute-start.17) | collective-permute-done | bytes 5152 | tf_op jit(solution)/shard_map/ppermute | solution.py:324
  42.6 1.0 %shard_map.94 = (f32[64,80]{1,0:T(8,128)S(1)}, bf16[64,80]{1,0:T(8,128)(2,1)S(1)}, bf16[16,80]{1,0:T(8,128)(2,1)S(1)}, bf16[32,80]{1,0:T(8,128)(2,1)S(1)}) custom-call(f32[64,80]{1,0:T(8,128)S(1)} %get-tuple-element.63.refs_0_, bf16[64,80]{1,0:T(8,128)(2,1)S(1)} %collective-permute-done.14.refs_1_, bf16[16,80]{1,0:T(8,128)(2,1)S(1)} %collective-permute-done.15.refs_2_, ...), custom_call_target="tpu_custom_call" | custom-call | tf_op jit(solution)/shard_map/pallas_call | solution.py:63
  43.6 2.1 %collective-permute-start.20 = (bf16[32,80]{1,0:T(8,128)(2,1)S(1)}, bf16[32,80]{1,0:T(8,128)(2,1)S(1)}, u32[]{:S(2)}, u32[]{:S(2)}) collective-permute-start(bf16[32,80]{1,0:T(8,128)(2,1)S(1)} %get-tuple-element.70), channel_id=1, source_target_pairs={{0,28},{1,31},{2,30},{3,29},{4,8},{5,11},{6,10},{7,9},{8,4},{9,7},... | collective-permute-start | bytes 15368 | tf_op jit(solution)/shard_map/ppermute | solution.py:330
  45.7 1.0 %collective-permute-start.18 = (bf16[64,80]{1,0:T(8,128)(2,1)S(1)}, bf16[64,80]{1,0:T(8,128)(2,1)S(1)}, u32[]{:S(2)}, u32[]{:S(2)}) collective-permute-start(bf16[64,80]{1,0:T(8,128)(2,1)S(1)} %get-tuple-element.68), channel_id=1, source_target_pairs={{0,3},{1,2},{2,1},{3,0},{4,7},{5,6},{6,5},{7,4},{8,11},{9,10},{10,... | collective-permute-start | bytes 30728 | tf_op jit(solution)/shard_map/ppermute | solution.py:333
  46.7 3.3 %collective-permute-done.20.refs_3_ = bf16[32,80]{1,0:T(8,128)(2,1)S(1)} collective-permute-done((bf16[32,80]{1,0:T(8,128)(2,1)S(1)}, bf16[32,80]{1,0:T(8,128)(2,1)S(1)}, u32[]{:S(2)}, u32[]{:S(2)}) %collective-permute-start.20) | collective-permute-done | bytes 5152 | tf_op jit(solution)/shard_map/ppermute | solution.py:330
  51.2 1.1 %shard_map.96 = (f32[12,80]{1,0:T(8,128)}, f32[4,320]{1,0:T(4,128)}) custom-call(f32[64,80]{1,0:T(8,128)S(1)} %get-tuple-element.67.refs_0_, bf16[64,80]{1,0:T(8,128)(2,1)S(1)} %collective-permute-done.18.refs_1_, bf16[16,80]{1,0:T(8,128)(2,1)S(1)} %collective-permute-done.19.refs_2_, bf16[32,80]{1,0:T(8,128)(2,1)S(1)} %collective-permute-done.20.refs_3_, ...), custom_call_target="tpu_custom_call" | custom-call | tf_op jit(solution)/shard_map/pallas_call | solution.py:63
  (43 shorter events, 6.7 us)
Async XLA Ops:
  3.3 1.4 %collective-permute-start = (f32[64,166]{1,0:T(8,128)S(1)}, f32[64,166]{1,0:T(8,128)S(1)}, u32[]{:S(2)}, u32[]{:S(2)}) collective-permute-start(f32[64,166]{1,0:T(8,128)S(1)} %get-tuple-element.39.packet), channel_id=1, source_target_pairs={{0,1},{1,0},{2,3},{3,2},{4,5},{5,4},{6,7},{7,6},{8,9},{9,8},{10,11... | collective-permute-start | bytes 127496 | tf_op jit(solution)/shard_map/ppermute | solution.py:324
  4.7 9.9 %collective-permute-start.3 = (f32[16,160]{1,0:T(8,128)S(1)}, f32[16,160]{1,0:T(8,128)S(1)}, u32[]{:S(2)}, u32[]{:S(2)}) collective-permute-start(f32[16,160]{1,0:T(8,128)S(1)} %get-tuple-element.48), channel_id=1, source_target_pairs={{0,28},{1,31},{2,30},{3,29},{4,8},{5,11},{6,10},{7,9},{8,4},{9,7},... | collective-permute-start | bytes 30728 | tf_op jit(solution)/shard_map/ppermute | solution.py:330
  10.7 3.9 %collective-permute-start.2 = (f32[32,160]{1,0:T(8,128)S(1)}, f32[32,160]{1,0:T(8,128)S(1)}, u32[]{:S(2)}, u32[]{:S(2)}) collective-permute-start(f32[32,160]{1,0:T(8,128)S(1)} %get-tuple-element.47), channel_id=1, source_target_pairs={{0,4},{1,7},{2,6},{3,5},{4,0},{5,3},{6,2},{7,1},{8,12},{9,15},{10,... | collective-permute-start | bytes 61448 | tf_op jit(solution)/shard_map/ppermute | solution.py:331
  11.9 4.7 %collective-permute-start.5 = (bf16[4,480,480]{2,1,0:T(8,128)(2,1)S(1)}, bf16[4,480,480]{2,1,0:T(8,128)(2,1)S(1)}, u32[]{:S(2)}, u32[]{:S(2)}) collective-permute-start(bf16[4,480,480]{2,1,0:T(8,128)(2,1)S(1)} %convolution_convert_fusion.refs_6_.refs_9_), channel_id=1, source_target_pairs={{0,1},{1,0},{2,3},{3,2},{4,5},{5,4},{6,7},{7,6},{8,9},{9,8},{10,11... | collective-permute-start | bytes 5529608 | tf_op jit(solution)/shard_map/ppermute | solution.py:324
  13.0 3.5 %collective-permute-start.1 = (f32[64,120]{1,0:T(8,128)S(1)}, f32[64,120]{1,0:T(8,128)S(1)}, u32[]{:S(2)}, u32[]{:S(2)}) collective-permute-start(f32[64,120]{1,0:T(8,128)S(1)} %shard_map.88), channel_id=1, source_target_pairs={{0,3},{1,2},{2,1},{3,0},{4,7},{5,6},{6,5},{7,4},{8,11},{9,10},{10,... | collective-permute-start | bytes 92168 | tf_op jit(solution)/shard_map/ppermute | solution.py:333
  14.6 2.0 %collective-permute-start.4 = (f32[32,160]{1,0:T(8,128)S(1)}, f32[32,160]{1,0:T(8,128)S(1)}, u32[]{:S(2)}, u32[]{:S(2)}) collective-permute-start(f32[32,160]{1,0:T(8,128)S(1)} %pad_maximum_fusion), channel_id=1, source_target_pairs={{0,1},{1,0},{2,3},{3,2},{4,5},{5,4},{6,7},{7,6},{8,9},{9,8},{10,11... | collective-permute-start | bytes 61448 | tf_op jit(solution)/shard_map/ppermute | solution.py:324
  17.7 6.4 %collective-permute-start.8 = (bf16[32,80]{1,0:T(8,128)(2,1)S(1)}, bf16[32,80]{1,0:T(8,128)(2,1)S(1)}, u32[]{:S(2)}, u32[]{:S(2)}) collective-permute-start(bf16[32,80]{1,0:T(8,128)(2,1)S(1)} %get-tuple-element.56), channel_id=1, source_target_pairs={{0,28},{1,31},{2,30},{3,29},{4,8},{5,11},{6,10},{7,9},{8,4},{9,7},... | collective-permute-start | bytes 15368 | tf_op jit(solution)/shard_map/ppermute | solution.py:330
  19.6 4.5 %collective-permute-start.7 = (bf16[16,80]{1,0:T(8,128)(2,1)S(1)}, bf16[16,80]{1,0:T(8,128)(2,1)S(1)}, u32[]{:S(2)}, u32[]{:S(2)}) collective-permute-start(bf16[16,80]{1,0:T(8,128)(2,1)S(1)} %get-tuple-element.55), channel_id=1, source_target_pairs={{0,4},{1,7},{2,6},{3,5},{4,0},{5,3},{6,2},{7,1},{8,12},{9,15},{10,... | collective-permute-start | bytes 7688 | tf_op jit(solution)/shard_map/ppermute | solution.py:331
  19.6 4.6 %collective-permute-start.6 = (bf16[64,80]{1,0:T(8,128)(2,1)S(1)}, bf16[64,80]{1,0:T(8,128)(2,1)S(1)}, u32[]{:S(2)}, u32[]{:S(2)}) collective-permute-start(bf16[64,80]{1,0:T(8,128)(2,1)S(1)} %get-tuple-element.54), channel_id=1, source_target_pairs={{0,3},{1,2},{2,1},{3,0},{4,7},{5,6},{6,5},{7,4},{8,11},{9,10},{10,... | collective-permute-start | bytes 30728 | tf_op jit(solution)/shard_map/ppermute | solution.py:333
  24.1 1.2 %collective-permute-start.9 = (bf16[32,80]{1,0:T(8,128)(2,1)S(1)}, bf16[32,80]{1,0:T(8,128)(2,1)S(1)}, u32[]{:S(2)}, u32[]{:S(2)}) collective-permute-start(bf16[32,80]{1,0:T(8,128)(2,1)S(1)} %pad_maximum_fusion.1), channel_id=1, source_target_pairs={{0,1},{1,0},{2,3},{3,2},{4,5},{5,4},{6,7},{7,6},{8,9},{9,8},{10,11... | collective-permute-start | bytes 15368 | tf_op jit(solution)/shard_map/ppermute | solution.py:324
  26.3 6.4 %collective-permute-start.12 = (bf16[32,80]{1,0:T(8,128)(2,1)S(1)}, bf16[32,80]{1,0:T(8,128)(2,1)S(1)}, u32[]{:S(2)}, u32[]{:S(2)}) collective-permute-start(bf16[32,80]{1,0:T(8,128)(2,1)S(1)} %get-tuple-element.62), channel_id=1, source_target_pairs={{0,28},{1,31},{2,30},{3,29},{4,8},{5,11},{6,10},{7,9},{8,4},{9,7},... | collective-permute-start | bytes 15368 | tf_op jit(solution)/shard_map/ppermute | solution.py:330
  28.4 4.4 %collective-permute-start.11 = (bf16[16,80]{1,0:T(8,128)(2,1)S(1)}, bf16[16,80]{1,0:T(8,128)(2,1)S(1)}, u32[]{:S(2)}, u32[]{:S(2)}) collective-permute-start(bf16[16,80]{1,0:T(8,128)(2,1)S(1)} %get-tuple-element.61), channel_id=1, source_target_pairs={{0,4},{1,7},{2,6},{3,5},{4,0},{5,3},{6,2},{7,1},{8,12},{9,15},{10,... | collective-permute-start | bytes 7688 | tf_op jit(solution)/shard_map/ppermute | solution.py:331
  28.4 4.4 %collective-permute-start.10 = (bf16[64,80]{1,0:T(8,128)(2,1)S(1)}, bf16[64,80]{1,0:T(8,128)(2,1)S(1)}, u32[]{:S(2)}, u32[]{:S(2)}) collective-permute-start(bf16[64,80]{1,0:T(8,128)(2,1)S(1)} %get-tuple-element.60), channel_id=1, source_target_pairs={{0,3},{1,2},{2,1},{3,0},{4,7},{5,6},{6,5},{7,4},{8,11},{9,10},{10,... | collective-permute-start | bytes 30728 | tf_op jit(solution)/shard_map/ppermute | solution.py:333
  32.7 1.2 %collective-permute-start.13 = (bf16[32,80]{1,0:T(8,128)(2,1)S(1)}, bf16[32,80]{1,0:T(8,128)(2,1)S(1)}, u32[]{:S(2)}, u32[]{:S(2)}) collective-permute-start(bf16[32,80]{1,0:T(8,128)(2,1)S(1)} %pad_maximum_fusion.2), channel_id=1, source_target_pairs={{0,1},{1,0},{2,3},{3,2},{4,5},{5,4},{6,7},{7,6},{8,9},{9,8},{10,11... | collective-permute-start | bytes 15368 | tf_op jit(solution)/shard_map/ppermute | solution.py:324
  35.0 6.4 %collective-permute-start.16 = (bf16[32,80]{1,0:T(8,128)(2,1)S(1)}, bf16[32,80]{1,0:T(8,128)(2,1)S(1)}, u32[]{:S(2)}, u32[]{:S(2)}) collective-permute-start(bf16[32,80]{1,0:T(8,128)(2,1)S(1)} %get-tuple-element.66), channel_id=1, source_target_pairs={{0,28},{1,31},{2,30},{3,29},{4,8},{5,11},{6,10},{7,9},{8,4},{9,7},... | collective-permute-start | bytes 15368 | tf_op jit(solution)/shard_map/ppermute | solution.py:330
  37.1 4.3 %collective-permute-start.15 = (bf16[16,80]{1,0:T(8,128)(2,1)S(1)}, bf16[16,80]{1,0:T(8,128)(2,1)S(1)}, u32[]{:S(2)}, u32[]{:S(2)}) collective-permute-start(bf16[16,80]{1,0:T(8,128)(2,1)S(1)} %get-tuple-element.65), channel_id=1, source_target_pairs={{0,4},{1,7},{2,6},{3,5},{4,0},{5,3},{6,2},{7,1},{8,12},{9,15},{10,... | collective-permute-start | bytes 7688 | tf_op jit(solution)/shard_map/ppermute | solution.py:331
  37.1 4.3 %collective-permute-start.14 = (bf16[64,80]{1,0:T(8,128)(2,1)S(1)}, bf16[64,80]{1,0:T(8,128)(2,1)S(1)}, u32[]{:S(2)}, u32[]{:S(2)}) collective-permute-start(bf16[64,80]{1,0:T(8,128)(2,1)S(1)} %get-tuple-element.64), channel_id=1, source_target_pairs={{0,3},{1,2},{2,1},{3,0},{4,7},{5,6},{6,5},{7,4},{8,11},{9,10},{10,... | collective-permute-start | bytes 30728 | tf_op jit(solution)/shard_map/ppermute | solution.py:333
  41.4 1.2 %collective-permute-start.17 = (bf16[32,80]{1,0:T(8,128)(2,1)S(1)}, bf16[32,80]{1,0:T(8,128)(2,1)S(1)}, u32[]{:S(2)}, u32[]{:S(2)}) collective-permute-start(bf16[32,80]{1,0:T(8,128)(2,1)S(1)} %pad_maximum_fusion.3), channel_id=1, source_target_pairs={{0,1},{1,0},{2,3},{3,2},{4,5},{5,4},{6,7},{7,6},{8,9},{9,8},{10,11... | collective-permute-start | bytes 15368 | tf_op jit(solution)/shard_map/ppermute | solution.py:324
  43.6 6.4 %collective-permute-start.20 = (bf16[32,80]{1,0:T(8,128)(2,1)S(1)}, bf16[32,80]{1,0:T(8,128)(2,1)S(1)}, u32[]{:S(2)}, u32[]{:S(2)}) collective-permute-start(bf16[32,80]{1,0:T(8,128)(2,1)S(1)} %get-tuple-element.70), channel_id=1, source_target_pairs={{0,28},{1,31},{2,30},{3,29},{4,8},{5,11},{6,10},{7,9},{8,4},{9,7},... | collective-permute-start | bytes 15368 | tf_op jit(solution)/shard_map/ppermute | solution.py:330
  45.7 4.3 %collective-permute-start.19 = (bf16[16,80]{1,0:T(8,128)(2,1)S(1)}, bf16[16,80]{1,0:T(8,128)(2,1)S(1)}, u32[]{:S(2)}, u32[]{:S(2)}) collective-permute-start(bf16[16,80]{1,0:T(8,128)(2,1)S(1)} %get-tuple-element.69), channel_id=1, source_target_pairs={{0,4},{1,7},{2,6},{3,5},{4,0},{5,3},{6,2},{7,1},{8,12},{9,15},{10,... | collective-permute-start | bytes 7688 | tf_op jit(solution)/shard_map/ppermute | solution.py:331
  45.7 4.8 %collective-permute-start.18 = (bf16[64,80]{1,0:T(8,128)(2,1)S(1)}, bf16[64,80]{1,0:T(8,128)(2,1)S(1)}, u32[]{:S(2)}, u32[]{:S(2)}) collective-permute-start(bf16[64,80]{1,0:T(8,128)(2,1)S(1)} %get-tuple-element.68), channel_id=1, source_target_pairs={{0,3},{1,2},{2,1},{3,0},{4,7},{5,6},{6,5},{7,4},{8,11},{9,10},{10,... | collective-permute-start | bytes 30728 | tf_op jit(solution)/shard_map/ppermute | solution.py:333
  50.0 1.2 %collective-permute-start.21 = (bf16[32,80]{1,0:T(8,128)(2,1)S(1)}, bf16[32,80]{1,0:T(8,128)(2,1)S(1)}, u32[]{:S(2)}, u32[]{:S(2)}) collective-permute-start(bf16[32,80]{1,0:T(8,128)(2,1)S(1)} %pad_maximum_fusion.4), channel_id=1, source_target_pairs={{0,1},{1,0},{2,3},{3,2},{4,5},{5,4},{6,7},{7,6},{8,9},{9,8},{10,11... | collective-permute-start | bytes 15368 | tf_op jit(solution)/shard_map/ppermute | solution.py:324

commit v10 on v8

--- a/solution.py
+++ b/solution.py
@@ -248,7 +248,7 @@
     picked = contract(hits[...], trace_now.astype(HALF), 1, 0)
     lam = to_lanes(picked, len(pieces), sides)
     terms = add_up([contract(masked(lam, e), block, 1, 0) for e, block in enumerate(pieces)])
-    return spread(spread_hits[...], to_rows(terms, sides, trace_now.shape[1]))
+    return contract(spread_hits[...], to_rows(terms, sides, trace_now.shape[1]).astype(HALF), 1, 0)
 
 
 def own_kernel(chip_faces, sums, *refs):

time: 52.7 us -> 52.5 us (level)
  no operation moved by 1% of the time
where the time goes in v10:
time: 52.5 us; the launch traced here: 52.4 us
  starting transfers between devices  21.7 us (41%)
  waiting for transfers between devices  18.9 us (36%)
  Pallas kernels  8.84 us (17%)
  matrix products  2.07 us (4%)
  between operations  0.81 us (2%)
    ppermute x5, starting transfers between devices, exchange(): lax.ppermute(to_second, AXES, partners(groups, chips, 1, s))  14.2 us
    ppermute x5, waiting for transfers between devices, exchange(): lax.ppermute(to_second, AXES, partners(groups, chips, 1, s))  13 us
    pallas_call x15, Pallas kernels, call(): pl.pallas_call(body, out_shape=outs, in_specs=[HBM] * stay + [VMEM] * (le...  8.84 us
    ppermute x5, starting transfers between devices, exchange(): lax.ppermute(sent, AXES, along_x(groups, chips, shift))  5.03 us
    ppermute x7, waiting for transfers between devices, swap_core(): return lax.ppermute(block, AXES, other_core(groups, chips))  4.06 us
    ppermute x7, starting transfers between devices, swap_core(): return lax.ppermute(block, AXES, other_core(groups, chips))  2.34 us
    dot_general x1, matrix products, local(): jnp.einsum('evs,evt->est', couple, down, preferred_element_type=F32)  1.22 us
  transfers between devices with their start and end apart: 22, of which 10 were waited for; matrix products, arithmetic and copies ran while one was open for 4% of the time, Pallas kernels for 2%

profile of v10, /device:TPU:0, one launch (start us, length us, event | category | flops | bytes accessed | tf_op | source)
XLA Modules:
  0.0 52.4 jit_solution(17856055921208033683)
XLA Ops:
  0.6 2.6 %shard_map.86 = (f32[8,320]{1,0:T(8,128)S(1)}, f32[64,166]{1,0:T(8,128)S(1)}, s32[8,6]{1,0:T(8,128)S(1)}, bf16[4,320,320]{2,1,0:T(8,128)(2,1)S(1)}, bf16[4,320,4...) custom-call(bf16[4,320,320]{2,1,0:T(8,128)(2,1)} %refs_0_.1, bf16[4,320,480]{2,1,0:T(8,128)(2,1)} %bitcast.5, ...), custom_call_target="tpu_custom_call" | custom-call | tf_op jit(solution)/shard_map/pallas_call | solution.py:63
  4.7 6.0 %collective-permute-start.3 = (f32[16,160]{1,0:T(8,128)S(1)}, f32[16,160]{1,0:T(8,128)S(1)}, u32[]{:S(2)}, u32[]{:S(2)}) collective-permute-start(f32[16,160]{1,0:T(8,128)S(1)} %get-tuple-element.48), channel_id=1, source_target_pairs={{0,28},{1,31},{2,30},{3,29},{4,8},{5,11},{6,10},{7,9},{8,4},{9,7},... | collective-permute-start | bytes 30728 | tf_op jit(solution)/shard_map/ppermute | solution.py:352
  10.7 1.2 %convolution_convert_fusion.refs_6_.rest_3_ = bf16[4,480,480]{2,1,0:T(8,128)(2,1)S(1)} fusion(bf16[4,320,480]{2,1,0:T(8,128)(2,1)S(1)} %convolution_convert_fusion.1.couple, bf16[4,320,480]{2,1,0:T(8,128)(2,1)S(1)} %get-tuple-element.45), kind=kOutput, calls=%fused_computation | convolution fusion | flops 590745600 | bytes 4300800 | tf_op jit(solution)/shard_map/evs,evt->est/dot_general | solution.py:394
  15.5 1.0 %collective-permute-done.1.refs_0_ = f32[64,120]{1,0:T(8,128)S(1)} collective-permute-done((f32[64,120]{1,0:T(8,128)S(1)}, f32[64,120]{1,0:T(8,128)S(1)}, u32[]{:S(2)}, u32[]{:S(2)}) %collective-permute-start.1) | collective-permute-done | bytes 30752 | tf_op jit(solution)/shard_map/ppermute | solution.py:355
  16.6 1.1 %shard_map.91 = (f32[64,80]{1,0:T(8,128)S(1)}, f32[64,80]{1,0:T(8,128)S(1)}, f32[64,80]{1,0:T(8,128)S(1)}, bf16[64,80]{1,0:T(8,128)(2,1)S(1)}, bf16[16,80]{1,0:T(8,128)(2,1)S(1)}, /*index=5*/bf16[32,80]{1,0:T(8,128)(2,1)S(1)}) custom-call(f32[64,160]{1,0:T(8,128)S(1)} %shard_map.89.refs_0_, f32[32,160]{1,0:T(8,128)S(1)} %collective-permute-done.2.refs_1_, ...), custom_call_target="tpu_custom_call" | custom-call | tf_op jit(solution)/shard_map/pallas_call | solution.py:63
  17.7 1.9 %collective-permute-start.8 = (bf16[32,80]{1,0:T(8,128)(2,1)S(1)}, bf16[32,80]{1,0:T(8,128)(2,1)S(1)}, u32[]{:S(2)}, u32[]{:S(2)}) collective-permute-start(bf16[32,80]{1,0:T(8,128)(2,1)S(1)} %get-tuple-element.56), channel_id=1, source_target_pairs={{0,28},{1,31},{2,30},{3,29},{4,8},{5,11},{6,10},{7,9},{8,4},{9,7},... | collective-permute-start | bytes 15368 | tf_op jit(solution)/shard_map/ppermute | solution.py:352
  19.6 1.0 %collective-permute-start.6 = (bf16[64,80]{1,0:T(8,128)(2,1)S(1)}, bf16[64,80]{1,0:T(8,128)(2,1)S(1)}, u32[]{:S(2)}, u32[]{:S(2)}) collective-permute-start(bf16[64,80]{1,0:T(8,128)(2,1)S(1)} %get-tuple-element.54), channel_id=1, source_target_pairs={{0,3},{1,2},{2,1},{3,0},{4,7},{5,6},{6,5},{7,4},{8,11},{9,10},{10,... | collective-permute-start | bytes 30728 | tf_op jit(solution)/shard_map/ppermute | solution.py:355
  20.6 3.5 %collective-permute-done.8.refs_3_ = bf16[32,80]{1,0:T(8,128)(2,1)S(1)} collective-permute-done((bf16[32,80]{1,0:T(8,128)(2,1)S(1)}, bf16[32,80]{1,0:T(8,128)(2,1)S(1)}, u32[]{:S(2)}, u32[]{:S(2)}) %collective-permute-start.8) | collective-permute-done | bytes 5152 | tf_op jit(solution)/shard_map/ppermute | solution.py:352
  24.2 1.1 %collective-permute-done.9.mate = bf16[32,80]{1,0:T(8,128)(2,1)S(1)} collective-permute-done((bf16[32,80]{1,0:T(8,128)(2,1)S(1)}, bf16[32,80]{1,0:T(8,128)(2,1)S(1)}, u32[]{:S(2)}, u32[]{:S(2)}) %collective-permute-start.9) | collective-permute-done | bytes 5152 | tf_op jit(solution)/shard_map/ppermute | solution.py:346
  25.3 1.0 %shard_map.93 = (f32[64,80]{1,0:T(8,128)S(1)}, bf16[64,80]{1,0:T(8,128)(2,1)S(1)}, bf16[16,80]{1,0:T(8,128)(2,1)S(1)}, bf16[32,80]{1,0:T(8,128)(2,1)S(1)}) custom-call(f32[64,80]{1,0:T(8,128)S(1)} %shard_map.92.known, bf16[32,80]{1,0:T(8,128)(2,1)S(1)} %collective-permute-done.9.mate, f32[64,80]{1,0:T(8,128)S(1)} %get-tuple-element.58.rest_0_, ...), custom_call_target="tpu_custom_call" | custom-call | tf_op jit(solution)/shard_map/pallas_call | solution.py:63
  26.3 2.0 %collective-permute-start.12 = (bf16[32,80]{1,0:T(8,128)(2,1)S(1)}, bf16[32,80]{1,0:T(8,128)(2,1)S(1)}, u32[]{:S(2)}, u32[]{:S(2)}) collective-permute-start(bf16[32,80]{1,0:T(8,128)(2,1)S(1)} %get-tuple-element.62), channel_id=1, source_target_pairs={{0,28},{1,31},{2,30},{3,29},{4,8},{5,11},{6,10},{7,9},{8,4},{9,7},... | collective-permute-start | bytes 15368 | tf_op jit(solution)/shard_map/ppermute | solution.py:352
  28.4 1.4 %collective-permute-start.10 = (bf16[64,80]{1,0:T(8,128)(2,1)S(1)}, bf16[64,80]{1,0:T(8,128)(2,1)S(1)}, u32[]{:S(2)}, u32[]{:S(2)}) collective-permute-start(bf16[64,80]{1,0:T(8,128)(2,1)S(1)} %get-tuple-element.60), channel_id=1, source_target_pairs={{0,3},{1,2},{2,1},{3,0},{4,7},{5,6},{6,5},{7,4},{8,11},{9,10},{10,... | collective-permute-start | bytes 30728 | tf_op jit(solution)/shard_map/ppermute | solution.py:355
  29.8 2.9 %collective-permute-done.12.refs_3_ = bf16[32,80]{1,0:T(8,128)(2,1)S(1)} collective-permute-done((bf16[32,80]{1,0:T(8,128)(2,1)S(1)}, bf16[32,80]{1,0:T(8,128)(2,1)S(1)}, u32[]{:S(2)}, u32[]{:S(2)}) %collective-permute-start.12) | collective-permute-done | bytes 5152 | tf_op jit(solution)/shard_map/ppermute | solution.py:352
  32.8 1.1 %collective-permute-done.13.mate = bf16[32,80]{1,0:T(8,128)(2,1)S(1)} collective-permute-done((bf16[32,80]{1,0:T(8,128)(2,1)S(1)}, bf16[32,80]{1,0:T(8,128)(2,1)S(1)}, u32[]{:S(2)}, u32[]{:S(2)}) %collective-permute-start.13) | collective-permute-done | bytes 5152 | tf_op jit(solution)/shard_map/ppermute | solution.py:346
  34.0 1.0 %shard_map.95 = (f32[64,80]{1,0:T(8,128)S(1)}, bf16[64,80]{1,0:T(8,128)(2,1)S(1)}, bf16[16,80]{1,0:T(8,128)(2,1)S(1)}, bf16[32,80]{1,0:T(8,128)(2,1)S(1)}) custom-call(f32[64,80]{1,0:T(8,128)S(1)} %shard_map.94.known, bf16[32,80]{1,0:T(8,128)(2,1)S(1)} %collective-permute-done.13.mate, f32[64,80]{1,0:T(8,128)S(1)} %get-tuple-element.58.rest_0_, ...), custom_call_target="tpu_custom_call" | custom-call | tf_op jit(solution)/shard_map/pallas_call | solution.py:63
  34.9 2.1 %collective-permute-start.16 = (bf16[32,80]{1,0:T(8,128)(2,1)S(1)}, bf16[32,80]{1,0:T(8,128)(2,1)S(1)}, u32[]{:S(2)}, u32[]{:S(2)}) collective-permute-start(bf16[32,80]{1,0:T(8,128)(2,1)S(1)} %get-tuple-element.66), channel_id=1, source_target_pairs={{0,28},{1,31},{2,30},{3,29},{4,8},{5,11},{6,10},{7,9},{8,4},{9,7},... | collective-permute-start | bytes 15368 | tf_op jit(solution)/shard_map/ppermute | solution.py:352
  37.1 1.0 %collective-permute-start.14 = (bf16[64,80]{1,0:T(8,128)(2,1)S(1)}, bf16[64,80]{1,0:T(8,128)(2,1)S(1)}, u32[]{:S(2)}, u32[]{:S(2)}) collective-permute-start(bf16[64,80]{1,0:T(8,128)(2,1)S(1)} %get-tuple-element.64), channel_id=1, source_target_pairs={{0,3},{1,2},{2,1},{3,0},{4,7},{5,6},{6,5},{7,4},{8,11},{9,10},{10,... | collective-permute-start | bytes 30728 | tf_op jit(solution)/shard_map/ppermute | solution.py:355
  38.0 3.3 %collective-permute-done.16.refs_3_ = bf16[32,80]{1,0:T(8,128)(2,1)S(1)} collective-permute-done((bf16[32,80]{1,0:T(8,128)(2,1)S(1)}, bf16[32,80]{1,0:T(8,128)(2,1)S(1)}, u32[]{:S(2)}, u32[]{:S(2)}) %collective-permute-start.16) | collective-permute-done | bytes 5152 | tf_op jit(solution)/shard_map/ppermute | solution.py:352
  41.5 1.1 %collective-permute-done.17.mate = bf16[32,80]{1,0:T(8,128)(2,1)S(1)} collective-permute-done((bf16[32,80]{1,0:T(8,128)(2,1)S(1)}, bf16[32,80]{1,0:T(8,128)(2,1)S(1)}, u32[]{:S(2)}, u32[]{:S(2)}) %collective-permute-start.17) | collective-permute-done | bytes 5152 | tf_op jit(solution)/shard_map/ppermute | solution.py:346
  42.6 1.0 %shard_map.97 = (f32[64,80]{1,0:T(8,128)S(1)}, bf16[64,80]{1,0:T(8,128)(2,1)S(1)}, bf16[16,80]{1,0:T(8,128)(2,1)S(1)}, bf16[32,80]{1,0:T(8,128)(2,1)S(1)}) custom-call(f32[64,80]{1,0:T(8,128)S(1)} %shard_map.96.known, bf16[32,80]{1,0:T(8,128)(2,1)S(1)} %collective-permute-done.17.mate, f32[64,80]{1,0:T(8,128)S(1)} %get-tuple-element.58.rest_0_, ...), custom_call_target="tpu_custom_call" | custom-call | tf_op jit(solution)/shard_map/pallas_call | solution.py:63
  43.6 2.1 %collective-permute-start.20 = (bf16[32,80]{1,0:T(8,128)(2,1)S(1)}, bf16[32,80]{1,0:T(8,128)(2,1)S(1)}, u32[]{:S(2)}, u32[]{:S(2)}) collective-permute-start(bf16[32,80]{1,0:T(8,128)(2,1)S(1)} %get-tuple-element.70), channel_id=1, source_target_pairs={{0,28},{1,31},{2,30},{3,29},{4,8},{5,11},{6,10},{7,9},{8,4},{9,7},... | collective-permute-start | bytes 15368 | tf_op jit(solution)/shard_map/ppermute | solution.py:352
  45.7 1.0 %collective-permute-start.18 = (bf16[64,80]{1,0:T(8,128)(2,1)S(1)}, bf16[64,80]{1,0:T(8,128)(2,1)S(1)}, u32[]{:S(2)}, u32[]{:S(2)}) collective-permute-start(bf16[64,80]{1,0:T(8,128)(2,1)S(1)} %get-tuple-element.68), channel_id=1, source_target_pairs={{0,3},{1,2},{2,1},{3,0},{4,7},{5,6},{6,5},{7,4},{8,11},{9,10},{10,... | collective-permute-start | bytes 30728 | tf_op jit(solution)/shard_map/ppermute | solution.py:355
  46.7 3.3 %collective-permute-done.20.refs_3_ = bf16[32,80]{1,0:T(8,128)(2,1)S(1)} collective-permute-done((bf16[32,80]{1,0:T(8,128)(2,1)S(1)}, bf16[32,80]{1,0:T(8,128)(2,1)S(1)}, u32[]{:S(2)}, u32[]{:S(2)}) %collective-permute-start.20) | collective-permute-done | bytes 5152 | tf_op jit(solution)/shard_map/ppermute | solution.py:352
  51.2 1.1 %shard_map.100 = (f32[12,80]{1,0:T(8,128)}, f32[4,320]{1,0:T(4,128)}) custom-call(f32[64,80]{1,0:T(8,128)S(1)} %shard_map.98.known, bf16[32,80]{1,0:T(8,128)(2,1)S(1)} %collective-permute-done.21.mate, f32[64,80]{1,0:T(8,128)S(1)} %get-tuple-element.58.rest_0_, bf16[48,64]{1,0:T(8,128)(2,1)S(1)} %get-tuple-element.50.refs_4_.rest_1_, ...), custom_call_target="tpu_custom_call" | custom-call | tf_op jit(solution)/shard_map/pallas_call | solution.py:63
  (47 shorter events, 6.8 us)
Async XLA Ops:
  3.3 1.4 %collective-permute-start = (f32[64,166]{1,0:T(8,128)S(1)}, f32[64,166]{1,0:T(8,128)S(1)}, u32[]{:S(2)}, u32[]{:S(2)}) collective-permute-start(f32[64,166]{1,0:T(8,128)S(1)} %get-tuple-element.39.packet), channel_id=1, source_target_pairs={{0,1},{1,0},{2,3},{3,2},{4,5},{5,4},{6,7},{7,6},{8,9},{9,8},{10,11... | collective-permute-start | bytes 127496 | tf_op jit(solution)/shard_map/ppermute | solution.py:346
  4.7 9.9 %collective-permute-start.3 = (f32[16,160]{1,0:T(8,128)S(1)}, f32[16,160]{1,0:T(8,128)S(1)}, u32[]{:S(2)}, u32[]{:S(2)}) collective-permute-start(f32[16,160]{1,0:T(8,128)S(1)} %get-tuple-element.48), channel_id=1, source_target_pairs={{0,28},{1,31},{2,30},{3,29},{4,8},{5,11},{6,10},{7,9},{8,4},{9,7},... | collective-permute-start | bytes 30728 | tf_op jit(solution)/shard_map/ppermute | solution.py:352
  10.7 3.9 %collective-permute-start.2 = (f32[32,160]{1,0:T(8,128)S(1)}, f32[32,160]{1,0:T(8,128)S(1)}, u32[]{:S(2)}, u32[]{:S(2)}) collective-permute-start(f32[32,160]{1,0:T(8,128)S(1)} %get-tuple-element.47), channel_id=1, source_target_pairs={{0,4},{1,7},{2,6},{3,5},{4,0},{5,3},{6,2},{7,1},{8,12},{9,15},{10,... | collective-permute-start | bytes 61448 | tf_op jit(solution)/shard_map/ppermute | solution.py:353
  11.9 4.7 %collective-permute-start.5 = (bf16[4,480,480]{2,1,0:T(8,128)(2,1)S(1)}, bf16[4,480,480]{2,1,0:T(8,128)(2,1)S(1)}, u32[]{:S(2)}, u32[]{:S(2)}) collective-permute-start(bf16[4,480,480]{2,1,0:T(8,128)(2,1)S(1)} %convolution_convert_fusion.refs_6_.rest_3_), channel_id=1, source_target_pairs={{0,1},{1,0},{2,3},{3,2},{4,5},{5,4},{6,7},{7,6},{8,9},{9,8},{10,11... | collective-permute-start | bytes 5529608 | tf_op jit(solution)/shard_map/ppermute | solution.py:346
  13.0 3.5 %collective-permute-start.1 = (f32[64,120]{1,0:T(8,128)S(1)}, f32[64,120]{1,0:T(8,128)S(1)}, u32[]{:S(2)}, u32[]{:S(2)}) collective-permute-start(f32[64,120]{1,0:T(8,128)S(1)} %shard_map.88), channel_id=1, source_target_pairs={{0,3},{1,2},{2,1},{3,0},{4,7},{5,6},{6,5},{7,4},{8,11},{9,10},{10,... | collective-permute-start | bytes 92168 | tf_op jit(solution)/shard_map/ppermute | solution.py:355
  14.6 2.0 %collective-permute-start.4 = (f32[32,160]{1,0:T(8,128)S(1)}, f32[32,160]{1,0:T(8,128)S(1)}, u32[]{:S(2)}, u32[]{:S(2)}) collective-permute-start(f32[32,160]{1,0:T(8,128)S(1)} %pad_maximum_fusion), channel_id=1, source_target_pairs={{0,1},{1,0},{2,3},{3,2},{4,5},{5,4},{6,7},{7,6},{8,9},{9,8},{10,11... | collective-permute-start | bytes 61448 | tf_op jit(solution)/shard_map/ppermute | solution.py:346
  17.7 6.4 %collective-permute-start.8 = (bf16[32,80]{1,0:T(8,128)(2,1)S(1)}, bf16[32,80]{1,0:T(8,128)(2,1)S(1)}, u32[]{:S(2)}, u32[]{:S(2)}) collective-permute-start(bf16[32,80]{1,0:T(8,128)(2,1)S(1)} %get-tuple-element.56), channel_id=1, source_target_pairs={{0,28},{1,31},{2,30},{3,29},{4,8},{5,11},{6,10},{7,9},{8,4},{9,7},... | collective-permute-start | bytes 15368 | tf_op jit(solution)/shard_map/ppermute | solution.py:352
  19.6 4.5 %collective-permute-start.7 = (bf16[16,80]{1,0:T(8,128)(2,1)S(1)}, bf16[16,80]{1,0:T(8,128)(2,1)S(1)}, u32[]{:S(2)}, u32[]{:S(2)}) collective-permute-start(bf16[16,80]{1,0:T(8,128)(2,1)S(1)} %get-tuple-element.55), channel_id=1, source_target_pairs={{0,4},{1,7},{2,6},{3,5},{4,0},{5,3},{6,2},{7,1},{8,12},{9,15},{10,... | collective-permute-start | bytes 7688 | tf_op jit(solution)/shard_map/ppermute | solution.py:353
  19.6 4.6 %collective-permute-start.6 = (bf16[64,80]{1,0:T(8,128)(2,1)S(1)}, bf16[64,80]{1,0:T(8,128)(2,1)S(1)}, u32[]{:S(2)}, u32[]{:S(2)}) collective-permute-start(bf16[64,80]{1,0:T(8,128)(2,1)S(1)} %get-tuple-element.54), channel_id=1, source_target_pairs={{0,3},{1,2},{2,1},{3,0},{4,7},{5,6},{6,5},{7,4},{8,11},{9,10},{10,... | collective-permute-start | bytes 30728 | tf_op jit(solution)/shard_map/ppermute | solution.py:355
  24.1 1.2 %collective-permute-start.9 = (bf16[32,80]{1,0:T(8,128)(2,1)S(1)}, bf16[32,80]{1,0:T(8,128)(2,1)S(1)}, u32[]{:S(2)}, u32[]{:S(2)}) collective-permute-start(bf16[32,80]{1,0:T(8,128)(2,1)S(1)} %pad_maximum_fusion.1), channel_id=1, source_target_pairs={{0,1},{1,0},{2,3},{3,2},{4,5},{5,4},{6,7},{7,6},{8,9},{9,8},{10,11... | collective-permute-start | bytes 15368 | tf_op jit(solution)/shard_map/ppermute | solution.py:346
  26.3 6.4 %collective-permute-start.12 = (bf16[32,80]{1,0:T(8,128)(2,1)S(1)}, bf16[32,80]{1,0:T(8,128)(2,1)S(1)}, u32[]{:S(2)}, u32[]{:S(2)}) collective-permute-start(bf16[32,80]{1,0:T(8,128)(2,1)S(1)} %get-tuple-element.62), channel_id=1, source_target_pairs={{0,28},{1,31},{2,30},{3,29},{4,8},{5,11},{6,10},{7,9},{8,4},{9,7},... | collective-permute-start | bytes 15368 | tf_op jit(solution)/shard_map/ppermute | solution.py:352
  28.4 4.4 %collective-permute-start.11 = (bf16[16,80]{1,0:T(8,128)(2,1)S(1)}, bf16[16,80]{1,0:T(8,128)(2,1)S(1)}, u32[]{:S(2)}, u32[]{:S(2)}) collective-permute-start(bf16[16,80]{1,0:T(8,128)(2,1)S(1)} %get-tuple-element.61), channel_id=1, source_target_pairs={{0,4},{1,7},{2,6},{3,5},{4,0},{5,3},{6,2},{7,1},{8,12},{9,15},{10,... | collective-permute-start | bytes 7688 | tf_op jit(solution)/shard_map/ppermute | solution.py:353
  28.4 4.4 %collective-permute-start.10 = (bf16[64,80]{1,0:T(8,128)(2,1)S(1)}, bf16[64,80]{1,0:T(8,128)(2,1)S(1)}, u32[]{:S(2)}, u32[]{:S(2)}) collective-permute-start(bf16[64,80]{1,0:T(8,128)(2,1)S(1)} %get-tuple-element.60), channel_id=1, source_target_pairs={{0,3},{1,2},{2,1},{3,0},{4,7},{5,6},{6,5},{7,4},{8,11},{9,10},{10,... | collective-permute-start | bytes 30728 | tf_op jit(solution)/shard_map/ppermute | solution.py:355
  32.7 1.2 %collective-permute-start.13 = (bf16[32,80]{1,0:T(8,128)(2,1)S(1)}, bf16[32,80]{1,0:T(8,128)(2,1)S(1)}, u32[]{:S(2)}, u32[]{:S(2)}) collective-permute-start(bf16[32,80]{1,0:T(8,128)(2,1)S(1)} %pad_maximum_fusion.2), channel_id=1, source_target_pairs={{0,1},{1,0},{2,3},{3,2},{4,5},{5,4},{6,7},{7,6},{8,9},{9,8},{10,11... | collective-permute-start | bytes 15368 | tf_op jit(solution)/shard_map/ppermute | solution.py:346
  34.9 6.4 %collective-permute-start.16 = (bf16[32,80]{1,0:T(8,128)(2,1)S(1)}, bf16[32,80]{1,0:T(8,128)(2,1)S(1)}, u32[]{:S(2)}, u32[]{:S(2)}) collective-permute-start(bf16[32,80]{1,0:T(8,128)(2,1)S(1)} %get-tuple-element.66), channel_id=1, source_target_pairs={{0,28},{1,31},{2,30},{3,29},{4,8},{5,11},{6,10},{7,9},{8,4},{9,7},... | collective-permute-start | bytes 15368 | tf_op jit(solution)/shard_map/ppermute | solution.py:352
  37.1 4.3 %collective-permute-start.15 = (bf16[16,80]{1,0:T(8,128)(2,1)S(1)}, bf16[16,80]{1,0:T(8,128)(2,1)S(1)}, u32[]{:S(2)}, u32[]{:S(2)}) collective-permute-start(bf16[16,80]{1,0:T(8,128)(2,1)S(1)} %get-tuple-element.65), channel_id=1, source_target_pairs={{0,4},{1,7},{2,6},{3,5},{4,0},{5,3},{6,2},{7,1},{8,12},{9,15},{10,... | collective-permute-start | bytes 7688 | tf_op jit(solution)/shard_map/ppermute | solution.py:353
  37.1 4.3 %collective-permute-start.14 = (bf16[64,80]{1,0:T(8,128)(2,1)S(1)}, bf16[64,80]{1,0:T(8,128)(2,1)S(1)}, u32[]{:S(2)}, u32[]{:S(2)}) collective-permute-start(bf16[64,80]{1,0:T(8,128)(2,1)S(1)} %get-tuple-element.64), channel_id=1, source_target_pairs={{0,3},{1,2},{2,1},{3,0},{4,7},{5,6},{6,5},{7,4},{8,11},{9,10},{10,... | collective-permute-start | bytes 30728 | tf_op jit(solution)/shard_map/ppermute | solution.py:355
  41.4 1.2 %collective-permute-start.17 = (bf16[32,80]{1,0:T(8,128)(2,1)S(1)}, bf16[32,80]{1,0:T(8,128)(2,1)S(1)}, u32[]{:S(2)}, u32[]{:S(2)}) collective-permute-start(bf16[32,80]{1,0:T(8,128)(2,1)S(1)} %pad_maximum_fusion.3), channel_id=1, source_target_pairs={{0,1},{1,0},{2,3},{3,2},{4,5},{5,4},{6,7},{7,6},{8,9},{9,8},{10,11... | collective-permute-start | bytes 15368 | tf_op jit(solution)/shard_map/ppermute | solution.py:346
  43.6 6.4 %collective-permute-start.20 = (bf16[32,80]{1,0:T(8,128)(2,1)S(1)}, bf16[32,80]{1,0:T(8,128)(2,1)S(1)}, u32[]{:S(2)}, u32[]{:S(2)}) collective-permute-start(bf16[32,80]{1,0:T(8,128)(2,1)S(1)} %get-tuple-element.70), channel_id=1, source_target_pairs={{0,28},{1,31},{2,30},{3,29},{4,8},{5,11},{6,10},{7,9},{8,4},{9,7},... | collective-permute-start | bytes 15368 | tf_op jit(solution)/shard_map/ppermute | solution.py:352
  45.7 4.3 %collective-permute-start.19 = (bf16[16,80]{1,0:T(8,128)(2,1)S(1)}, bf16[16,80]{1,0:T(8,128)(2,1)S(1)}, u32[]{:S(2)}, u32[]{:S(2)}) collective-permute-start(bf16[16,80]{1,0:T(8,128)(2,1)S(1)} %get-tuple-element.69), channel_id=1, source_target_pairs={{0,4},{1,7},{2,6},{3,5},{4,0},{5,3},{6,2},{7,1},{8,12},{9,15},{10,... | collective-permute-start | bytes 7688 | tf_op jit(solution)/shard_map/ppermute | solution.py:353
  45.7 4.8 %collective-permute-start.18 = (bf16[64,80]{1,0:T(8,128)(2,1)S(1)}, bf16[64,80]{1,0:T(8,128)(2,1)S(1)}, u32[]{:S(2)}, u32[]{:S(2)}) collective-permute-start(bf16[64,80]{1,0:T(8,128)(2,1)S(1)} %get-tuple-element.68), channel_id=1, source_target_pairs={{0,3},{1,2},{2,1},{3,0},{4,7},{5,6},{6,5},{7,4},{8,11},{9,10},{10,... | collective-permute-start | bytes 30728 | tf_op jit(solution)/shard_map/ppermute | solution.py:355
  50.0 1.2 %collective-permute-start.21 = (bf16[32,80]{1,0:T(8,128)(2,1)S(1)}, bf16[32,80]{1,0:T(8,128)(2,1)S(1)}, u32[]{:S(2)}, u32[]{:S(2)}) collective-permute-start(bf16[32,80]{1,0:T(8,128)(2,1)S(1)} %pad_maximum_fusion.4), channel_id=1, source_target_pairs={{0,1},{1,0},{2,3},{3,2},{4,5},{5,4},{6,7},{7,6},{8,9},{9,8},{10,11... | collective-permute-start | bytes 15368 | tf_op jit(solution)/shard_map/ppermute | solution.py:346
